TPU v7x, 512 devices: a whole 4x8x8 slice. The times are simulated.
512 devices in a mesh: layer: 32 (over y, x), space: 16 (over z, core).
Axes of the slice: x: 4, y: 8, z: 8, core: 2. Of those that a mesh axis runs over, the one named last changes fastest.
Arguments:
- images: float32 [4, 32, 32, 128], P(None, 'space'), may hold values from -6 to 6
- end_guess: float32 [32, 4, 32, 32, 128], P('layer', None, 'space'), may hold values from -6 to 6
- end_adjoint: float32 [32, 4, 32, 32, 128], P('layer', None, 'space'), may hold values from -6 to 6
- weights: bfloat16 [128, 1152, 128], P('layer'), may hold values from -0.1875 to 0.1875
Outputs:
- section_ends: float32 [32, 4, 32, 32, 128], P('layer', None, 'space')
- start_adjoint: float32 [32, 4, 32, 32, 128], P('layer', None, 'space')
- weight_grad: float32 [128, 1152, 128], P('layer', 'space')
All inputs are finite; a program needn't handle non-finite values.
Results may differ from a plain program's by a relative error of at most 0.0065.
Values may be sent and summed in bfloat16 or wider, within the bound.
No kernel may reach another device: no remote copies, remote signals or barrier semaphores. Data moves between devices by JAX's collectives and lax.ppermute only.
A program may use at most 64 MiB of HBM per device.

v0:
```python
import jax
import jax.numpy as jnp
from jax import lax
from jax.sharding import PartitionSpec as P

SECTION = 4


STEP_SIZE = 0.1


def padded_2(x, sides, width):
    for axis, dim in sides:
        size, length = (lax.axis_size(axis), x.shape[dim])
        up = [(i, (i + 1) % size) for i in range(size - 1)]
        down = [(j, i) for i, j in up]
        last = lax.slice_in_dim(x, length - width, length, axis=dim)
        leading = lax.slice_in_dim(x, 0, width, axis=dim)
        before = lax.ppermute(last, axis, up)
        after = lax.ppermute(leading, axis, down)
        x = jnp.concatenate([before, x, after], axis=dim)
    return x


def from_behind(block, axis, distance):
    devices = range(lax.axis_size(axis))
    route = [(i - distance, i) for i in devices if i - distance in devices]
    return lax.ppermute(block, axis, route)


def patches(extended, margin, amount, direction):
    image_width = extended.shape[2]
    channels = extended.shape[3]
    padded = jnp.pad(extended, ((0, 0), (0, 0), (1, 1), (0, 0)))
    pieces = []
    for offset in range(9):
        row_shift = direction * (offset // 3 - 1)
        col_shift = direction * (offset % 3 - 1)
        pieces.append(
            padded[
                :,
                margin + row_shift : margin + row_shift + amount,
                1 + col_shift : 1 + col_shift + image_width,
            ]
        )
    return jnp.concatenate(pieces, axis=-1).reshape(
        extended.shape[0] * amount * image_width, 9 * channels
    )


def activation(states):
    return jnp.tanh(states).astype(jnp.bfloat16)


def flip_kernel(kernel):
    channels = kernel.shape[1]
    return kernel.reshape(9, channels, channels).transpose(0, 2, 1).reshape(9 * channels, channels)


def grad_term(columns, flat_adjoint):
    return STEP_SIZE * lax.dot_general(
        columns, flat_adjoint, (((0,), (0,)), ((), ())), preferred_element_type=jnp.float32
    )


def local(images, end_guess, end_adjoint, weights):
    image_count, tile_rows, image_width, channels = images.shape
    section = lax.axis_index("layer")
    sections = lax.axis_size("layer")
    section_phase = section % 4
    leading = weights[0]
    long_step = 4 * SECTION * STEP_SIZE

    def conv_own(active, kernel, direction):
        extended = padded_2(active, (("space", 1),), 1)
        columns = patches(extended, 1, tile_rows, direction)
        result = jnp.dot(columns, kernel, preferred_element_type=jnp.float32)
        return result.reshape(image_count, tile_rows, image_width, channels)

    def starts(ends):
        received = from_behind(ends, "layer", 1)
        return jnp.where(section == 0, images, received)

    def fine_run(begin_states, amount):
        states = [begin_states]
        first_term = None
        for segment_index in range(amount):
            result = conv_own(activation(states[-1]), weights[segment_index], 1)
            if segment_index == 0:
                first_term = result
            states.append(states[-1] + STEP_SIZE * result)
        return (states, first_term)

    relaxed = fine_run(starts(end_guess[0]), SECTION)[0][-1]
    begin_states = starts(relaxed)
    states, first_term = fine_run(begin_states, SECTION)
    defect = states[-1] - (begin_states + SECTION * STEP_SIZE * first_term)

    def level_round(level_values):
        received = starts(level_values)
        return received + SECTION * STEP_SIZE * conv_own(activation(received), leading, 1) + defect

    level_values = jnp.where(section_phase == 0, states[-1], relaxed)
    for segment_index in (1, 2):
        level_values = jnp.where(
            section_phase == segment_index, level_round(level_values), level_values
        )
    closing = level_round(level_values)
    group_begin = begin_states
    for turn in range(3):
        passed = from_behind(group_begin, "layer", 1)
        group_begin = jnp.where(section_phase == 0, begin_states, passed)
    defect_two = closing - (group_begin + long_step * conv_own(activation(group_begin), leading, 1))

    def chain_turn(turn, carried):
        received = from_behind(carried, "layer", 1)
        relayed = jnp.where(section == 0, images, received)
        update = received + long_step * conv_own(activation(received), leading, 1) + defect_two
        settled = jnp.where(turn == section, update, carried)
        return jnp.where(section_phase == 3, settled, relayed)

    coarse_value = lax.fori_loop(0, sections, chain_turn, images)
    level_values = jnp.where(section_phase == 3, coarse_value, level_values)
    for segment_index in (0, 1, 2):
        level_values = jnp.where(
            section_phase == segment_index, level_round(level_values), level_values
        )
    final_states = fine_run(starts(level_values), SECTION - 1)[0]
    slope_list = [jnp.tanh(states_now) for states_now in final_states]
    saved = jnp.stack([slopes.astype(jnp.bfloat16) for slopes in slope_list])
    saved_ext = padded_2(saved, (("space", 2),), 1)
    adjoint = end_adjoint[0]
    grad_list = [None] * SECTION
    for segment_index in reversed(range(SECTION)):
        slopes = slope_list[segment_index]
        adjoint_low = adjoint.astype(jnp.bfloat16)
        columns = patches(saved_ext[segment_index], 1, tile_rows, 1)
        flat_adjoint = adjoint_low.reshape(-1, channels)
        grad_list[segment_index] = lax.psum_scatter(
            grad_term(columns, flat_adjoint), "space", scatter_dimension=0, tiled=True
        )
        back_term = conv_own(adjoint_low, flip_kernel(weights[segment_index]), -1)
        adjoint = adjoint + STEP_SIZE * (1.0 - slopes * slopes) * back_term
    weight_grad = jnp.stack(grad_list)
    return (level_values[None], adjoint[None], weight_grad)


def solution(mesh):
    return jax.shard_map(
        local,
        mesh=mesh,
        in_specs=(
            P(None, "space", None, None),
            P("layer", None, "space", None, None),
            P("layer", None, "space", None, None),
            P("layer", None, None),
        ),
        out_specs=(
            P("layer", None, "space", None, None),
            P("layer", None, "space", None, None),
            P("layer", "space", None),
        ),
        check_vma=False,
    )
```

profile of v0, /device:TPU:6, one launch (start us, length us, event | category | flops | bytes accessed | tf_op | source)
XLA Modules:
  0.0 1211.0 jit_solution(16178200786539929097)
XLA Ops:
  83.8 6.8 collective-permute-start.17
  155.4 6.6 collective-permute-start.28
  163.6 592.9 %while.15 = (s32[]{:T(128)}, f32[4,2,32,128]{3,2,1,0:T(8,128)S(1)}, pred[]{:T(512)}, s32[]{:T(128)}, bf16[1152,128]{1,0:T(8,128)(2,1)S(1)}, /*index=5*/f32[4,2,3...) while((s32[]{:T(128)}, f32[4,2,32,128]{3,2,1,0:T(8,128)S(1)}, pred[]{:T(512)}, ...), condition=%wide.region_1.2_spmd, body=%wide.region_0.1_spmd.sunk | while | flops 76857344 | bytes 4235497 | solution.py:122
  281.5 6.5 collective-permute-start.2
  300.2 6.5 collective-permute-start.2
  356.2 6.5 collective-permute-start.2
  374.9 6.5 collective-permute-start.2
  393.6 6.5 collective-permute-start.2
  412.2 6.5 collective-permute-start.2
  430.9 6.5 collective-permute-start.2
  449.6 6.5 collective-permute-start.2
  468.3 6.5 collective-permute-start.2
  487.0 6.5 collective-permute-start.2
  505.6 6.5 collective-permute-start.2
  524.3 6.5 collective-permute-start.2
  543.0 6.5 collective-permute-start.2
  561.7 6.5 collective-permute-start.2
  580.3 6.5 collective-permute-start.2
  599.0 6.5 collective-permute-start.2
  617.7 6.5 collective-permute-start.2
  636.4 6.5 collective-permute-start.2
  756.5 7.1 collective-permute-start.35
  764.9 7.1 collective-permute-start.51
  795.1 7.7 collective-permute-start.41
  814.5 6.8 collective-permute-start.44
  834.0 7.2 collective-permute-start.47
  853.7 7.2 collective-permute-start.53
  871.5 6.9 collective-permute-start.57
  894.2 126.1 %reduce-scatter.19.cloned.1.call-done = f32[72,128]{1,0:T(8,128)} async-done(((f32[1152,128]{1,0:T(8,128)}), f32[72,128]{1,0:T(8,128)}) %reduce-scatter.19.cloned.1.call-update) | async-done | bytes 36880
  1020.2 61.0 %reduce-scatter.17.cloned.1.call-done = f32[72,128]{1,0:T(8,128)} async-done(((f32[1152,128]{1,0:T(8,128)}), f32[72,128]{1,0:T(8,128)}) %reduce-scatter.17.cloned.1.call-update) | async-done | bytes 36880
  1081.3 60.8 %reduce-scatter.15.cloned.1.call-done = f32[72,128]{1,0:T(8,128)} async-done(((f32[1152,128]{1,0:T(8,128)}), f32[72,128]{1,0:T(8,128)}) %reduce-scatter.15.cloned.1.call-update) | async-done | bytes 36880
  1142.1 60.9 %reduce-scatter.13.cloned.1.call-done = f32[72,128]{1,0:T(8,128)} async-done(((f32[1152,128]{1,0:T(8,128)}), f32[72,128]{1,0:T(8,128)}) %reduce-scatter.13.cloned.1.call-update) | async-done | bytes 36880
  (1053 shorter events, 701.7 us)
Async XLA Ops:
  7.2 1013.0 %reduce-scatter.19.cloned.1.call-start = ((), (), s32[]{:S(2)}) async-start(), calls=%async_computation.7 | async-start | bytes 626688
  51.9 11.7 collective-permute-start.14
  53.2 10.4 collective-permute-start.13
  66.0 9.0 collective-permute-start.31
  92.1 13.0 %collective-permute-start.20 = (bf16[4,1,32,128]{3,2,1,0:T(8,128)(2,1)S(1)}, bf16[4,1,32,128]{3,2,1,0:T(8,128)(2,1)S(1)}, u32[]{:S(2)}, u32[]{:S(2)}) collective-permute-start(bf16[4,1,32,128]{3,2,1,0:T(8,128)(2,1)S(1)} %get-tuple-element.253), channel_id=1, source_target_pairs={{1,0},{2,1},{3,2},{4,3},{5,4},{6,5},{7,6},{8,7},{9,8},{10,9},{11,1... | collective-permute-start | bytes 98312 | tf_op jit(solution)/shard_map/ppermute | solution.py:20
  93.4 11.7 collective-permute-start.19
  98.6 9.0 collective-permute-start.32
  108.5 11.6 collective-permute-start.34
  109.8 10.3 collective-permute-start.33
  113.9 8.7 collective-permute-start.21
  199.8 8.7 collective-permute-start
  234.7 8.7 collective-permute-start
  252.2 8.7 collective-permute-start
  270.9 8.7 collective-permute-start
  289.6 8.7 collective-permute-start
  308.2 8.7 collective-permute-start
  326.9 8.7 collective-permute-start
  383.0 8.7 collective-permute-start
  439.0 8.7 collective-permute-start
  457.7 8.7 collective-permute-start
  513.7 8.7 collective-permute-start
  532.4 8.7 collective-permute-start
  756.5 17.1 %collective-permute-start.35 = (f32[4,2,32,128]{3,2,1,0:T(8,128)S(1)}, f32[4,2,32,128]{3,2,1,0:T(8,128)S(1)}, u32[]{:S(2)}, u32[]{:S(2)}) collective-permute-start(f32[4,2,32,128]{3,2,1,0:T(8,128)S(1)} %broadcast_select_fusion), channel_id=1, source_target_pairs={{0,16},{16,32},{32,48},{48,64},{64,80},{80,96},{96,112},{112,128},... | collective-permute-start | bytes 393224 | tf_op jit(solution)/shard_map/ppermute | solution.py:28
  763.6 16.5 %collective-permute-start.52 = (bf16[4,1,32,128]{3,2,1,0:T(8,128)(2,1)S(1)}, bf16[4,1,32,128]{3,2,1,0:T(8,128)(2,1)S(1)}, u32[]{:S(2)}, u32[]{:S(2)}) collective-permute-start(bf16[4,1,32,128]{3,2,1,0:T(8,128)(2,1)S(1)} %get-tuple-element.239), channel_id=1, source_target_pairs={{1,0},{2,1},{3,2},{4,3},{5,4},{6,5},{7,6},{8,7},{9,8},{10,9},{11,1... | collective-permute-start | bytes 98312 | tf_op jit(solution)/shard_map/ppermute | solution.py:20
  764.9 15.2 %collective-permute-start.51 = (bf16[4,1,32,128]{3,2,1,0:T(8,128)(2,1)S(1)}, bf16[4,1,32,128]{3,2,1,0:T(8,128)(2,1)S(1)}, u32[]{:S(2)}, u32[]{:S(2)}) collective-permute-start(bf16[4,1,32,128]{3,2,1,0:T(8,128)(2,1)S(1)} %get-tuple-element.238), channel_id=1, source_target_pairs={{0,1},{1,2},{2,3},{3,4},{4,5},{5,6},{6,7},{7,8},{8,9},{9,10},{10,1... | collective-permute-start | bytes 98312 | tf_op jit(solution)/shard_map/ppermute | solution.py:19
  795.1 10.2 collective-permute-start.41
  814.5 9.3 collective-permute-start.44
  870.2 15.6 %collective-permute-start.58 = (bf16[4,1,32,128]{3,2,1,0:T(8,128)(2,1)S(1)}, bf16[4,1,32,128]{3,2,1,0:T(8,128)(2,1)S(1)}, u32[]{:S(2)}, u32[]{:S(2)}) collective-permute-start(bf16[4,1,32,128]{3,2,1,0:T(8,128)(2,1)S(1)} %get-tuple-element.227), channel_id=1, source_target_pairs={{1,0},{2,1},{3,2},{4,3},{5,4},{6,5},{7,6},{8,7},{9,8},{10,9},{11,1... | collective-permute-start | bytes 98312 | tf_op jit(solution)/shard_map/ppermute | solution.py:20
  871.5 14.3 %collective-permute-start.57 = (bf16[4,1,32,128]{3,2,1,0:T(8,128)(2,1)S(1)}, bf16[4,1,32,128]{3,2,1,0:T(8,128)(2,1)S(1)}, u32[]{:S(2)}, u32[]{:S(2)}) collective-permute-start(bf16[4,1,32,128]{3,2,1,0:T(8,128)(2,1)S(1)} %get-tuple-element.226), channel_id=1, source_target_pairs={{0,1},{1,2},{2,3},{3,4},{4,5},{5,6},{6,7},{7,8},{8,9},{9,10},{10,1... | collective-permute-start | bytes 98312 | tf_op jit(solution)/shard_map/ppermute | solution.py:19
  888.4 192.9 %reduce-scatter.17.cloned.1.call-start = ((), (), s32[]{:S(2)}) async-start(), calls=%async_computation.6 | async-start | bytes 626688
  890.0 252.0 %reduce-scatter.15.cloned.1.call-start = ((), (), s32[]{:S(2)}) async-start(), calls=%async_computation.5 | async-start | bytes 626688
  891.5 311.4 %reduce-scatter.13.cloned.1.call-start = ((), (), s32[]{:S(2)}) async-start(), calls=%async_computation.4 | async-start | bytes 626688
  (135 other events, 1037.5 us)
Sparse Core Ops, SparseCore 0:
  888.5 131.7 reduce-scatter.18
  1023.3 57.9 reduce-scatter.16
  1084.1 57.9 reduce-scatter.14
  1144.9 57.9 reduce-scatter.12
where the time goes:
time: 1220 us; the launch traced here: 1210 us
  starting transfers between devices  666 us (55%)
  waiting for transfers between devices  460 us (38%)
  local copies, waits for them, and re-layouts  32.6 us (3%)
  matrix products  22.6 us (2%)
  between operations  16.4 us (1%)
    ppermute x55, starting transfers between devices, padded_2(): before = lax.ppermute(last, axis, up)  328 us
    unnamed x8, waiting for transfers between devices  309 us
    ppermute x44, starting transfers between devices, from_behind(): return lax.ppermute(block, axis, route)  268 us
    ppermute x44, waiting for transfers between devices, from_behind(): return lax.ppermute(block, axis, route)  110 us
    ppermute x55, starting transfers between devices, padded_2(): after = lax.ppermute(leading, axis, down)  70.7 us
    ppermute x55, waiting for transfers between devices, padded_2(): before = lax.ppermute(last, axis, up)  40.3 us
  transfers between devices with their start and end apart: 158, of which 97 were waited for; matrix products, arithmetic and copies ran while one was open for 1% of the time, Pallas kernels for 0%

commit v1 on v0

v1 whole, which is shorter than its diff:
```python
import jax
import jax.numpy as jnp
from jax import lax
from jax.experimental import pallas as pl
from jax.experimental.pallas import tpu as pltpu
from jax.sharding import PartitionSpec as P

STEP_SIZE = 0.1
SECTION = 4
SIDE = 32
CHANNELS = 128
PIXELS = SIDE * SIDE
PADDED = PIXELS + 2 * SIDE
PIECE = 128
CHUNK = 256
LOW = jnp.bfloat16
FULL = jnp.float32
SENT = jnp.float16

IMAGE = (PIXELS, CHANNELS)
PAD_SCRATCH = (PADDED, 3 * CHANNELS)


def clear(pad):
    edge = jnp.zeros((SIDE, 3 * CHANNELS), LOW)
    pad[0:SIDE, :] = edge
    pad[SIDE + PIXELS : PADDED, :] = edge


def put(pad, piece, values):
    column = lax.broadcasted_iota(jnp.int32, values.shape, 0) % SIDE
    left = jnp.where(column == 0, 0.0, pltpu.roll(values, 1, 0))
    right = jnp.where(column == SIDE - 1, 0.0, pltpu.roll(values, PIECE - 1, 0))
    rows = pl.ds(SIDE + piece * PIECE, PIECE)
    pad[rows, 0:CHANNELS] = left.astype(LOW)
    pad[rows, CHANNELS : 2 * CHANNELS] = values.astype(LOW)
    pad[rows, 2 * CHANNELS : 3 * CHANNELS] = right.astype(LOW)


def put_active(pad, state):
    for piece in range(PIXELS // PIECE):
        put(pad, piece, jnp.tanh(state[pl.ds(piece * PIECE, PIECE), :]))


def conv(pad, kernel, chunk):
    columns = jnp.concatenate(
        [pad[pl.ds(chunk * CHUNK + SIDE * shift, CHUNK), :] for shift in range(3)], axis=1
    )
    return jnp.dot(columns, kernel[...], preferred_element_type=FULL)


def chunks():
    return [(chunk, pl.ds(chunk * CHUNK, CHUNK)) for chunk in range(PIXELS // CHUNK)]


def relax_kernel(begin, weights, out, state, pad):
    clear(pad)
    state[...] = begin[...]

    def step(layer, carry):
        put_active(pad, state)
        for chunk, rows in chunks():
            state[rows, :] += STEP_SIZE * conv(pad, weights.at[layer], chunk)
        return carry

    lax.fori_loop(0, SECTION, step, 0)
    out[...] = state[...]


def fine_kernel(place, own, received, weights, closing, defect_out, send_out, state, base, first, pad):
    section, phase = place[0], place[1]
    clear(pad)
    for _, rows in chunks():
        begin = jnp.where(section == 0, own[rows, :], received[rows, :])
        state[rows, :] = begin
        base[rows, :] = begin

    put_active(pad, state)
    for chunk, rows in chunks():
        term = conv(pad, weights.at[0], chunk)
        first[rows, :] = term
        state[rows, :] += STEP_SIZE * term

    @pl.when(phase == 0)
    def _():
        for chunk, rows in chunks():
            long_term = (4 * SECTION * STEP_SIZE) * conv(pad, closing.at[SECTION - 1], chunk)
            base[rows, :] += long_term

    def step(layer, carry):
        put_active(pad, state)
        for chunk, rows in chunks():
            state[rows, :] += STEP_SIZE * conv(pad, weights.at[layer], chunk)
        return carry

    lax.fori_loop(1, SECTION, step, 0)
    for _, rows in chunks():
        begin = jnp.where(section == 0, own[rows, :], received[rows, :])
        last = state[rows, :]
        defect = (last - begin) - SECTION * STEP_SIZE * first[rows, :]
        defect_out[rows, :] = defect.astype(LOW)
        send_out[0, rows, :] = jnp.where(phase == 0, last, defect)
        total = jnp.where(section == 0, begin, last - base[rows, :])
        send_out[1, rows, :] = jnp.where(phase == 0, total, defect)


def first_round_kernel(place, sent, received, leading, out, state, pad):
    phase, in_first_group = place[1], place[0] < 4

    @pl.when(phase < 2)
    def _():
        clear(pad)
        for _, rows in chunks():
            state[rows, :] = jnp.where(phase == 0, sent[0, rows, :], received[0, rows, :])
        put_active(pad, state)
        for chunk, rows in chunks():
            defect = jnp.where(phase == 0, received[0, rows, :], sent[0, rows, :])
            total = jnp.where(phase == 0, sent[1, rows, :], received[1, rows, :])
            change = SECTION * STEP_SIZE * conv(pad, leading.at[1], chunk) + defect
            out[0, rows, :] = state[rows, :] + change
            out[1, rows, :] = total + jnp.where(in_first_group, 0.0, change)

    @pl.when(phase >= 2)
    def _():
        for _, rows in chunks():
            out[0, rows, :] = jnp.where(phase == 2, sent[0, rows, :], received[0, rows, :])
            out[1, rows, :] = jnp.where(phase == 2, received[0, rows, :], sent[0, rows, :])


def closing_kernel(place, sent, received, leading, out, total, state, pad):
    phase, in_first_group = place[1], place[0] < 4
    clear(pad)
    for _, rows in chunks():
        state[rows, :] = jnp.where(phase < 2, sent[0, rows, :], received[0, rows, :])
        total[rows, :] = jnp.where(phase < 2, sent[1, rows, :], received[1, rows, :])

    def step(turn, carry):
        put_active(pad, state)
        for chunk, rows in chunks():
            defect = jnp.where(phase < 2, received[turn, rows, :], sent[turn, rows, :])
            change = SECTION * STEP_SIZE * conv(pad, leading.at[2 + turn], chunk) + defect
            state[rows, :] += change
            total[rows, :] += jnp.where(in_first_group, 0.0, change)
        return carry

    lax.fori_loop(0, 2, step, 0)
    for _, rows in chunks():
        out[rows, :] = jnp.where(in_first_group, state[rows, :], total[rows, :])


def chain_kernel(place, images, received, mine, near, far, coarse, before_out, own_out, last_out, pad):
    state = last_out
    section, use_received, turn_of = place[0], place[2], place[3]
    clear(pad)
    for _, rows in chunks():
        state[rows, :] = jnp.where(use_received == 1, received[rows, :], 0.0)

    def step(turn, carry):
        @pl.when(turn == turn_of)
        def _():
            for _, rows in chunks():
                before_out[rows, :] = jnp.where(section < 4, images[rows, :], state[rows, :])

        put_active(pad, state)
        same_pair = turn // 2 == turn_of // 2
        same_place = turn % 2 == turn_of % 2
        place_in_pair = jnp.where(same_place, 0, 1)
        for chunk, rows in chunks():
            defect = jnp.where(same_place, mine[rows, :], near[rows, :])
            defect = jnp.where(same_pair, defect, far[place_in_pair, rows, :])
            state[rows, :] += (4 * SECTION * STEP_SIZE) * conv(pad, coarse.at[turn], chunk) + defect

        @pl.when(turn == turn_of)
        def _():
            own_out[...] = state[...]

        return carry

    lax.fori_loop(0, 4, step, 0)


def final_kernel(
    place, before, own, defects, leading, weights, flipped, end_adjoint,
    ends_out, grad_out,
    state, begin, end, slopes, change, pads, back_pad, grads,
):
    phase, replica = place[1], place[4]
    clear(back_pad)
    for layer in range(SECTION):
        clear(pads.at[layer])
    state[...] = before[...]
    begin[...] = before[...]
    end[...] = own[...]

    def level_step(turn, carry):
        put_active(back_pad, state)
        for chunk, rows in chunks():
            state[rows, :] += (
                SECTION * STEP_SIZE * conv(back_pad, leading.at[turn], chunk)
                + defects[turn, rows, :].astype(FULL)
            )

        @pl.when(phase == turn)
        def _():
            end[...] = state[...]

        @pl.when(phase == turn + 1)
        def _():
            begin[...] = state[...]

        return carry

    lax.fori_loop(0, 3, level_step, 0)

    def active(layer):
        for piece in range(PIXELS // PIECE):
            rows = pl.ds(piece * PIECE, PIECE)
            slope = jnp.tanh(begin[rows, :])
            slopes[layer, rows, :] = STEP_SIZE * (1.0 - slope * slope)
            put(pads.at[layer], piece, slope)

    def forward(layer, carry):
        active(layer)
        for chunk, rows in chunks():
            begin[rows, :] += STEP_SIZE * conv(pads.at[layer], weights.at[layer], chunk)
        return carry

    lax.fori_loop(0, SECTION - 1, forward, 0)
    active(SECTION - 1)
    change[...] = jnp.zeros(IMAGE, FULL)

    def backward(turn, carry):
        layer = SECTION - 1 - turn
        for piece in range(PIXELS // PIECE):
            rows = pl.ds(piece * PIECE, PIECE)
            put(back_pad, piece, end_adjoint[rows, :] + change[rows, :])
        low = back_pad[pl.ds(SIDE, PIXELS), CHANNELS : 2 * CHANNELS]
        for part in range(3):
            offset = 2 * replica + part
            columns = pads[
                layer,
                pl.ds(pl.multiple_of(SIDE * (offset // 3), SIDE), PIXELS),
                pl.ds(pl.multiple_of(CHANNELS * (offset % 3), CHANNELS), CHANNELS),
            ]
            grads[pl.ds(part * CHANNELS, CHANNELS), :] = STEP_SIZE * lax.dot_general(
                columns, low, (((0,), (0,)), ((), ())), preferred_element_type=FULL
            )
        grad_out[layer] = grads[pl.ds(pl.multiple_of(SIDE * replica, SIDE), 288), :].astype(LOW)
        for chunk, rows in chunks():
            change[rows, :] += slopes[layer, rows, :] * conv(back_pad, flipped.at[layer], chunk)
        return carry

    lax.fori_loop(0, SECTION, backward, 0)
    kept = pl.ds(pl.multiple_of(replica * 256, 256), 256)
    high = end[kept, :].astype(LOW)
    ends_out[0] = high
    ends_out[1] = (end[kept, :] - high.astype(FULL)).astype(LOW)
    ends_out[2] = change[kept, :].astype(LOW)


def call(body, outs, scratch, megabytes, place, *operands):
    held = pl.BlockSpec(memory_space=pltpu.VMEM)
    in_specs = [held] * len(operands)
    if place is not None:
        in_specs = [pl.BlockSpec(memory_space=pltpu.SMEM)] + in_specs
        operands = (place,) + operands
    return pl.pallas_call(
        body,
        out_shape=outs,
        in_specs=in_specs,
        out_specs=jax.tree.map(lambda _: held, outs),
        scratch_shapes=scratch,
        compiler_params=pltpu.CompilerParams(vmem_limit_bytes=megabytes * 1024 * 1024),
    )(*operands)


def shape(*dims, dtype=FULL):
    return jax.ShapeDtypeStruct(dims, dtype)


def wide():
    return pltpu.VMEM(IMAGE, FULL)


def padding():
    return pltpu.VMEM(PAD_SCRATCH, LOW)


def swap(block, distance, sections):
    moved = lax.ppermute(block.astype(SENT), "layer", [(i, i ^ distance) for i in range(sections)])
    return moved.astype(block.dtype)


def shift(block, distance, sections):
    route = [(i, i + distance) for i in range(sections - distance)]
    return lax.ppermute(block.astype(SENT), "layer", route).astype(block.dtype)


def local(images, end_guess, end_adjoint, weights):
    section = lax.axis_index("layer")
    tile = lax.axis_index("space")
    sections = lax.axis_size("layer")
    tiles = lax.axis_size("space")
    replica = tile // 4
    group = section // 4
    place = jnp.stack([section, section % 4, jnp.int32(0), group % 4, replica]).astype(jnp.int32)
    place_later = place.at[2].set(jnp.where(section >= 16, 1, 0))
    rows_of_groups = [[4 * g + i for i in range(4)] for g in range(sections // 4)]
    quads = [[16 * q + 4 * i + j for i in range(4)] for q in range(sections // 16) for j in range(4)]

    guess = jnp.where(section == 0, images, shift(end_guess[0], 1, sections))
    both = jnp.stack([guess, end_adjoint[0]], axis=1).astype(SENT)
    both = lax.all_to_all(jnp.tile(both, (tiles // 4, 1, 1, 1, 1)), "space", 0, 0, tiled=True)
    both = both.astype(FULL)
    start, adjoint_whole = both[:, 0].reshape(IMAGE), both[:, 1].reshape(IMAGE)

    leading = lax.all_gather(weights[0], "layer", axis_index_groups=rows_of_groups)
    flipped = (
        weights.reshape(SECTION, 9, CHANNELS, CHANNELS)[:, ::-1]
        .transpose(0, 1, 3, 2)
        .reshape(SECTION, 9 * CHANNELS, CHANNELS)
    )
    image_shape, pair_shape = shape(*IMAGE), shape(2, *IMAGE)

    relaxed = call(relax_kernel, image_shape, [wide(), padding()], 8, None, start, weights)
    received = shift(relaxed, 1, sections)
    closing_weights, _ = lax.optimization_barrier((leading[3], relaxed))
    coarse = lax.all_gather(closing_weights, "layer", axis_index_groups=quads)
    defect, send = call(
        fine_kernel,
        (shape(*IMAGE, dtype=LOW), pair_shape),
        [wide(), wide(), wide(), padding()],
        12, place, start, received, weights, leading,
    )
    defects = lax.all_gather(defect, "layer", axis_index_groups=rows_of_groups)
    received = swap(send, 1, sections)
    send = call(first_round_kernel, pair_shape, [wide(), padding()], 10, place, send, received, leading)
    received = swap(send, 2, sections)
    defect_two, base = call(
        closing_kernel, (image_shape, image_shape), [wide(), padding()], 10, place, send, received, leading
    )
    mine = defect_two.astype(SENT)
    near = lax.ppermute(mine, "layer", [(i, i ^ 4) for i in range(sections)])
    far = swap(jnp.stack([mine, near]), 8, sections).astype(FULL)
    near = near.astype(FULL)

    def chain(where, start_value):
        return call(
            chain_kernel,
            (image_shape, image_shape, image_shape),
            [padding()],
            12, where, base, start_value, defect_two, near, far, coarse,
        )

    last = chain(place, base)[2]
    before, own, _ = chain(place_later, shift(last, 16, sections))

    ends, grads = call(
        final_kernel,
        (shape(3, 256, CHANNELS, dtype=LOW), shape(SECTION, 288, CHANNELS, dtype=LOW)),
        [
            wide(), wide(), wide(),
            pltpu.VMEM((SECTION, *IMAGE), FULL),
            wide(),
            pltpu.VMEM((SECTION, *PAD_SCRATCH), LOW),
            padding(),
            pltpu.VMEM((3 * CHANNELS, CHANNELS), FULL),
        ],
        24, place, before, own, defects, leading, weights, flipped, adjoint_whole,
    )
    parts = jnp.concatenate(
        [
            ends.reshape(3, 4, 64, CHANNELS).transpose(1, 0, 2, 3).reshape(4, 192, CHANNELS),
            grads.reshape(SECTION, 4, 72, CHANNELS).transpose(1, 0, 2, 3).reshape(4, 288, CHANNELS),
        ],
        axis=1,
    )
    row_groups = [[4 * r + n for n in range(4)] for r in range(tiles // 4)]
    parts = lax.all_to_all(parts, "space", 0, 0, axis_index_groups=row_groups, tiled=True).astype(FULL)
    tile_shape = (1, 4, 2, SIDE, CHANNELS)
    section_ends = (parts[:, 0:64] + parts[:, 64:128]).reshape(tile_shape)
    start_adjoint = end_adjoint + parts[:, 128:192].reshape(tile_shape)
    weight_grad = parts[:, 192:].sum(0).reshape(SECTION, 72, CHANNELS)
    return section_ends, start_adjoint, weight_grad


def solution(mesh):
    return jax.shard_map(
        local,
        mesh=mesh,
        in_specs=(
            P(None, "space", None, None),
            P("layer", None, "space", None, None),
            P("layer", None, "space", None, None),
            P("layer", None, None),
        ),
        out_specs=(
            P("layer", None, "space", None, None),
            P("layer", None, "space", None, None),
            P("layer", "space", None),
        ),
        check_vma=False,
    )
```

time: 1220 us -> 223 us (0.18)
  the two profiles are of different devices: /device:TPU:6 before, /device:TPU:48 now
where the time goes in v1:
time: 223 us; the launch traced here: 222 us
  waiting for transfers between devices  83.4 us (37%)
  blocking collectives  37.1 us (17%)
  Pallas kernels  31.8 us (14%)
  local copies, waits for them, and re-layouts  25.8 us (12%)
  starting transfers between devices  19.5 us (9%)
  between operations  14.2 us (6%)
  other arithmetic  9.97 us (4%)
    ppermute x3, waiting for transfers between devices, swap(): lax.ppermute(block.astype(SENT), 'layer', [(i, i ^ distance) for i in ran...  49.4 us
    pallas_call x7, Pallas kernels, call(): pl.pallas_call(body, out_shape=outs, in_specs=in_specs, out_specs=jax.tre...  31.8 us
    ppermute x3, waiting for transfers between devices, shift(): return lax.ppermute(block.astype(SENT), 'layer', route).astype(block.dtype)  27.4 us
    all_to_all x1, blocking collectives, local(): lax.all_to_all(jnp.tile(both, (tiles // 4, 1, 1, 1, 1)), 'space', 0, 0, t...  26.2 us
    unnamed x45, local copies, waits for them, and re-layouts  17.3 us
    all_to_all x1, blocking collectives, local(): lax.all_to_all(parts, 'space', 0, 0, axis_index_groups=row_groups, tiled=...  10.9 us
    ppermute x3, starting transfers between devices, swap(): lax.ppermute(block.astype(SENT), 'layer', [(i, i ^ distance) for i in ran...  10 us
    ppermute x3, starting transfers between devices, shift(): return lax.ppermute(block.astype(SENT), 'layer', route).astype(block.dtype)  6.77 us
  transfers between devices with their start and end apart: 10, of which 7 were waited for; matrix products, arithmetic and copies ran while one was open for 6% of the time, Pallas kernels for 10%

profile of v1, /device:TPU:48, one launch (start us, length us, event | category | flops | bytes accessed | tf_op | source)
XLA Modules:
  0.0 221.7 jit_solution(1745317122910718512)
XLA Ops:
  8.2 3.4 %collective-permute-start = (f16[4,2,32,128]{3,2,1,0:T(8,128)(2,1)S(1)}, f16[4,2,32,128]{3,2,1,0:T(8,128)(2,1)S(1)}, u32[]{:S(2)}, u32[]{:S(2)}) collective-permute-start(f16[4,2,32,128]{3,2,1,0:T(8,128)(2,1)S(1)} %convert_bitcast_fusion.1), channel_id=1, source_target_pairs={{0,16},{16,32},{32,48},{48,64},{64,80},{80,96},{96,112},{112,128},... | collective-permute-start | bytes 196616 | tf_op jit(solution)/shard_map/ppermute | solution.py:296
  11.6 1.7 slice.35
  14.3 2.2 collective-permute-done
  16.7 26.2 %all_to_all.10 = f16[16,2,2,32,128]{4,3,2,1,0:T(8,128)(2,1)S(1)} all-to-all(f16[16,2,2,32,128]{4,3,2,1,0:T(8,128)(2,1)S(1)} %bitcast.46), channel_id=1, replica_groups=mesh['layer'=32,'space'=16] {'space'}, dimensions={0} | all-to-all | bytes 1048576 | tf_op jit(solution)/shard_map/all_to_all | solution.py:313
  44.5 3.2 %shard_map.67 = f32[1024,128]{1,0:T(8,128)S(1)} custom-call(f32[1024,128]{1,0:T(8,128)S(1)} %bitcast.40, bf16[4,1152,128]{2,1,0:T(8,128)(2,1)S(1)} %copy-done.1), custom_call_target="tpu_custom_call" | custom-call | tf_op jit(solution)/shard_map/pallas_call | solution.py:267
  47.8 1.8 slice_bitcast_fusion
  50.4 1.9 collective-permute-start.1
  52.5 10.7 %collective-permute-done.1 = f16[1024,128]{1,0:T(8,128)(2,1)S(1)} collective-permute-done((f16[1024,128]{1,0:T(8,128)(2,1)}, f16[1024,128]{1,0:T(8,128)(2,1)S(1)}, u32[]{:S(2)}, u32[]{:S(2)}) %collective-permute-start.1) | collective-permute-done | bytes 262176 | tf_op jit(solution)/shard_map/ppermute | solution.py:296
  63.2 4.6 %shard_map.68 = (bf16[1024,128]{1,0:T(8,128)(2,1)S(1)}, f32[2,1024,128]{2,1,0:T(8,128)S(1)}) custom-call(s32[5]{0:T(128)S(1)} %stack.36.place, f32[1024,128]{1,0:T(8,128)S(1)} %bitcast.41, f32[1024,128]{1,0:T(8,128)S(1)} %convert_element_type.58.received, bf16[4,1152,128]{2,1,0:T(8,128)(2,1)S(1)} %copy-done.1, bf16[4,1152,128]{2,1,0:T(8,128)(2,1)S(1)} %copy-done), custom_call_target="tpu_custom_call" | custom-call | tf_op jit(solution)/shard_map/pallas_call | solution.py:267
  68.6 1.9 collective-permute-start.2
  70.5 14.3 %collective-permute-done.2 = f16[2,1024,128]{2,1,0:T(8,128)(2,1)S(1)} collective-permute-done((f16[2,1024,128]{2,1,0:T(8,128)(2,1)S(1)}, f16[2,1024,128]{2,1,0:T(8,128)(2,1)S(1)}, u32[]{:S(2)}, u32[]{:S(2)}) %collective-permute-start.2) | collective-permute-done | bytes 524320 | tf_op jit(solution)/shard_map/ppermute | solution.py:290
  84.9 1.5 shard_map.69.sent
  87.3 1.9 collective-permute-start.3
  89.2 15.4 %collective-permute-done.3 = f16[2,1024,128]{2,1,0:T(8,128)(2,1)} collective-permute-done((f16[2,1024,128]{2,1,0:T(8,128)(2,1)}, f16[2,1024,128]{2,1,0:T(8,128)(2,1)}, u32[]{:S(2)}, u32[]{:S(2)}) %collective-permute-start.3) | collective-permute-done | bytes 524320 | tf_op jit(solution)/shard_map/ppermute | solution.py:290
  104.6 1.1 convert_element_type.62.received
  105.7 2.5 %shard_map.70 = (f32[1024,128]{1,0:T(8,128)S(1)}, f32[1024,128]{1,0:T(8,128)S(1)}) custom-call(s32[5]{0:T(128)S(1)} %stack.36.place, f32[2,1024,128]{2,1,0:T(8,128)S(1)} %shard_map.69.sent, f32[2,1024,128]{2,1,0:T(8,128)S(1)} %convert_element_type.62.received, bf16[4,1152,128]{2,1,0:T(8,128)(2,1)S(1)} %copy-done), custom_call_target="tpu_custom_call" | custom-call | tf_op jit(solution)/shard_map/pallas_call | solution.py:267
  108.3 2.6 %collective-permute-start.4 = (f16[1024,128]{1,0:T(8,128)(2,1)S(1)}, f16[1024,128]{1,0:T(8,128)(2,1)S(1)}, u32[]{:S(2)}, u32[]{:S(2)}) collective-permute-start(f16[1024,128]{1,0:T(8,128)(2,1)S(1)} %convert_element_type.63), channel_id=1, source_target_pairs={{0,64},{16,80},{32,96},{48,112},{64,0},{80,16},{96,32},{112,48},{1... | collective-permute-start | bytes 786440 | tf_op jit(solution)/shard_map/ppermute | solution.py:343
  110.9 6.4 %collective-permute-done.4 = f16[1024,128]{1,0:T(8,128)(2,1)S(1)} collective-permute-done((f16[1024,128]{1,0:T(8,128)(2,1)S(1)}, f16[1024,128]{1,0:T(8,128)(2,1)S(1)}, u32[]{:S(2)}, u32[]{:S(2)}) %collective-permute-start.4) | collective-permute-done | bytes 262176 | tf_op jit(solution)/shard_map/ppermute | solution.py:343
  117.5 6.2 %collective-permute-start.5 = (f16[2,1024,128]{2,1,0:T(8,128)(2,1)S(1)}, f16[2,1024,128]{2,1,0:T(8,128)(2,1)S(1)}, u32[]{:S(2)}, u32[]{:S(2)}) collective-permute-start(f16[2,1024,128]{2,1,0:T(8,128)(2,1)S(1)} %pad_maximum_fusion), channel_id=1, source_target_pairs={{0,128},{16,144},{32,160},{48,176},{64,192},{80,208},{96,224},{112... | collective-permute-start | bytes 1572872 | tf_op jit(solution)/shard_map/ppermute | solution.py:290
  124.5 19.7 %collective-permute-done.5 = f16[2,1024,128]{2,1,0:T(8,128)(2,1)S(1)} collective-permute-done((f16[2,1024,128]{2,1,0:T(8,128)(2,1)S(1)}, f16[2,1024,128]{2,1,0:T(8,128)(2,1)S(1)}, u32[]{:S(2)}, u32[]{:S(2)}) %collective-permute-start.5) | collective-permute-done | bytes 524320 | tf_op jit(solution)/shard_map/ppermute | solution.py:290
  145.4 1.3 copy-done.5
  148.8 5.2 %shard_map.71 = (f32[1024,128]{1,0:T(8,128)}, f32[1024,128]{1,0:T(8,128)}, f32[1024,128]{1,0:T(8,128)S(1)}) custom-call(s32[5]{0:T(128)S(1)} %stack.36.place, f32[1024,128]{1,0:T(8,128)S(1)} %copy-done.8, f32[1024,128]{1,0:T(8,128)S(1)} %copy-done.8, f32[1024,128]{1,0:T(8,128)S(1)} %copy-done.3, f32[1024,128]{1,0:T(8,128)S(1)} %copy-done.10, ...), custom_call_target="tpu_custom_call" | custom-call | tf_op jit(solution)/shard_map/pallas_call | solution.py:267
  154.7 1.5 collective-permute-start.6
  156.2 1.4 copy.12
  157.6 2.4 %rev.3 = bf16[4,9,128,128]{2,3,1,0:T(8,128)(2,1)} reverse(bf16[4,9,128,128]{2,3,1,0:T(8,128)(2,1)} %copy.12), dimensions={1} | reverse | bytes 2359296 | tf_op jit(solution)/shard_map/rev | solution.py:319
  160.0 14.6 %collective-permute-done.6 = f16[1024,128]{1,0:T(8,128)(2,1)} collective-permute-done((f16[1024,128]{1,0:T(8,128)(2,1)}, f16[1024,128]{1,0:T(8,128)(2,1)}, u32[]{:S(2)}, u32[]{:S(2)}) %collective-permute-start.6) | collective-permute-done | bytes 262176 | tf_op jit(solution)/shard_map/ppermute | solution.py:296
  176.7 1.3 copy-done.6
  180.0 4.6 %shard_map.72 = (f32[1024,128]{1,0:T(8,128)S(1)}, f32[1024,128]{1,0:T(8,128)S(1)}, f32[1024,128]{1,0:T(8,128)}) custom-call(s32[5]{0:T(128)S(1)} %constant_dynamic-update-slice_fusion.place, f32[1024,128]{1,0:T(8,128)S(1)} %copy-done.9, f32[1024,128]{1,0:T(8,128)S(1)} %convert_element_type.67.received, f32[1024,128]{1,0:T(8,128)S(1)} %copy-done.4, ...), custom_call_target="tpu_custom_call" | custom-call | tf_op jit(solution)/shard_map/pallas_call | solution.py:267
  186.3 1.3 copy-done.12
  188.6 1.2 copy-done.14
  191.9 10.2 %shard_map.73 = (bf16[3,256,128]{2,1,0:T(8,128)(2,1)S(1)}, bf16[4,288,128]{2,1,0:T(8,128)(2,1)S(1)}) custom-call(s32[5]{0:T(128)S(1)} %stack.36.place, f32[1024,128]{1,0:T(8,128)S(1)} %copy-done.16, f32[1024,128]{1,0:T(8,128)S(1)} %copy-done.18, bf16[4,1024,128]{2,1,0:T(8,128)(2,1)S(1)} %bitcast.43, bf16[4,1152,128]{2,1,0:T(8,128)(2,1)S(1)} %copy-done, ...), custom_call_target="tpu_custom_call" | custom-call | tf_op jit(solution)/shard_map/pallas_call | solution.py:267
  202.1 10.9 %all_to_all.11 = bf16[4,480,128]{2,1,0:T(8,128)(2,1)S(1)} all-to-all(bf16[4,480,128]{2,1,0:T(8,128)(2,1)S(1)} %pad_maximum_fusion.1), channel_id=1, replica_groups={{0,1,2,3},{4,5,6,7},{8,9,10,11},{12,13,14,15},{16,17,18,19},{20,21,22,2..., dimensions={0} | all-to-all | bytes 983040 | tf_op jit(solution)/shard_map/all_to_all | solution.py:379
  (80 shorter events, 22.5 us)
Async XLA Ops:
  7.2 9.3 %copy-start.21 = (f32[4,2,32,128]{3,2,1,0:T(8,128)S(1)}, f32[4,2,32,128]{3,2,1,0:T(8,128)}, u32[]{:S(2)}) copy-start(f32[4,2,32,128]{3,2,1,0:T(8,128)} %param.6) | copy-start | bytes 393220
  7.2 40.6 %all-gather.6.cloned.1.call-start = ((), (), s32[]{:S(2)}) async-start(), calls=%async_computation.2 | async-start | bytes 1474560 | tf_op jit(solution)/shard_map/all_gather | solution.py:317
  8.2 8.3 %collective-permute-start = (f16[4,2,32,128]{3,2,1,0:T(8,128)(2,1)S(1)}, f16[4,2,32,128]{3,2,1,0:T(8,128)(2,1)S(1)}, u32[]{:S(2)}, u32[]{:S(2)}) collective-permute-start(f16[4,2,32,128]{3,2,1,0:T(8,128)(2,1)S(1)} %convert_bitcast_fusion.1), channel_id=1, source_target_pairs={{0,16},{16,32},{32,48},{48,64},{64,80},{80,96},{96,112},{112,128},... | collective-permute-start | bytes 196616 | tf_op jit(solution)/shard_map/ppermute | solution.py:296
  13.3 131.1 %all-gather.8.cloned.1.call-start = ((), (), s32[]{:S(2)}) async-start(), calls=%async_computation.3 | async-start | bytes 1474560 | tf_op jit(solution)/shard_map/all_gather | solution.py:328
  43.0 1.5 copy-start.1
  47.8 15.4 %copy-start = (bf16[4,1152,128]{2,1,0:T(8,128)(2,1)S(1)}, bf16[4,1152,128]{2,1,0:T(8,128)(2,1)}, u32[]{:S(2)}) copy-start(bf16[4,1152,128]{2,1,0:T(8,128)(2,1)} %all-gather.6.cloned.1.call-done.closing.leading) | copy-start | bytes 3538948
  49.6 136.6 %all-gather.10.cloned.1.call-start = ((), (), s32[]{:S(2)}) async-start(), calls=%async_computation.4 | async-start | bytes 1310720 | tf_op jit(solution)/shard_map/all_gather | solution.py:335
  50.4 12.7 %collective-permute-start.1 = (f16[1024,128]{1,0:T(8,128)(2,1)}, f16[1024,128]{1,0:T(8,128)(2,1)S(1)}, u32[]{:S(2)}, u32[]{:S(2)}) collective-permute-start(f16[1024,128]{1,0:T(8,128)(2,1)} %convert_element_type.57), channel_id=1, source_target_pairs={{0,16},{16,32},{32,48},{48,64},{64,80},{80,96},{96,112},{112,128},... | collective-permute-start | bytes 786440 | tf_op jit(solution)/shard_map/ppermute | solution.py:296
  67.8 0.7 copy-start.19
  68.6 16.2 %collective-permute-start.2 = (f16[2,1024,128]{2,1,0:T(8,128)(2,1)S(1)}, f16[2,1024,128]{2,1,0:T(8,128)(2,1)S(1)}, u32[]{:S(2)}, u32[]{:S(2)}) collective-permute-start(f16[2,1024,128]{2,1,0:T(8,128)(2,1)S(1)} %convert_element_type.59), channel_id=1, source_target_pairs={{0,16},{16,0},{32,48},{48,32},{64,80},{80,64},{96,112},{112,96},{1... | collective-permute-start | bytes 1572872 | tf_op jit(solution)/shard_map/ppermute | solution.py:290
  87.3 17.3 %collective-permute-start.3 = (f16[2,1024,128]{2,1,0:T(8,128)(2,1)}, f16[2,1024,128]{2,1,0:T(8,128)(2,1)}, u32[]{:S(2)}, u32[]{:S(2)}) collective-permute-start(f16[2,1024,128]{2,1,0:T(8,128)(2,1)} %convert_element_type.61), channel_id=1, source_target_pairs={{0,32},{16,48},{32,0},{48,16},{64,96},{80,112},{96,64},{112,80},{1... | collective-permute-start | bytes 1572872 | tf_op jit(solution)/shard_map/ppermute | solution.py:290
  108.2 9.3 %copy-start.2 = (f32[1024,128]{1,0:T(8,128)}, f32[1024,128]{1,0:T(8,128)S(1)}, u32[]{:S(2)}) copy-start(f32[1024,128]{1,0:T(8,128)S(1)} %get-tuple-element.27.mine) | copy-start | bytes 1572868
  108.2 9.3 %copy-start.7 = (f32[1024,128]{1,0:T(8,128)}, f32[1024,128]{1,0:T(8,128)S(1)}, u32[]{:S(2)}) copy-start(f32[1024,128]{1,0:T(8,128)S(1)} %get-tuple-element.26.images.received) | copy-start | bytes 1572868
  108.3 9.0 %collective-permute-start.4 = (f16[1024,128]{1,0:T(8,128)(2,1)S(1)}, f16[1024,128]{1,0:T(8,128)(2,1)S(1)}, u32[]{:S(2)}, u32[]{:S(2)}) collective-permute-start(f16[1024,128]{1,0:T(8,128)(2,1)S(1)} %convert_element_type.63), channel_id=1, source_target_pairs={{0,64},{16,80},{32,96},{48,112},{64,0},{80,16},{96,32},{112,48},{1... | collective-permute-start | bytes 786440 | tf_op jit(solution)/shard_map/ppermute | solution.py:343
  117.5 26.8 %collective-permute-start.5 = (f16[2,1024,128]{2,1,0:T(8,128)(2,1)S(1)}, f16[2,1024,128]{2,1,0:T(8,128)(2,1)S(1)}, u32[]{:S(2)}, u32[]{:S(2)}) collective-permute-start(f16[2,1024,128]{2,1,0:T(8,128)(2,1)S(1)} %pad_maximum_fusion), channel_id=1, source_target_pairs={{0,128},{16,144},{32,160},{48,176},{64,192},{80,208},{96,224},{112... | collective-permute-start | bytes 1572872 | tf_op jit(solution)/shard_map/ppermute | solution.py:290
  144.4 1.0 copy-start.3
  145.4 1.3 copy-start.5
  146.7 1.0 copy-start.8
  147.7 1.0 copy-start.10
  154.7 19.9 %collective-permute-start.6 = (f16[1024,128]{1,0:T(8,128)(2,1)}, f16[1024,128]{1,0:T(8,128)(2,1)}, u32[]{:S(2)}, u32[]{:S(2)}) collective-permute-start(f16[1024,128]{1,0:T(8,128)(2,1)} %convert_element_type.66), channel_id=1, source_target_pairs={{0,256},{16,272},{32,288},{48,304},{64,320},{80,336},{96,352},{112... | collective-permute-start | bytes 786440 | tf_op jit(solution)/shard_map/ppermute | solution.py:296
  175.6 1.0 copy-start.4
  176.7 1.3 copy-start.6
  177.9 1.0 copy-start.9
  179.0 1.0 copy-start.11
  184.6 0.8 copy-start.15
  185.4 0.8 copy-start.17
  186.3 1.3 copy-start.12
  187.5 1.0 copy-start.13
  188.6 1.2 copy-start.14
  189.8 1.0 copy-start.16
  190.8 1.0 copy-start.18
  213.0 1.4 copy-start.20
Sparse Core Ops, SparseCore 0:
  13.4 33.5 all-gather.5
  49.7 35.9 all-gather.7
  89.3 29.1 all-gather.9

commit v2 on v1

--- a/solution.py
+++ b/solution.py
@@ -67,9 +67,12 @@
     out[...] = state[...]
 
 
-def fine_kernel(place, own, received, weights, closing, defect_out, send_out, state, base, first, pad):
+def fine_kernel(
+    place, own, received, weights, closing, defect_out, send_out, closing_out, state, base, first, pad
+):
     section, phase = place[0], place[1]
     clear(pad)
+    closing_out[...] = closing[SECTION - 1]
     for _, rows in chunks():
         begin = jnp.where(section == 0, own[rows, :], received[rows, :])
         state[rows, :] = begin
@@ -148,49 +151,48 @@
         out[rows, :] = jnp.where(in_first_group, state[rows, :], total[rows, :])
 
 
-def chain_kernel(place, images, received, mine, near, far, coarse, before_out, own_out, last_out, pad):
-    state = last_out
-    section, use_received, turn_of = place[0], place[2], place[3]
-    clear(pad)
-    for _, rows in chunks():
-        state[rows, :] = jnp.where(use_received == 1, received[rows, :], 0.0)
-
-    def step(turn, carry):
-        @pl.when(turn == turn_of)
-        def _():
-            for _, rows in chunks():
-                before_out[rows, :] = jnp.where(section < 4, images[rows, :], state[rows, :])
-
-        put_active(pad, state)
-        same_pair = turn // 2 == turn_of // 2
-        same_place = turn % 2 == turn_of % 2
-        place_in_pair = jnp.where(same_place, 0, 1)
-        for chunk, rows in chunks():
-            defect = jnp.where(same_place, mine[rows, :], near[rows, :])
-            defect = jnp.where(same_pair, defect, far[place_in_pair, rows, :])
-            state[rows, :] += (4 * SECTION * STEP_SIZE) * conv(pad, coarse.at[turn], chunk) + defect
-
-        @pl.when(turn == turn_of)
-        def _():
-            own_out[...] = state[...]
-
-        return carry
-
-    lax.fori_loop(0, 4, step, 0)
-
-
-def final_kernel(
-    place, before, own, defects, leading, weights, flipped, end_adjoint,
-    ends_out, grad_out,
-    state, begin, end, slopes, change, pads, back_pad, grads,
-):
-    phase, replica = place[1], place[4]
+def final_kernel(place, *refs):
+    stored, (ends_out, grad_out), refs = refs[:15], refs[15:17], refs[17:]
+    state, begin, end, slopes, change, pads, back_pad, grads, slots = refs[:9]
+    held, arrived = refs[9:16], refs[16]
+    coarse, images, defects, leading, weights, flipped, end_adjoint = held
+    phase, group, replica = place[1], place[2], place[3]
+    targets = [slots.at[number] for number in range(8)] + list(held)
+    copies = [
+        pltpu.make_async_copy(source, target, arrived.at[number])
+        for number, (source, target) in enumerate(zip(stored, targets))
+    ]
+    for copy in copies:
+        copy.start()
     clear(back_pad)
     for layer in range(SECTION):
         clear(pads.at[layer])
-    state[...] = before[...]
-    begin[...] = before[...]
-    end[...] = own[...]
+
+    for copy in copies[:10]:
+        copy.wait()
+    for _, rows in chunks():
+        state[rows, :] = slots[group, rows, :]
+
+    def chain_step(turn, carry):
+        put_active(back_pad, state)
+        for chunk, rows in chunks():
+            long_term = (4 * SECTION * STEP_SIZE) * conv(back_pad, coarse.at[turn], chunk)
+            state[rows, :] += long_term + slots[group - turn, rows, :]
+        return carry
+
+    lax.fori_loop(1, group, chain_step, 0)
+    for _, rows in chunks():
+        begin[rows, :] = jnp.where(group == 0, images[rows, :], state[rows, :])
+
+    @pl.when(group > 0)
+    def _():
+        chain_step(group, 0)
+
+    for _, rows in chunks():
+        end[rows, :] = state[rows, :]
+        state[rows, :] = begin[rows, :]
+    for copy in copies[10:]:
+        copy.wait()
 
     def level_step(turn, carry):
         put_active(back_pad, state)
@@ -258,9 +260,10 @@
     ends_out[2] = change[kept, :].astype(LOW)
 
 
-def call(body, outs, scratch, megabytes, place, *operands):
+def call(body, outs, scratch, megabytes, place, *operands, stored=()):
     held = pl.BlockSpec(memory_space=pltpu.VMEM)
-    in_specs = [held] * len(operands)
+    in_specs = [held] * len(operands) + [pl.BlockSpec(memory_space=pltpu.HBM)] * len(stored)
+    operands += tuple(stored)
     if place is not None:
         in_specs = [pl.BlockSpec(memory_space=pltpu.SMEM)] + in_specs
         operands = (place,) + operands
@@ -303,10 +306,9 @@
     tiles = lax.axis_size("space")
     replica = tile // 4
     group = section // 4
-    place = jnp.stack([section, section % 4, jnp.int32(0), group % 4, replica]).astype(jnp.int32)
-    place_later = place.at[2].set(jnp.where(section >= 16, 1, 0))
+    place = jnp.stack([section, section % 4, group, replica]).astype(jnp.int32)
     rows_of_groups = [[4 * g + i for i in range(4)] for g in range(sections // 4)]
-    quads = [[16 * q + 4 * i + j for i in range(4)] for q in range(sections // 16) for j in range(4)]
+    columns_of_groups = [[4 * g + i for g in range(sections // 4)] for i in range(4)]
 
     guess = jnp.where(section == 0, images, shift(end_guess[0], 1, sections))
     both = jnp.stack([guess, end_adjoint[0]], axis=1).astype(SENT)
@@ -324,37 +326,30 @@
 
     relaxed = call(relax_kernel, image_shape, [wide(), padding()], 8, None, start, weights)
     received = shift(relaxed, 1, sections)
-    closing_weights, _ = lax.optimization_barrier((leading[3], relaxed))
-    coarse = lax.all_gather(closing_weights, "layer", axis_index_groups=quads)
-    defect, send = call(
+    defect, send, closing_weights = call(
         fine_kernel,
-        (shape(*IMAGE, dtype=LOW), pair_shape),
+        (shape(*IMAGE, dtype=LOW), pair_shape, shape(9 * CHANNELS, CHANNELS, dtype=LOW)),
         [wide(), wide(), wide(), padding()],
         12, place, start, received, weights, leading,
     )
+    coarse = lax.all_gather(closing_weights, "layer", axis_index_groups=columns_of_groups)
     defects = lax.all_gather(defect, "layer", axis_index_groups=rows_of_groups)
     received = swap(send, 1, sections)
     send = call(first_round_kernel, pair_shape, [wide(), padding()], 10, place, send, received, leading)
-    received = swap(send, 2, sections)
+    received = swap(send, 3, sections)
     defect_two, base = call(
         closing_kernel, (image_shape, image_shape), [wide(), padding()], 10, place, send, received, leading
     )
-    mine = defect_two.astype(SENT)
-    near = lax.ppermute(mine, "layer", [(i, i ^ 4) for i in range(sections)])
-    far = swap(jnp.stack([mine, near]), 8, sections).astype(FULL)
-    near = near.astype(FULL)
-
-    def chain(where, start_value):
-        return call(
-            chain_kernel,
-            (image_shape, image_shape, image_shape),
-            [padding()],
-            12, where, base, start_value, defect_two, near, far, coarse,
-        )
-
-    last = chain(place, base)[2]
-    before, own, _ = chain(place_later, shift(last, 16, sections))
-
+    up = [(i, (i + 4) % sections) for i in range(sections)]
+    down = [(j, i) for i, j in up]
+    ups, downs = [defect_two.astype(SENT)], [defect_two.astype(SENT)]
+    for turn in range(4):
+        ups.append(lax.ppermute(ups[-1], "layer", up))
+        if turn < 3:
+            downs.append(lax.ppermute(downs[-1], "layer", down))
+    slots = [defect_two] + [block.astype(FULL) for block in ups[1:] + downs[:0:-1]]
+
+    stored = (coarse, base, defects, leading, weights, flipped, adjoint_whole)
     ends, grads = call(
         final_kernel,
         (shape(3, 256, CHANNELS, dtype=LOW), shape(SECTION, 288, CHANNELS, dtype=LOW)),
@@ -365,8 +360,11 @@
             pltpu.VMEM((SECTION, *PAD_SCRATCH), LOW),
             padding(),
             pltpu.VMEM((3 * CHANNELS, CHANNELS), FULL),
+            pltpu.VMEM((8, *IMAGE), FULL),
+            *[pltpu.VMEM(array.shape, array.dtype) for array in stored],
+            pltpu.SemaphoreType.DMA((8 + len(stored),)),
         ],
-        24, place, before, own, defects, leading, weights, flipped, adjoint_whole,
+        60, place, stored=(*slots, *stored),
     )
     parts = jnp.concatenate(
         [

time: 223 us -> 211 us (0.946)
  the two profiles are of different devices: /device:TPU:48 before, /device:TPU:24 now
where the time goes in v2:
time: 211 us; the launch traced here: 210 us
  waiting for transfers between devices  65 us (31%)
  starting transfers between devices  40.3 us (19%)
  blocking collectives  37.1 us (18%)
  Pallas kernels  28.4 us (13%)
  other arithmetic  14.4 us (7%)
  between operations  14.1 us (7%)
  local copies, waits for them, and re-layouts  10.5 us (5%)
    ppermute x2, waiting for transfers between devices, swap(): lax.ppermute(block.astype(SENT), 'layer', [(i, i ^ distance) for i in ran...  31.4 us
    pallas_call x5, Pallas kernels, call(): pl.pallas_call(body, out_shape=outs, in_specs=in_specs, out_specs=jax.tre...  28.4 us
    all_to_all x1, blocking collectives, local(): lax.all_to_all(jnp.tile(both, (tiles // 4, 1, 1, 1, 1)), 'space', 0, 0, t...  26.2 us
    ppermute x4, starting transfers between devices, local(): ups.append(lax.ppermute(ups[-1], 'layer', up))  24.9 us
    ppermute x4, waiting for transfers between devices, local(): ups.append(lax.ppermute(ups[-1], 'layer', up))  19.4 us
    ppermute x2, waiting for transfers between devices, shift(): return lax.ppermute(block.astype(SENT), 'layer', route).astype(block.dtype)  12.6 us
    all_to_all x1, blocking collectives, local(): lax.all_to_all(parts, 'space', 0, 0, axis_index_groups=row_groups, tiled=...  10.9 us
    convert_element_type x7, other arithmetic, local(): block.astype(FULL)  9.75 us
  transfers between devices with their start and end apart: 14, of which 9 were waited for; matrix products, arithmetic and copies ran while one was open for 8% of the time, Pallas kernels for 3%

profile of v2, /device:TPU:24, one launch (start us, length us, event | category | flops | bytes accessed | tf_op | source)
XLA Modules:
  0.0 209.9 jit_solution(2687926244608745647)
XLA Ops:
  8.2 3.4 %collective-permute-start = (f16[4,2,32,128]{3,2,1,0:T(8,128)(2,1)S(1)}, f16[4,2,32,128]{3,2,1,0:T(8,128)(2,1)S(1)}, u32[]{:S(2)}, u32[]{:S(2)}) collective-permute-start(f16[4,2,32,128]{3,2,1,0:T(8,128)(2,1)S(1)} %convert_bitcast_fusion.1), channel_id=1, source_target_pairs={{0,16},{16,32},{32,48},{48,64},{64,80},{80,96},{96,112},{112,128},... | collective-permute-start | bytes 196616 | tf_op jit(solution)/shard_map/ppermute | solution.py:299
  11.6 1.7 slice.22
  14.3 2.2 %collective-permute-done = f16[4,2,32,128]{3,2,1,0:T(8,128)(2,1)S(1)} collective-permute-done((f16[4,2,32,128]{3,2,1,0:T(8,128)(2,1)S(1)}, f16[4,2,32,128]{3,2,1,0:T(8,128)(2,1)S(1)}, u32[]{:S(2)}, u32[]{:S(2)}) %collective-permute-start) | collective-permute-done | bytes 65568 | tf_op jit(solution)/shard_map/ppermute | solution.py:299
  16.7 26.2 %all_to_all.10 = f16[16,2,2,32,128]{4,3,2,1,0:T(8,128)(2,1)S(1)} all-to-all(f16[16,2,2,32,128]{4,3,2,1,0:T(8,128)(2,1)S(1)} %bitcast.35), channel_id=1, replica_groups=mesh['layer'=32,'space'=16] {'space'}, dimensions={0} | all-to-all | bytes 1048576 | tf_op jit(solution)/shard_map/all_to_all | solution.py:315
  44.5 3.2 %shard_map.67 = f32[1024,128]{1,0:T(8,128)S(1)} custom-call(f32[1024,128]{1,0:T(8,128)S(1)} %bitcast.31, bf16[4,1152,128]{2,1,0:T(8,128)(2,1)S(1)} %copy-done), custom_call_target="tpu_custom_call" | custom-call | tf_op jit(solution)/shard_map/pallas_call | solution.py:270
  47.8 1.9 collective-permute-start.1
  49.8 10.5 %collective-permute-done.1 = f16[1024,128]{1,0:T(8,128)(2,1)S(1)} collective-permute-done((f16[1024,128]{1,0:T(8,128)(2,1)S(1)}, f16[1024,128]{1,0:T(8,128)(2,1)S(1)}, u32[]{:S(2)}, u32[]{:S(2)}) %collective-permute-start.1) | collective-permute-done | bytes 262176 | tf_op jit(solution)/shard_map/ppermute | solution.py:299
  60.4 1.3 copy-done.1
  61.6 4.6 %shard_map.68 = (bf16[1024,128]{1,0:T(8,128)(2,1)S(1)}, f32[2,1024,128]{2,1,0:T(8,128)S(1)}, bf16[1152,128]{1,0:T(8,128)(2,1)S(1)}) custom-call(s32[4]{0:T(128)S(1)} %pad_add_fusion.place, f32[1024,128]{1,0:T(8,128)S(1)} %bitcast.32, f32[1024,128]{1,0:T(8,128)S(1)} %convert_element_type.68.received, bf16[4,1152,128]{2,1,0:T(8,128)(2,1)S(1)} %copy-done, ...), custom_call_target="tpu_custom_call" | custom-call | tf_op jit(solution)/shard_map/pallas_call | solution.py:270
  68.6 2.1 collective-permute-start.2
  70.6 15.9 %collective-permute-done.2 = f16[2,1024,128]{2,1,0:T(8,128)(2,1)S(1)} collective-permute-done((f16[2,1024,128]{2,1,0:T(8,128)(2,1)S(1)}, f16[2,1024,128]{2,1,0:T(8,128)(2,1)S(1)}, u32[]{:S(2)}, u32[]{:S(2)}) %collective-permute-start.2) | collective-permute-done | bytes 524320 | tf_op jit(solution)/shard_map/ppermute | solution.py:293
  86.6 1.5 shard_map.69.sent
  88.2 2.1 %collective-permute-start.3 = (f16[2,1024,128]{2,1,0:T(8,128)(2,1)S(1)}, f16[2,1024,128]{2,1,0:T(8,128)(2,1)S(1)}, u32[]{:S(2)}, u32[]{:S(2)}) collective-permute-start(f16[2,1024,128]{2,1,0:T(8,128)(2,1)S(1)} %convert_element_type.71), channel_id=1, source_target_pairs={{0,48},{16,32},{32,16},{48,0},{64,112},{80,96},{96,80},{112,64},{1... | collective-permute-start | bytes 1572872 | tf_op jit(solution)/shard_map/ppermute | solution.py:293
  90.3 15.4 %collective-permute-done.3 = f16[2,1024,128]{2,1,0:T(8,128)(2,1)S(1)} collective-permute-done((f16[2,1024,128]{2,1,0:T(8,128)(2,1)S(1)}, f16[2,1024,128]{2,1,0:T(8,128)(2,1)S(1)}, u32[]{:S(2)}, u32[]{:S(2)}) %collective-permute-start.3) | collective-permute-done | bytes 524320 | tf_op jit(solution)/shard_map/ppermute | solution.py:293
  105.8 2.4 %shard_map.70 = (f32[1024,128]{1,0:T(8,128)S(1)}, f32[1024,128]{1,0:T(8,128)S(1)}) custom-call(s32[4]{0:T(128)S(1)} %pad_add_fusion.place, f32[2,1024,128]{2,1,0:T(8,128)S(1)} %shard_map.69.sent, f32[2,1024,128]{2,1,0:T(8,128)S(1)} %convert_element_type.72.received, bf16[4,1152,128]{2,1,0:T(8,128)(2,1)S(1)} %copy-done.2), custom_call_target="tpu_custom_call" | custom-call | tf_op jit(solution)/shard_map/pallas_call | solution.py:270
  109.1 8.0 %collective-permute-start.4 = (f16[1024,128]{1,0:T(8,128)(2,1)S(1)}, f16[1024,128]{1,0:T(8,128)(2,1)S(1)}, u32[]{:S(2)}, u32[]{:S(2)}) collective-permute-start(f16[1024,128]{1,0:T(8,128)(2,1)S(1)} %convert_element_type.73), channel_id=1, source_target_pairs={{0,64},{16,80},{32,96},{48,112},{64,128},{80,144},{96,160},{112,17... | collective-permute-start | bytes 786440 | tf_op jit(solution)/shard_map/ppermute | solution.py:347
  117.1 1.9 collective-permute-start.8
  119.0 9.1 %collective-permute-done.4 = f16[1024,128]{1,0:T(8,128)(2,1)S(1)} collective-permute-done((f16[1024,128]{1,0:T(8,128)(2,1)S(1)}, f16[1024,128]{1,0:T(8,128)(2,1)S(1)}, u32[]{:S(2)}, u32[]{:S(2)}) %collective-permute-start.4) | collective-permute-done | bytes 262176 | tf_op jit(solution)/shard_map/ppermute | solution.py:347
  128.1 5.6 %collective-permute-start.5 = (f16[1024,128]{1,0:T(8,128)(2,1)S(1)}, f16[1024,128]{1,0:T(8,128)(2,1)S(1)}, u32[]{:S(2)}, u32[]{:S(2)}) collective-permute-start(f16[1024,128]{1,0:T(8,128)(2,1)S(1)} %collective-permute-done.4), channel_id=1, source_target_pairs={{0,64},{16,80},{32,96},{48,112},{64,128},{80,144},{96,160},{112,17... | collective-permute-start | bytes 786440 | tf_op jit(solution)/shard_map/ppermute | solution.py:347
  133.9 1.9 collective-permute-start.9
  135.8 8.4 %collective-permute-done.5 = f16[1024,128]{1,0:T(8,128)(2,1)S(1)} collective-permute-done((f16[1024,128]{1,0:T(8,128)(2,1)S(1)}, f16[1024,128]{1,0:T(8,128)(2,1)S(1)}, u32[]{:S(2)}, u32[]{:S(2)}) %collective-permute-start.5) | collective-permute-done | bytes 262176 | tf_op jit(solution)/shard_map/ppermute | solution.py:347
  144.2 5.6 %collective-permute-start.6 = (f16[1024,128]{1,0:T(8,128)(2,1)S(1)}, f16[1024,128]{1,0:T(8,128)(2,1)}, u32[]{:S(2)}, u32[]{:S(2)}) collective-permute-start(f16[1024,128]{1,0:T(8,128)(2,1)S(1)} %collective-permute-done.5), channel_id=1, source_target_pairs={{0,64},{16,80},{32,96},{48,112},{64,128},{80,144},{96,160},{112,17... | collective-permute-start | bytes 786440 | tf_op jit(solution)/shard_map/ppermute | solution.py:347
  150.6 1.9 collective-permute-start.10
  152.5 1.9 collective-permute-done.6
  154.4 5.7 %collective-permute-start.7 = (f16[1024,128]{1,0:T(8,128)(2,1)}, f16[1024,128]{1,0:T(8,128)(2,1)}, u32[]{:S(2)}, u32[]{:S(2)}) collective-permute-start(f16[1024,128]{1,0:T(8,128)(2,1)} %collective-permute-done.6), channel_id=1, source_target_pairs={{0,64},{16,80},{32,96},{48,112},{64,128},{80,144},{96,160},{112,17... | collective-permute-start | bytes 786440 | tf_op jit(solution)/shard_map/ppermute | solution.py:347
  160.8 1.1 rev.3
  164.5 1.8 convert_element_type.79.refs_6_
  166.3 1.8 convert_element_type.76.refs_3_
  168.1 1.8 convert_element_type.78.refs_5_
  169.9 1.8 convert_element_type.77.refs_4_
  171.7 16.6 %shard_map.71 = (bf16[3,256,128]{2,1,0:T(8,128)(2,1)}, bf16[4,288,128]{2,1,0:T(8,128)(2,1)}) custom-call(s32[4]{0:T(128)} %copy-done.7, f32[1024,128]{1,0:T(8,128)} %copy-done.3, f32[1024,128]{1,0:T(8,128)} %convert_element_type.74.refs_1_, f32[1024,128]{1,0:T(8,128)} %convert_element_type.75.refs_2_, f32[1024,128]{1,0:T(8,128)} %convert_element_type.76.refs_3_, ...), custom_call_target="tpu_custom_call" | custom-call | tf_op jit(solution)/shard_map/pallas_call | solution.py:270
  190.3 10.9 %all_to_all.11 = bf16[4,480,128]{2,1,0:T(8,128)(2,1)S(1)} all-to-all(bf16[4,480,128]{2,1,0:T(8,128)(2,1)S(1)} %pad_maximum_fusion), channel_id=1, replica_groups={{0,1,2,3},{4,5,6,7},{8,9,10,11},{12,13,14,15},{16,17,18,19},{20,21,22,2..., dimensions={0} | all-to-all | bytes 983040 | tf_op jit(solution)/shard_map/all_to_all | solution.py:377
  (64 shorter events, 15.5 us)
Async XLA Ops:
  7.2 9.3 %copy-start.11 = (f32[4,2,32,128]{3,2,1,0:T(8,128)S(1)}, f32[4,2,32,128]{3,2,1,0:T(8,128)}, u32[]{:S(2)}) copy-start(f32[4,2,32,128]{3,2,1,0:T(8,128)} %param.4) | copy-start | bytes 393220
  7.2 53.2 %all-gather.6.cloned.1.call-start = ((), (), s32[]{:S(2)}) async-start(), calls=%async_computation.2 | async-start | bytes 1474560 | tf_op jit(solution)/shard_map/all_gather | solution.py:319
  8.2 8.3 %collective-permute-start = (f16[4,2,32,128]{3,2,1,0:T(8,128)(2,1)S(1)}, f16[4,2,32,128]{3,2,1,0:T(8,128)(2,1)S(1)}, u32[]{:S(2)}, u32[]{:S(2)}) collective-permute-start(f16[4,2,32,128]{3,2,1,0:T(8,128)(2,1)S(1)} %convert_bitcast_fusion.1), channel_id=1, source_target_pairs={{0,16},{16,32},{32,48},{48,64},{64,80},{80,96},{96,112},{112,128},... | collective-permute-start | bytes 196616 | tf_op jit(solution)/shard_map/ppermute | solution.py:299
  13.3 158.4 %all-gather.10.cloned.1.call-start = ((), (), s32[]{:S(2)}) async-start(), calls=%async_computation.4 | async-start | bytes 1310720 | tf_op jit(solution)/shard_map/all_gather | solution.py:336
  43.0 1.5 copy-start
  47.8 12.5 %collective-permute-start.1 = (f16[1024,128]{1,0:T(8,128)(2,1)S(1)}, f16[1024,128]{1,0:T(8,128)(2,1)S(1)}, u32[]{:S(2)}, u32[]{:S(2)}) collective-permute-start(f16[1024,128]{1,0:T(8,128)(2,1)S(1)} %convert_element_type.67), channel_id=1, source_target_pairs={{0,16},{16,32},{32,48},{48,64},{64,80},{80,96},{96,112},{112,128},... | collective-permute-start | bytes 786440 | tf_op jit(solution)/shard_map/ppermute | solution.py:299
  49.8 56.0 %copy-start.7 = (s32[4]{0:T(128)}, s32[4]{0:T(128)S(1)}, u32[]{:S(2)}) copy-start(s32[4]{0:T(128)S(1)} %pad_add_fusion.place) | copy-start | bytes 52
  60.4 1.3 copy-start.1
  66.3 0.7 copy-start.5
  67.0 0.7 copy-start.6
  67.7 104.0 %all-gather.8.cloned.1.call-start = ((), (), s32[]{:S(2)}) async-start(), calls=%async_computation.3 | async-start | bytes 2654208 | tf_op jit(solution)/shard_map/all_gather | solution.py:335
  68.5 18.1 %copy-start.2 = (bf16[4,1152,128]{2,1,0:T(8,128)(2,1)S(1)}, bf16[4,1152,128]{2,1,0:T(8,128)(2,1)}, u32[]{:S(2)}) copy-start(bf16[4,1152,128]{2,1,0:T(8,128)(2,1)} %all-gather.6.cloned.1.call-done.closing.leading.refs_11_) | copy-start | bytes 3538948
  68.6 18.0 %collective-permute-start.2 = (f16[2,1024,128]{2,1,0:T(8,128)(2,1)S(1)}, f16[2,1024,128]{2,1,0:T(8,128)(2,1)S(1)}, u32[]{:S(2)}, u32[]{:S(2)}) collective-permute-start(f16[2,1024,128]{2,1,0:T(8,128)(2,1)S(1)} %convert_element_type.69), channel_id=1, source_target_pairs={{0,16},{16,0},{32,48},{48,32},{64,80},{80,64},{96,112},{112,96},{1... | collective-permute-start | bytes 1572872 | tf_op jit(solution)/shard_map/ppermute | solution.py:293
  88.2 17.5 %collective-permute-start.3 = (f16[2,1024,128]{2,1,0:T(8,128)(2,1)S(1)}, f16[2,1024,128]{2,1,0:T(8,128)(2,1)S(1)}, u32[]{:S(2)}, u32[]{:S(2)}) collective-permute-start(f16[2,1024,128]{2,1,0:T(8,128)(2,1)S(1)} %convert_element_type.71), channel_id=1, source_target_pairs={{0,48},{16,32},{32,16},{48,0},{64,112},{80,96},{96,80},{112,64},{1... | collective-permute-start | bytes 1572872 | tf_op jit(solution)/shard_map/ppermute | solution.py:293
  108.2 0.8 copy-start.4
  109.0 51.8 %copy-start.3 = (f32[1024,128]{1,0:T(8,128)}, f32[1024,128]{1,0:T(8,128)S(1)}, u32[]{:S(2)}) copy-start(f32[1024,128]{1,0:T(8,128)S(1)} %get-tuple-element.11.refs_0_) | copy-start | bytes 1572868
  109.1 19.1 %collective-permute-start.4 = (f16[1024,128]{1,0:T(8,128)(2,1)S(1)}, f16[1024,128]{1,0:T(8,128)(2,1)S(1)}, u32[]{:S(2)}, u32[]{:S(2)}) collective-permute-start(f16[1024,128]{1,0:T(8,128)(2,1)S(1)} %convert_element_type.73), channel_id=1, source_target_pairs={{0,64},{16,80},{32,96},{48,112},{64,128},{80,144},{96,160},{112,17... | collective-permute-start | bytes 786440 | tf_op jit(solution)/shard_map/ppermute | solution.py:347
  117.1 16.8 %collective-permute-start.8 = (f16[1024,128]{1,0:T(8,128)(2,1)S(1)}, f16[1024,128]{1,0:T(8,128)(2,1)S(1)}, u32[]{:S(2)}, u32[]{:S(2)}) collective-permute-start(f16[1024,128]{1,0:T(8,128)(2,1)S(1)} %convert_element_type.73), channel_id=1, source_target_pairs={{64,0},{80,16},{96,32},{112,48},{128,64},{144,80},{160,96},{176,11... | collective-permute-start | bytes 786440 | tf_op jit(solution)/shard_map/ppermute | solution.py:349
  128.1 16.1 %collective-permute-start.5 = (f16[1024,128]{1,0:T(8,128)(2,1)S(1)}, f16[1024,128]{1,0:T(8,128)(2,1)S(1)}, u32[]{:S(2)}, u32[]{:S(2)}) collective-permute-start(f16[1024,128]{1,0:T(8,128)(2,1)S(1)} %collective-permute-done.4), channel_id=1, source_target_pairs={{0,64},{16,80},{32,96},{48,112},{64,128},{80,144},{96,160},{112,17... | collective-permute-start | bytes 786440 | tf_op jit(solution)/shard_map/ppermute | solution.py:347
  133.9 16.6 %collective-permute-start.9 = (f16[1024,128]{1,0:T(8,128)(2,1)S(1)}, f16[1024,128]{1,0:T(8,128)(2,1)}, u32[]{:S(2)}, u32[]{:S(2)}) collective-permute-start(f16[1024,128]{1,0:T(8,128)(2,1)S(1)} %collective-permute-done.8), channel_id=1, source_target_pairs={{64,0},{80,16},{96,32},{112,48},{128,64},{144,80},{160,96},{176,11... | collective-permute-start | bytes 786440 | tf_op jit(solution)/shard_map/ppermute | solution.py:349
  144.2 15.8 %copy-start.9 = (f16[1024,128]{1,0:T(8,128)(2,1)}, f16[1024,128]{1,0:T(8,128)(2,1)S(1)}, u32[]{:S(2)}) copy-start(f16[1024,128]{1,0:T(8,128)(2,1)S(1)} %collective-permute-done.5) | copy-start | bytes 786436
  144.2 10.1 %collective-permute-start.6 = (f16[1024,128]{1,0:T(8,128)(2,1)S(1)}, f16[1024,128]{1,0:T(8,128)(2,1)}, u32[]{:S(2)}, u32[]{:S(2)}) collective-permute-start(f16[1024,128]{1,0:T(8,128)(2,1)S(1)} %collective-permute-done.5), channel_id=1, source_target_pairs={{0,64},{16,80},{32,96},{48,112},{64,128},{80,144},{96,160},{112,17... | collective-permute-start | bytes 786440 | tf_op jit(solution)/shard_map/ppermute | solution.py:347
  150.6 17.5 %collective-permute-start.10 = (f16[1024,128]{1,0:T(8,128)(2,1)}, f16[1024,128]{1,0:T(8,128)(2,1)}, u32[]{:S(2)}, u32[]{:S(2)}) collective-permute-start(f16[1024,128]{1,0:T(8,128)(2,1)} %collective-permute-done.9), channel_id=1, source_target_pairs={{64,0},{80,16},{96,32},{112,48},{128,64},{144,80},{160,96},{176,11... | collective-permute-start | bytes 786440 | tf_op jit(solution)/shard_map/ppermute | solution.py:349
  154.4 15.5 %collective-permute-start.7 = (f16[1024,128]{1,0:T(8,128)(2,1)}, f16[1024,128]{1,0:T(8,128)(2,1)}, u32[]{:S(2)}, u32[]{:S(2)}) collective-permute-start(f16[1024,128]{1,0:T(8,128)(2,1)} %collective-permute-done.6), channel_id=1, source_target_pairs={{0,64},{16,80},{32,96},{48,112},{64,128},{80,144},{96,160},{112,17... | collective-permute-start | bytes 786440 | tf_op jit(solution)/shard_map/ppermute | solution.py:347
  161.9 1.7 copy-start.10
  201.2 1.4 copy-start.8
Sparse Core Ops, SparseCore 0:
  13.4 33.8 all-gather.5
  67.9 28.5 all-gather.9
  98.5 54.4 all-gather.7

commit v3 on v2

--- a/solution.py
+++ b/solution.py
@@ -67,12 +67,9 @@
     out[...] = state[...]
 
 
-def fine_kernel(
-    place, own, received, weights, closing, defect_out, send_out, closing_out, state, base, first, pad
-):
+def fine_kernel(place, own, received, weights, closing, defect_out, send_out, state, base, first, pad):
     section, phase = place[0], place[1]
     clear(pad)
-    closing_out[...] = closing[SECTION - 1]
     for _, rows in chunks():
         begin = jnp.where(section == 0, own[rows, :], received[rows, :])
         state[rows, :] = begin
@@ -151,48 +148,58 @@
         out[rows, :] = jnp.where(in_first_group, state[rows, :], total[rows, :])
 
 
-def final_kernel(place, *refs):
-    stored, (ends_out, grad_out), refs = refs[:15], refs[15:17], refs[17:]
-    state, begin, end, slopes, change, pads, back_pad, grads, slots = refs[:9]
-    held, arrived = refs[9:16], refs[16]
-    coarse, images, defects, leading, weights, flipped, end_adjoint = held
-    phase, group, replica = place[1], place[2], place[3]
-    targets = [slots.at[number] for number in range(8)] + list(held)
+def load(sources, targets, arrived):
     copies = [
         pltpu.make_async_copy(source, target, arrived.at[number])
-        for number, (source, target) in enumerate(zip(stored, targets))
+        for number, (source, target) in enumerate(zip(sources, targets))
     ]
     for copy in copies:
         copy.start()
+    return copies
+
+
+def chain_kernel(place, *refs):
+    stored, outs, (state, begin, pad, slots, coarse, images, arrived) = refs[:10], refs[10:12], refs[12:]
+    group = place[2]
+    copies = load(stored, [slots.at[number] for number in range(8)] + [coarse, images], arrived)
+    clear(pad)
+    for copy in copies:
+        copy.wait()
+    for _, rows in chunks():
+        state[rows, :] = slots[group, rows, :]
+
+    def chain_step(turn, carry):
+        put_active(pad, state)
+        for chunk, rows in chunks():
+            long_term = (4 * SECTION * STEP_SIZE) * conv(pad, coarse.at[turn], chunk)
+            state[rows, :] += long_term + slots[group - turn, rows, :]
+        return carry
+
+    lax.fori_loop(1, group, chain_step, 0)
+    for _, rows in chunks():
+        begin[rows, :] = jnp.where(group == 0, images[rows, :], state[rows, :])
+
+    @pl.when(group > 0)
+    def _():
+        chain_step(group, 0)
+
+    for copy in load([begin, state], outs, arrived):
+        copy.wait()
+
+
+def final_kernel(place, *refs):
+    stored, (ends_out, grad_out), refs = refs[:7], refs[7:9], refs[9:]
+    begin, slopes, change, pads, back_pad, grads = refs[:6]
+    held, arrived = refs[6:13], refs[13]
+    state, end, defects, leading, weights, flipped, end_adjoint = held
+    phase, replica = place[1], place[3]
+    copies = load(stored, held, arrived)
     clear(back_pad)
     for layer in range(SECTION):
         clear(pads.at[layer])
-
-    for copy in copies[:10]:
+    for copy in copies[:4]:
         copy.wait()
-    for _, rows in chunks():
-        state[rows, :] = slots[group, rows, :]
-
-    def chain_step(turn, carry):
-        put_active(back_pad, state)
-        for chunk, rows in chunks():
-            long_term = (4 * SECTION * STEP_SIZE) * conv(back_pad, coarse.at[turn], chunk)
-            state[rows, :] += long_term + slots[group - turn, rows, :]
-        return carry
-
-    lax.fori_loop(1, group, chain_step, 0)
-    for _, rows in chunks():
-        begin[rows, :] = jnp.where(group == 0, images[rows, :], state[rows, :])
-
-    @pl.when(group > 0)
-    def _():
-        chain_step(group, 0)
-
-    for _, rows in chunks():
-        end[rows, :] = state[rows, :]
-        state[rows, :] = begin[rows, :]
-    for copy in copies[10:]:
-        copy.wait()
+    begin[...] = state[...]
 
     def level_step(turn, carry):
         put_active(back_pad, state)
@@ -213,6 +220,8 @@
         return carry
 
     lax.fori_loop(0, 3, level_step, 0)
+    for copy in copies[4:]:
+        copy.wait()
 
     def active(layer):
         for piece in range(PIXELS // PIECE):
@@ -260,7 +269,7 @@
     ends_out[2] = change[kept, :].astype(LOW)
 
 
-def call(body, outs, scratch, megabytes, place, *operands, stored=()):
+def call(body, outs, scratch, megabytes, place, *operands, stored=(), store=False):
     held = pl.BlockSpec(memory_space=pltpu.VMEM)
     in_specs = [held] * len(operands) + [pl.BlockSpec(memory_space=pltpu.HBM)] * len(stored)
     operands += tuple(stored)
@@ -271,7 +280,7 @@
         body,
         out_shape=outs,
         in_specs=in_specs,
-        out_specs=jax.tree.map(lambda _: held, outs),
+        out_specs=jax.tree.map(lambda _: pl.BlockSpec(memory_space=pltpu.HBM) if store else held, outs),
         scratch_shapes=scratch,
         compiler_params=pltpu.CompilerParams(vmem_limit_bytes=megabytes * 1024 * 1024),
     )(*operands)
@@ -310,13 +319,14 @@
     rows_of_groups = [[4 * g + i for i in range(4)] for g in range(sections // 4)]
     columns_of_groups = [[4 * g + i for g in range(sections // 4)] for i in range(4)]
 
-    guess = jnp.where(section == 0, images, shift(end_guess[0], 1, sections))
+    guess, leading = lax.optimization_barrier((end_guess[0].astype(SENT), weights[0]))
+    leading = lax.all_gather(leading, "layer", axis_index_groups=rows_of_groups)
+    guess = jnp.where(section == 0, images, shift(guess, 1, sections).astype(FULL))
     both = jnp.stack([guess, end_adjoint[0]], axis=1).astype(SENT)
     both = lax.all_to_all(jnp.tile(both, (tiles // 4, 1, 1, 1, 1)), "space", 0, 0, tiled=True)
     both = both.astype(FULL)
     start, adjoint_whole = both[:, 0].reshape(IMAGE), both[:, 1].reshape(IMAGE)
 
-    leading = lax.all_gather(weights[0], "layer", axis_index_groups=rows_of_groups)
     flipped = (
         weights.reshape(SECTION, 9, CHANNELS, CHANNELS)[:, ::-1]
         .transpose(0, 1, 3, 2)
@@ -325,14 +335,15 @@
     image_shape, pair_shape = shape(*IMAGE), shape(2, *IMAGE)
 
     relaxed = call(relax_kernel, image_shape, [wide(), padding()], 8, None, start, weights)
+    closing_weights, _ = lax.optimization_barrier((leading[3], relaxed))
     received = shift(relaxed, 1, sections)
-    defect, send, closing_weights = call(
+    coarse = lax.all_gather(closing_weights, "layer", axis_index_groups=columns_of_groups)
+    defect, send = call(
         fine_kernel,
-        (shape(*IMAGE, dtype=LOW), pair_shape, shape(9 * CHANNELS, CHANNELS, dtype=LOW)),
+        (shape(*IMAGE, dtype=LOW), pair_shape),
         [wide(), wide(), wide(), padding()],
         12, place, start, received, weights, leading,
     )
-    coarse = lax.all_gather(closing_weights, "layer", axis_index_groups=columns_of_groups)
     defects = lax.all_gather(defect, "layer", axis_index_groups=rows_of_groups)
     received = swap(send, 1, sections)
     send = call(first_round_kernel, pair_shape, [wide(), padding()], 10, place, send, received, leading)
@@ -342,29 +353,49 @@
     )
     up = [(i, (i + 4) % sections) for i in range(sections)]
     down = [(j, i) for i, j in up]
-    ups, downs = [defect_two.astype(SENT)], [defect_two.astype(SENT)]
+    ups, downs, widened = [defect_two.astype(SENT)], [defect_two.astype(SENT)], {}
     for turn in range(4):
-        ups.append(lax.ppermute(ups[-1], "layer", up))
+        moved = [lax.ppermute(ups[-1], "layer", up)]
         if turn < 3:
-            downs.append(lax.ppermute(downs[-1], "layer", down))
-    slots = [defect_two] + [block.astype(FULL) for block in ups[1:] + downs[:0:-1]]
-
-    stored = (coarse, base, defects, leading, weights, flipped, adjoint_whole)
+            moved.append(lax.ppermute(downs[-1], "layer", down))
+        if turn:
+            ready = [ups[-1].astype(FULL), downs[-1].astype(FULL)]
+            moved, (widened[turn], widened[8 - turn]) = lax.optimization_barrier((moved, ready))
+        ups.append(moved[0])
+        if turn < 3:
+            downs.append(moved[1])
+    widened[4] = ups[-1].astype(FULL)
+    slots = [defect_two] + [widened[distance] for distance in range(1, 8)]
+
+    def scratch_like(*arrays):
+        return [pltpu.VMEM(array.shape, array.dtype) for array in arrays]
+
+    before, own = call(
+        chain_kernel,
+        (image_shape, image_shape),
+        [
+            wide(), wide(), padding(),
+            pltpu.VMEM((8, *IMAGE), FULL),
+            *scratch_like(coarse, base),
+            pltpu.SemaphoreType.DMA((10,)),
+        ],
+        60, place, stored=(*slots, coarse, base), store=True,
+    )
+    stored = (before, own, defects, leading, weights, flipped, adjoint_whole)
     ends, grads = call(
         final_kernel,
         (shape(3, 256, CHANNELS, dtype=LOW), shape(SECTION, 288, CHANNELS, dtype=LOW)),
         [
-            wide(), wide(), wide(),
+            wide(),
             pltpu.VMEM((SECTION, *IMAGE), FULL),
             wide(),
             pltpu.VMEM((SECTION, *PAD_SCRATCH), LOW),
             padding(),
             pltpu.VMEM((3 * CHANNELS, CHANNELS), FULL),
-            pltpu.VMEM((8, *IMAGE), FULL),
-            *[pltpu.VMEM(array.shape, array.dtype) for array in stored],
-            pltpu.SemaphoreType.DMA((8 + len(stored),)),
+            *scratch_like(*stored),
+            pltpu.SemaphoreType.DMA((len(stored),)),
         ],
-        60, place, stored=(*slots, *stored),
+        60, place, stored=stored,
     )
     parts = jnp.concatenate(
         [

time: 211 us -> 202 us (0.957)
  starting transfers between devices: 40.3 us -> 34 us
  waiting for transfers between devices: 65 us -> 61.3 us
  Pallas kernels: 28.4 us -> 31.9 us
    ppermute x7, starting transfers between devices: 30.7 us -> 24.7 us  [the longest x4 16.9 us: local(): moved = [lax.ppermute(ups[-1], 'layer', up)]]
    pallas_call x5 -> x6, Pallas kernels: 28.4 us -> 31.9 us  [call(): pl.pallas_call(body, out_shape=outs, in_specs=in_specs, out_specs=jax.tre...]
    ppermute x7, waiting for transfers between devices: 20.3 us -> 17.3 us  [the longest x4 8.78 us: local(): moved = [lax.ppermute(ups[-1], 'layer', up)]]
    convert_element_type x8 -> x9, other arithmetic: 9.79 us -> 6.96 us  [the longest x6 5.17 us: local(): ready = [ups[-1].astype(FULL), downs[-1].astype(FULL)]]
    unnamed x24 -> x16, local copies, waits for them, and re-layouts: 4.05 us -> 1.28 us
  transfers between devices with their start and end apart: 14 -> 14, of which waited for: 9 -> 10; matrix products, arithmetic and copies ran while one was open for 8% -> 6% of each run, Pallas kernels for 3% -> 9%
where the time goes in v3:
time: 202 us; the launch traced here: 201 us
  waiting for transfers between devices  61.3 us (30%)
  blocking collectives  37.1 us (18%)
  starting transfers between devices  34 us (17%)
  Pallas kernels  31.9 us (16%)
  between operations  14.1 us (7%)
  other arithmetic  13.2 us (7%)
  local copies, waits for them, and re-layouts  9.63 us (5%)
    pallas_call x6, Pallas kernels, call(): pl.pallas_call(body, out_shape=outs, in_specs=in_specs, out_specs=jax.tre...  31.9 us
    ppermute x2, waiting for transfers between devices, swap(): lax.ppermute(block.astype(SENT), 'layer', [(i, i ^ distance) for i in ran...  29.4 us
    all_to_all x1, blocking collectives, local(): lax.all_to_all(jnp.tile(both, (tiles // 4, 1, 1, 1, 1)), 'space', 0, 0, t...  26.2 us
    ppermute x4, starting transfers between devices, local(): moved = [lax.ppermute(ups[-1], 'layer', up)]  16.9 us
    ppermute x2, waiting for transfers between devices, shift(): return lax.ppermute(block.astype(SENT), 'layer', route).astype(block.dtype)  14.5 us
    all_to_all x1, blocking collectives, local(): lax.all_to_all(parts, 'space', 0, 0, axis_index_groups=row_groups, tiled=...  10.9 us
    ppermute x4, waiting for transfers between devices, local(): moved = [lax.ppermute(ups[-1], 'layer', up)]  8.78 us
    ppermute x3, waiting for transfers between devices, local(): moved.append(lax.ppermute(downs[-1], 'layer', down))  8.48 us
  transfers between devices with their start and end apart: 14, of which 10 were waited for; matrix products, arithmetic and copies ran while one was open for 6% of the time, Pallas kernels for 9%

profile of v3, /device:TPU:24, one launch (start us, length us, event | category | flops | bytes accessed | tf_op | source)
XLA Modules:
  0.0 201.2 jit_solution(14948852733707215425)
XLA Ops:
  7.2 1.7 slice_bitcast_fusion
  9.9 3.4 %collective-permute-start = (f16[4,2,32,128]{3,2,1,0:T(8,128)(2,1)S(1)}, f16[4,2,32,128]{3,2,1,0:T(8,128)(2,1)S(1)}, u32[]{:S(2)}, u32[]{:S(2)}) collective-permute-start(f16[4,2,32,128]{3,2,1,0:T(8,128)(2,1)S(1)} %convert_bitcast_fusion.1), channel_id=1, source_target_pairs={{0,16},{16,32},{32,48},{48,64},{64,80},{80,96},{96,112},{112,128},... | collective-permute-start | bytes 196616 | tf_op jit(solution)/shard_map/ppermute | solution.py:308
  14.3 3.9 %collective-permute-done = f16[4,2,32,128]{3,2,1,0:T(8,128)(2,1)S(1)} collective-permute-done((f16[4,2,32,128]{3,2,1,0:T(8,128)(2,1)S(1)}, f16[4,2,32,128]{3,2,1,0:T(8,128)(2,1)S(1)}, u32[]{:S(2)}, u32[]{:S(2)}) %collective-permute-start) | collective-permute-done | bytes 65568 | tf_op jit(solution)/shard_map/ppermute | solution.py:308
  18.4 26.2 %all_to_all.10 = f16[16,2,2,32,128]{4,3,2,1,0:T(8,128)(2,1)S(1)} all-to-all(f16[16,2,2,32,128]{4,3,2,1,0:T(8,128)(2,1)S(1)} %bitcast.42), channel_id=1, replica_groups=mesh['layer'=32,'space'=16] {'space'}, dimensions={0} | all-to-all | bytes 1048576 | tf_op jit(solution)/shard_map/all_to_all | solution.py:326
  46.2 3.2 %shard_map.67 = f32[1024,128]{1,0:T(8,128)S(1)} custom-call(f32[1024,128]{1,0:T(8,128)S(1)} %bitcast.38, bf16[4,1152,128]{2,1,0:T(8,128)(2,1)S(1)} %copy-done.1), custom_call_target="tpu_custom_call" | custom-call | tf_op jit(solution)/shard_map/pallas_call | solution.py:279
  49.5 1.8 slice.34
  52.1 1.9 collective-permute-start.1
  54.1 10.7 %collective-permute-done.1 = f16[1024,128]{1,0:T(8,128)(2,1)S(1)} collective-permute-done((f16[1024,128]{1,0:T(8,128)(2,1)}, f16[1024,128]{1,0:T(8,128)(2,1)S(1)}, u32[]{:S(2)}, u32[]{:S(2)}) %collective-permute-start.1) | collective-permute-done | bytes 262176 | tf_op jit(solution)/shard_map/ppermute | solution.py:308
  64.8 4.6 %shard_map.68 = (bf16[1024,128]{1,0:T(8,128)(2,1)S(1)}, f32[2,1024,128]{2,1,0:T(8,128)S(1)}) custom-call(s32[4]{0:T(128)S(1)} %pad_add_fusion.place, f32[1024,128]{1,0:T(8,128)S(1)} %bitcast.39, f32[1024,128]{1,0:T(8,128)S(1)} %convert_element_type.68.received, bf16[4,1152,128]{2,1,0:T(8,128)(2,1)S(1)} %copy-done.1, bf16[4,1152,128]{2,1,0:T(8,128)(2,1)S(1)} %bitcast.34), custom_call_target="tpu_custom_call" | custom-call | tf_op jit(solution)/shard_map/pallas_call | solution.py:279
  70.2 1.9 collective-permute-start.2
  72.2 14.3 %collective-permute-done.2 = f16[2,1024,128]{2,1,0:T(8,128)(2,1)S(1)} collective-permute-done((f16[2,1024,128]{2,1,0:T(8,128)(2,1)S(1)}, f16[2,1024,128]{2,1,0:T(8,128)(2,1)S(1)}, u32[]{:S(2)}, u32[]{:S(2)}) %collective-permute-start.2) | collective-permute-done | bytes 524320 | tf_op jit(solution)/shard_map/ppermute | solution.py:302
  86.5 1.5 shard_map.69.sent
  88.9 1.9 collective-permute-start.3
  90.9 15.1 %collective-permute-done.3 = f16[2,1024,128]{2,1,0:T(8,128)(2,1)} collective-permute-done((f16[2,1024,128]{2,1,0:T(8,128)(2,1)}, f16[2,1024,128]{2,1,0:T(8,128)(2,1)}, u32[]{:S(2)}, u32[]{:S(2)}) %collective-permute-start.3) | collective-permute-done | bytes 524320 | tf_op jit(solution)/shard_map/ppermute | solution.py:302
  106.0 1.1 convert_element_type.72.received
  107.1 2.4 %shard_map.70 = (f32[1024,128]{1,0:T(8,128)S(1)}, f32[1024,128]{1,0:T(8,128)S(1)}) custom-call(s32[4]{0:T(128)S(1)} %pad_add_fusion.place, f32[2,1024,128]{2,1,0:T(8,128)S(1)} %shard_map.69.sent, f32[2,1024,128]{2,1,0:T(8,128)S(1)} %convert_element_type.72.received, bf16[4,1152,128]{2,1,0:T(8,128)(2,1)S(1)} %bitcast.36), custom_call_target="tpu_custom_call" | custom-call | tf_op jit(solution)/shard_map/pallas_call | solution.py:279
  109.6 7.5 %collective-permute-start.4 = (f16[1024,128]{1,0:T(8,128)(2,1)S(1)}, f16[1024,128]{1,0:T(8,128)(2,1)S(1)}, u32[]{:S(2)}, u32[]{:S(2)}) collective-permute-start(f16[1024,128]{1,0:T(8,128)(2,1)S(1)} %convert_element_type.73), channel_id=1, source_target_pairs={{0,64},{16,80},{32,96},{48,112},{64,128},{80,144},{96,160},{112,17... | collective-permute-start | bytes 786440 | tf_op jit(solution)/shard_map/ppermute | solution.py:358
  117.2 1.9 collective-permute-start.6
  119.1 3.9 %collective-permute-done.4 = f16[1024,128]{1,0:T(8,128)(2,1)S(1)} collective-permute-done((f16[1024,128]{1,0:T(8,128)(2,1)S(1)}, f16[1024,128]{1,0:T(8,128)(2,1)S(1)}, u32[]{:S(2)}, u32[]{:S(2)}) %collective-permute-start.4) | collective-permute-done | bytes 262176 | tf_op jit(solution)/shard_map/ppermute | solution.py:358
  123.0 5.6 %collective-permute-start.5 = (f16[1024,128]{1,0:T(8,128)(2,1)S(1)}, f16[1024,128]{1,0:T(8,128)(2,1)S(1)}, u32[]{:S(2)}, u32[]{:S(2)}) collective-permute-start(f16[1024,128]{1,0:T(8,128)(2,1)S(1)} %collective-permute-done.4), channel_id=1, source_target_pairs={{0,64},{16,80},{32,96},{48,112},{64,128},{80,144},{96,160},{112,17... | collective-permute-start | bytes 786440 | tf_op jit(solution)/shard_map/ppermute | solution.py:358
  128.6 1.9 collective-permute-start.7
  132.2 1.4 collective-permute-done.5
  133.7 5.3 %collective-permute-done.7 = f16[1024,128]{1,0:T(8,128)(2,1)S(1)} collective-permute-done((f16[1024,128]{1,0:T(8,128)(2,1)S(1)}, f16[1024,128]{1,0:T(8,128)(2,1)S(1)}, u32[]{:S(2)}, u32[]{:S(2)}) %collective-permute-start.7) | collective-permute-done | bytes 262176 | tf_op jit(solution)/shard_map/ppermute | solution.py:360
  139.0 1.9 collective-permute-start.8
  140.9 3.9 %collective-permute-start.9 = (f16[1024,128]{1,0:T(8,128)(2,1)S(1)}, f16[1024,128]{1,0:T(8,128)(2,1)S(1)}, u32[]{:S(2)}, u32[]{:S(2)}) collective-permute-start(f16[1024,128]{1,0:T(8,128)(2,1)S(1)} %collective-permute-done.7), channel_id=1, source_target_pairs={{64,0},{80,16},{96,32},{112,48},{128,64},{144,80},{160,96},{176,11... | collective-permute-start | bytes 786440 | tf_op jit(solution)/shard_map/ppermute | solution.py:360
  147.3 3.1 %collective-permute-done.9 = f16[1024,128]{1,0:T(8,128)(2,1)S(1)} collective-permute-done((f16[1024,128]{1,0:T(8,128)(2,1)S(1)}, f16[1024,128]{1,0:T(8,128)(2,1)S(1)}, u32[]{:S(2)}, u32[]{:S(2)}) %collective-permute-start.9) | collective-permute-done | bytes 262176 | tf_op jit(solution)/shard_map/ppermute | solution.py:360
  150.4 1.9 collective-permute-start.10
  153.1 1.1 rev.3
  155.9 2.8 %collective-permute-done.10 = f16[1024,128]{1,0:T(8,128)(2,1)S(1)} collective-permute-done((f16[1024,128]{1,0:T(8,128)(2,1)S(1)}, f16[1024,128]{1,0:T(8,128)(2,1)S(1)}, u32[]{:S(2)}, u32[]{:S(2)}) %collective-permute-start.10) | collective-permute-done | bytes 262176 | tf_op jit(solution)/shard_map/ppermute | solution.py:358
  159.5 7.3 %shard_map.71 = (f32[1024,128]{1,0:T(8,128)}, f32[1024,128]{1,0:T(8,128)}) custom-call(s32[4]{0:T(128)} %copy-done.5, f32[1024,128]{1,0:T(8,128)} %copy-done.2, f32[1024,128]{1,0:T(8,128)} %convert_element_type.74.refs_1_, f32[1024,128]{1,0:T(8,128)} %convert_element_type.76.refs_2_, f32[1024,128]{1,0:T(8,128)} %convert_element_type.78.refs_3_, ...), custom_call_target="tpu_custom_call" | custom-call | tf_op jit(solution)/shard_map/pallas_call | solution.py:279
  166.9 12.8 %shard_map.72 = (bf16[3,256,128]{2,1,0:T(8,128)(2,1)}, bf16[4,288,128]{2,1,0:T(8,128)(2,1)}) custom-call(s32[4]{0:T(128)} %copy-done.5, f32[1024,128]{1,0:T(8,128)} %get-tuple-element.42.refs_0_, f32[1024,128]{1,0:T(8,128)} %get-tuple-element.43.refs_1_, bf16[4,1024,128]{2,1,0:T(8,128)(2,1)} %bitcast.45, bf16[4,1152,128]{2,1,0:T(8,128)(2,1)} %bitcast.33, ...), custom_call_target="tpu_custom_call" | custom-call | tf_op jit(solution)/shard_map/pallas_call | solution.py:279
  181.7 10.9 %all_to_all.11 = bf16[4,480,128]{2,1,0:T(8,128)(2,1)S(1)} all-to-all(bf16[4,480,128]{2,1,0:T(8,128)(2,1)S(1)} %pad_maximum_fusion), channel_id=1, replica_groups={{0,1,2,3},{4,5,6,7},{8,9,10,11},{12,13,14,15},{16,17,18,19},{20,21,22,2..., dimensions={0} | all-to-all | bytes 983040 | tf_op jit(solution)/shard_map/all_to_all | solution.py:408
  (58 shorter events, 17.9 us)
Async XLA Ops:
  7.2 11.0 %copy-start.7 = (f32[4,2,32,128]{3,2,1,0:T(8,128)S(1)}, f32[4,2,32,128]{3,2,1,0:T(8,128)}, u32[]{:S(2)}) copy-start(f32[4,2,32,128]{3,2,1,0:T(8,128)} %param.4) | copy-start | bytes 393220
  7.2 42.3 %all-gather.7.cloned.1.call-start = ((), (), s32[]{:S(2)}) async-start(), calls=%async_computation.2 | async-start | bytes 1474560 | tf_op jit(solution)/shard_map/all_gather | solution.py:323
  9.9 8.3 %collective-permute-start = (f16[4,2,32,128]{3,2,1,0:T(8,128)(2,1)S(1)}, f16[4,2,32,128]{3,2,1,0:T(8,128)(2,1)S(1)}, u32[]{:S(2)}, u32[]{:S(2)}) collective-permute-start(f16[4,2,32,128]{3,2,1,0:T(8,128)(2,1)S(1)} %convert_bitcast_fusion.1), channel_id=1, source_target_pairs={{0,16},{16,32},{32,48},{48,64},{64,80},{80,96},{96,112},{112,128},... | collective-permute-start | bytes 196616 | tf_op jit(solution)/shard_map/ppermute | solution.py:308
  13.3 146.2 %all-gather.9.cloned.1.call-start = ((), (), s32[]{:S(2)}) async-start(), calls=%async_computation.3 | async-start | bytes 2654208 | tf_op jit(solution)/shard_map/all_gather | solution.py:340
  44.7 1.5 copy-start.1
  49.4 15.4 %copy-start = (bf16[4608,128]{1,0:T(8,128)(2,1)S(1)}, bf16[4608,128]{1,0:T(8,128)(2,1)}, u32[]{:S(2)}) copy-start(bf16[4608,128]{1,0:T(8,128)(2,1)} %all-gather.7.cloned.1.call-done) | copy-start | bytes 3538948
  51.3 115.6 %all-gather.11.cloned.1.call-start = ((), (), s32[]{:S(2)}) async-start(), calls=%async_computation.4 | async-start | bytes 1310720 | tf_op jit(solution)/shard_map/all_gather | solution.py:347
  52.1 12.7 %collective-permute-start.1 = (f16[1024,128]{1,0:T(8,128)(2,1)}, f16[1024,128]{1,0:T(8,128)(2,1)S(1)}, u32[]{:S(2)}, u32[]{:S(2)}) collective-permute-start(f16[1024,128]{1,0:T(8,128)(2,1)} %convert_element_type.67), channel_id=1, source_target_pairs={{0,16},{16,32},{32,48},{48,64},{64,80},{80,96},{96,112},{112,128},... | collective-permute-start | bytes 786440 | tf_op jit(solution)/shard_map/ppermute | solution.py:308
  54.1 53.0 %copy-start.5 = (s32[4]{0:T(128)}, s32[4]{0:T(128)S(1)}, u32[]{:S(2)}) copy-start(s32[4]{0:T(128)S(1)} %pad_add_fusion.place) | copy-start | bytes 52
  69.4 0.7 copy-start.4
  70.2 16.2 %collective-permute-start.2 = (f16[2,1024,128]{2,1,0:T(8,128)(2,1)S(1)}, f16[2,1024,128]{2,1,0:T(8,128)(2,1)S(1)}, u32[]{:S(2)}, u32[]{:S(2)}) collective-permute-start(f16[2,1024,128]{2,1,0:T(8,128)(2,1)S(1)} %convert_element_type.69), channel_id=1, source_target_pairs={{0,16},{16,0},{32,48},{48,32},{64,80},{80,64},{96,112},{112,96},{1... | collective-permute-start | bytes 1572872 | tf_op jit(solution)/shard_map/ppermute | solution.py:302
  88.9 17.1 %collective-permute-start.3 = (f16[2,1024,128]{2,1,0:T(8,128)(2,1)}, f16[2,1024,128]{2,1,0:T(8,128)(2,1)}, u32[]{:S(2)}, u32[]{:S(2)}) collective-permute-start(f16[2,1024,128]{2,1,0:T(8,128)(2,1)} %convert_element_type.71), channel_id=1, source_target_pairs={{0,48},{16,32},{32,16},{48,0},{64,112},{80,96},{96,80},{112,64},{1... | collective-permute-start | bytes 1572872 | tf_op jit(solution)/shard_map/ppermute | solution.py:302
  109.6 22.7 %copy-start.2 = (f32[1024,128]{1,0:T(8,128)}, f32[1024,128]{1,0:T(8,128)S(1)}, u32[]{:S(2)}) copy-start(f32[1024,128]{1,0:T(8,128)S(1)} %get-tuple-element.28.refs_0_) | copy-start | bytes 1572868
  109.6 22.7 %copy-start.3 = (f32[1024,128]{1,0:T(8,128)}, f32[1024,128]{1,0:T(8,128)S(1)}, u32[]{:S(2)}) copy-start(f32[1024,128]{1,0:T(8,128)S(1)} %get-tuple-element.41.refs_9_) | copy-start | bytes 1572868
  109.6 13.4 %collective-permute-start.4 = (f16[1024,128]{1,0:T(8,128)(2,1)S(1)}, f16[1024,128]{1,0:T(8,128)(2,1)S(1)}, u32[]{:S(2)}, u32[]{:S(2)}) collective-permute-start(f16[1024,128]{1,0:T(8,128)(2,1)S(1)} %convert_element_type.73), channel_id=1, source_target_pairs={{0,64},{16,80},{32,96},{48,112},{64,128},{80,144},{96,160},{112,17... | collective-permute-start | bytes 786440 | tf_op jit(solution)/shard_map/ppermute | solution.py:358
  117.2 11.4 %collective-permute-start.6 = (f16[1024,128]{1,0:T(8,128)(2,1)S(1)}, f16[1024,128]{1,0:T(8,128)(2,1)S(1)}, u32[]{:S(2)}, u32[]{:S(2)}) collective-permute-start(f16[1024,128]{1,0:T(8,128)(2,1)S(1)} %convert_element_type.73), channel_id=1, source_target_pairs={{64,0},{80,16},{96,32},{112,48},{128,64},{144,80},{160,96},{176,11... | collective-permute-start | bytes 786440 | tf_op jit(solution)/shard_map/ppermute | solution.py:360
  123.0 10.7 %collective-permute-start.5 = (f16[1024,128]{1,0:T(8,128)(2,1)S(1)}, f16[1024,128]{1,0:T(8,128)(2,1)S(1)}, u32[]{:S(2)}, u32[]{:S(2)}) collective-permute-start(f16[1024,128]{1,0:T(8,128)(2,1)S(1)} %collective-permute-done.4), channel_id=1, source_target_pairs={{0,64},{16,80},{32,96},{48,112},{64,128},{80,144},{96,160},{112,17... | collective-permute-start | bytes 786440 | tf_op jit(solution)/shard_map/ppermute | solution.py:358
  128.6 10.4 %collective-permute-start.7 = (f16[1024,128]{1,0:T(8,128)(2,1)S(1)}, f16[1024,128]{1,0:T(8,128)(2,1)S(1)}, u32[]{:S(2)}, u32[]{:S(2)}) collective-permute-start(f16[1024,128]{1,0:T(8,128)(2,1)S(1)} %collective-permute-done.6), channel_id=1, source_target_pairs={{64,0},{80,16},{96,32},{112,48},{128,64},{144,80},{160,96},{176,11... | collective-permute-start | bytes 786440 | tf_op jit(solution)/shard_map/ppermute | solution.py:360
  139.0 8.3 %collective-permute-start.8 = (f16[1024,128]{1,0:T(8,128)(2,1)S(1)}, f16[1024,128]{1,0:T(8,128)(2,1)S(1)}, u32[]{:S(2)}, u32[]{:S(2)}) collective-permute-start(f16[1024,128]{1,0:T(8,128)(2,1)S(1)} %collective-permute-done.5), channel_id=1, source_target_pairs={{0,64},{16,80},{32,96},{48,112},{64,128},{80,144},{96,160},{112,17... | collective-permute-start | bytes 786440 | tf_op jit(solution)/shard_map/ppermute | solution.py:358
  140.9 9.5 %collective-permute-start.9 = (f16[1024,128]{1,0:T(8,128)(2,1)S(1)}, f16[1024,128]{1,0:T(8,128)(2,1)S(1)}, u32[]{:S(2)}, u32[]{:S(2)}) collective-permute-start(f16[1024,128]{1,0:T(8,128)(2,1)S(1)} %collective-permute-done.7), channel_id=1, source_target_pairs={{64,0},{80,16},{96,32},{112,48},{128,64},{144,80},{160,96},{176,11... | collective-permute-start | bytes 786440 | tf_op jit(solution)/shard_map/ppermute | solution.py:360
  150.4 8.3 %collective-permute-start.10 = (f16[1024,128]{1,0:T(8,128)(2,1)S(1)}, f16[1024,128]{1,0:T(8,128)(2,1)S(1)}, u32[]{:S(2)}, u32[]{:S(2)}) collective-permute-start(f16[1024,128]{1,0:T(8,128)(2,1)S(1)} %collective-permute-done.8), channel_id=1, source_target_pairs={{0,64},{16,80},{32,96},{48,112},{64,128},{80,144},{96,160},{112,17... | collective-permute-start | bytes 786440 | tf_op jit(solution)/shard_map/ppermute | solution.py:358
  192.6 1.4 copy-start.6
Sparse Core Ops, SparseCore 0:
  13.4 33.8 all-gather.6
  51.4 41.9 all-gather.8
  95.5 28.9 all-gather.10

commit v4 on v3

--- a/solution.py
+++ b/solution.py
@@ -53,101 +53,6 @@
     return [(chunk, pl.ds(chunk * CHUNK, CHUNK)) for chunk in range(PIXELS // CHUNK)]
 
 
-def relax_kernel(begin, weights, out, state, pad):
-    clear(pad)
-    state[...] = begin[...]
-
-    def step(layer, carry):
-        put_active(pad, state)
-        for chunk, rows in chunks():
-            state[rows, :] += STEP_SIZE * conv(pad, weights.at[layer], chunk)
-        return carry
-
-    lax.fori_loop(0, SECTION, step, 0)
-    out[...] = state[...]
-
-
-def fine_kernel(place, own, received, weights, closing, defect_out, send_out, state, base, first, pad):
-    section, phase = place[0], place[1]
-    clear(pad)
-    for _, rows in chunks():
-        begin = jnp.where(section == 0, own[rows, :], received[rows, :])
-        state[rows, :] = begin
-        base[rows, :] = begin
-
-    put_active(pad, state)
-    for chunk, rows in chunks():
-        term = conv(pad, weights.at[0], chunk)
-        first[rows, :] = term
-        state[rows, :] += STEP_SIZE * term
-
-    @pl.when(phase == 0)
-    def _():
-        for chunk, rows in chunks():
-            long_term = (4 * SECTION * STEP_SIZE) * conv(pad, closing.at[SECTION - 1], chunk)
-            base[rows, :] += long_term
-
-    def step(layer, carry):
-        put_active(pad, state)
-        for chunk, rows in chunks():
-            state[rows, :] += STEP_SIZE * conv(pad, weights.at[layer], chunk)
-        return carry
-
-    lax.fori_loop(1, SECTION, step, 0)
-    for _, rows in chunks():
-        begin = jnp.where(section == 0, own[rows, :], received[rows, :])
-        last = state[rows, :]
-        defect = (last - begin) - SECTION * STEP_SIZE * first[rows, :]
-        defect_out[rows, :] = defect.astype(LOW)
-        send_out[0, rows, :] = jnp.where(phase == 0, last, defect)
-        total = jnp.where(section == 0, begin, last - base[rows, :])
-        send_out[1, rows, :] = jnp.where(phase == 0, total, defect)
-
-
-def first_round_kernel(place, sent, received, leading, out, state, pad):
-    phase, in_first_group = place[1], place[0] < 4
-
-    @pl.when(phase < 2)
-    def _():
-        clear(pad)
-        for _, rows in chunks():
-            state[rows, :] = jnp.where(phase == 0, sent[0, rows, :], received[0, rows, :])
-        put_active(pad, state)
-        for chunk, rows in chunks():
-            defect = jnp.where(phase == 0, received[0, rows, :], sent[0, rows, :])
-            total = jnp.where(phase == 0, sent[1, rows, :], received[1, rows, :])
-            change = SECTION * STEP_SIZE * conv(pad, leading.at[1], chunk) + defect
-            out[0, rows, :] = state[rows, :] + change
-            out[1, rows, :] = total + jnp.where(in_first_group, 0.0, change)
-
-    @pl.when(phase >= 2)
-    def _():
-        for _, rows in chunks():
-            out[0, rows, :] = jnp.where(phase == 2, sent[0, rows, :], received[0, rows, :])
-            out[1, rows, :] = jnp.where(phase == 2, received[0, rows, :], sent[0, rows, :])
-
-
-def closing_kernel(place, sent, received, leading, out, total, state, pad):
-    phase, in_first_group = place[1], place[0] < 4
-    clear(pad)
-    for _, rows in chunks():
-        state[rows, :] = jnp.where(phase < 2, sent[0, rows, :], received[0, rows, :])
-        total[rows, :] = jnp.where(phase < 2, sent[1, rows, :], received[1, rows, :])
-
-    def step(turn, carry):
-        put_active(pad, state)
-        for chunk, rows in chunks():
-            defect = jnp.where(phase < 2, received[turn, rows, :], sent[turn, rows, :])
-            change = SECTION * STEP_SIZE * conv(pad, leading.at[2 + turn], chunk) + defect
-            state[rows, :] += change
-            total[rows, :] += jnp.where(in_first_group, 0.0, change)
-        return carry
-
-    lax.fori_loop(0, 2, step, 0)
-    for _, rows in chunks():
-        out[rows, :] = jnp.where(in_first_group, state[rows, :], total[rows, :])
-
-
 def load(sources, targets, arrived):
     copies = [
         pltpu.make_async_copy(source, target, arrived.at[number])
@@ -158,6 +63,111 @@
     return copies
 
 
+def fine_kernel(
+    place, start, previous_stored, weights_stored, leading_stored,
+    send_out, defect_out, closing_out,
+    state, begin, base, first, pad, previous, weights, closing, defect, arrived,
+):
+    section, phase = place[0], place[1]
+    last_leading = leading_stored.at[SECTION - 1]
+    copies = load(
+        [previous_stored, weights_stored, last_leading, last_leading],
+        [previous, weights, closing, closing_out],
+        arrived,
+    )
+    clear(pad)
+    state[...] = start[...]
+    copies[0].wait()
+
+    def relax(layer, carry):
+        put_active(pad, state)
+        for chunk, rows in chunks():
+            state[rows, :] += STEP_SIZE * conv(pad, previous.at[layer], chunk)
+        return carry
+
+    lax.fori_loop(0, SECTION, relax, 0)
+    for _, rows in chunks():
+        value = jnp.where(section == 0, start[rows, :], state[rows, :])
+        state[rows, :] = value
+        begin[rows, :] = value
+        base[rows, :] = value
+    copies[1].wait()
+    copies[2].wait()
+
+    put_active(pad, state)
+    for chunk, rows in chunks():
+        term = conv(pad, weights.at[0], chunk)
+        first[rows, :] = term
+        state[rows, :] += STEP_SIZE * term
+
+    @pl.when(phase == 0)
+    def _():
+        for chunk, rows in chunks():
+            base[rows, :] += (4 * SECTION * STEP_SIZE) * conv(pad, closing, chunk)
+
+    def step(layer, carry):
+        put_active(pad, state)
+        for chunk, rows in chunks():
+            state[rows, :] += STEP_SIZE * conv(pad, weights.at[layer], chunk)
+        return carry
+
+    lax.fori_loop(1, SECTION, step, 0)
+    for _, rows in chunks():
+        last = state[rows, :]
+        term = (last - begin[rows, :]) - SECTION * STEP_SIZE * first[rows, :]
+        defect[rows, :] = term.astype(LOW)
+        send_out[0, rows, :] = jnp.where(phase == 0, last, term)
+        total = jnp.where(section == 0, begin[rows, :], last - base[rows, :])
+        send_out[1, rows, :] = jnp.where(phase == 0, total, term)
+    copies[3].wait()
+    for copy in load([defect], [defect_out], arrived):
+        copy.wait()
+
+
+def first_round_kernel(place, sent, received, leading, out, state, pad):
+    phase, in_first_group = place[1], place[0] < 4
+
+    @pl.when(phase < 2)
+    def _():
+        clear(pad)
+        for _, rows in chunks():
+            state[rows, :] = jnp.where(phase == 0, sent[0, rows, :], received[0, rows, :])
+        put_active(pad, state)
+        for chunk, rows in chunks():
+            defect = jnp.where(phase == 0, received[0, rows, :], sent[0, rows, :])
+            total = jnp.where(phase == 0, sent[1, rows, :], received[1, rows, :])
+            change = SECTION * STEP_SIZE * conv(pad, leading.at[1], chunk) + defect
+            out[0, rows, :] = state[rows, :] + change
+            out[1, rows, :] = total + jnp.where(in_first_group, 0.0, change)
+
+    @pl.when(phase >= 2)
+    def _():
+        for _, rows in chunks():
+            out[0, rows, :] = jnp.where(phase == 2, sent[0, rows, :], received[0, rows, :])
+            out[1, rows, :] = jnp.where(phase == 2, received[0, rows, :], sent[0, rows, :])
+
+
+def closing_kernel(place, sent, received, leading, out, total, state, pad):
+    phase, in_first_group = place[1], place[0] < 4
+    clear(pad)
+    for _, rows in chunks():
+        state[rows, :] = jnp.where(phase < 2, sent[0, rows, :], received[0, rows, :])
+        total[rows, :] = jnp.where(phase < 2, sent[1, rows, :], received[1, rows, :])
+
+    def step(turn, carry):
+        put_active(pad, state)
+        for chunk, rows in chunks():
+            defect = jnp.where(phase < 2, received[turn, rows, :], sent[turn, rows, :])
+            change = SECTION * STEP_SIZE * conv(pad, leading.at[2 + turn], chunk) + defect
+            state[rows, :] += change
+            total[rows, :] += jnp.where(in_first_group, 0.0, change)
+        return carry
+
+    lax.fori_loop(0, 2, step, 0)
+    for _, rows in chunks():
+        out[rows, :] = jnp.where(in_first_group, state[rows, :], total[rows, :])
+
+
 def chain_kernel(place, *refs):
     stored, outs, (state, begin, pad, slots, coarse, images, arrived) = refs[:10], refs[10:12], refs[12:]
     group = place[2]
@@ -188,7 +198,7 @@
 
 
 def final_kernel(place, *refs):
-    stored, (ends_out, grad_out), refs = refs[:7], refs[7:9], refs[9:]
+    stored, out, refs = refs[:7], refs[7], refs[8:]
     begin, slopes, change, pads, back_pad, grads = refs[:6]
     held, arrived = refs[6:13], refs[13]
     state, end, defects, leading, weights, flipped, end_adjoint = held
@@ -200,6 +210,7 @@
     for copy in copies[:4]:
         copy.wait()
     begin[...] = state[...]
+    grads[3 * CHANNELS :, :] = jnp.zeros((8, CHANNELS), FULL)
 
     def level_step(turn, carry):
         put_active(back_pad, state)
@@ -256,20 +267,23 @@
             grads[pl.ds(part * CHANNELS, CHANNELS), :] = STEP_SIZE * lax.dot_general(
                 columns, low, (((0,), (0,)), ((), ())), preferred_element_type=FULL
             )
-        grad_out[layer] = grads[pl.ds(pl.multiple_of(SIDE * replica, SIDE), 288), :].astype(LOW)
+        for block in range(4):
+            rows = pl.ds(pl.multiple_of(SIDE * replica + 72 * block, 8), 80)
+            out[block, pl.ds(pl.multiple_of(192 + 80 * layer, 16), 80), :] = grads[rows, :].astype(LOW)
         for chunk, rows in chunks():
             change[rows, :] += slopes[layer, rows, :] * conv(back_pad, flipped.at[layer], chunk)
         return carry
 
     lax.fori_loop(0, SECTION, backward, 0)
-    kept = pl.ds(pl.multiple_of(replica * 256, 256), 256)
-    high = end[kept, :].astype(LOW)
-    ends_out[0] = high
-    ends_out[1] = (end[kept, :] - high.astype(FULL)).astype(LOW)
-    ends_out[2] = change[kept, :].astype(LOW)
-
-
-def call(body, outs, scratch, megabytes, place, *operands, stored=(), store=False):
+    for block in range(4):
+        kept = pl.ds(pl.multiple_of(replica * 256 + block * 64, 64), 64)
+        high = end[kept, :].astype(LOW)
+        out[block, 0:64, :] = high
+        out[block, 64:128, :] = (end[kept, :] - high.astype(FULL)).astype(LOW)
+        out[block, 128:192, :] = change[kept, :].astype(LOW)
+
+
+def call(body, outs, scratch, megabytes, place, *operands, stored=(), store=()):
     held = pl.BlockSpec(memory_space=pltpu.VMEM)
     in_specs = [held] * len(operands) + [pl.BlockSpec(memory_space=pltpu.HBM)] * len(stored)
     operands += tuple(stored)
@@ -280,7 +294,10 @@
         body,
         out_shape=outs,
         in_specs=in_specs,
-        out_specs=jax.tree.map(lambda _: pl.BlockSpec(memory_space=pltpu.HBM) if store else held, outs),
+        out_specs=jax.tree.unflatten(
+            jax.tree.structure(outs),
+            [pl.BlockSpec(memory_space=pltpu.HBM) if n in store else held for n in range(len(jax.tree.leaves(outs)))],
+        ),
         scratch_shapes=scratch,
         compiler_params=pltpu.CompilerParams(vmem_limit_bytes=megabytes * 1024 * 1024),
     )(*operands)
@@ -321,7 +338,8 @@
 
     guess, leading = lax.optimization_barrier((end_guess[0].astype(SENT), weights[0]))
     leading = lax.all_gather(leading, "layer", axis_index_groups=rows_of_groups)
-    guess = jnp.where(section == 0, images, shift(guess, 1, sections).astype(FULL))
+    previous = lax.ppermute(weights, "layer", [(i, i + 1) for i in range(sections - 1)])
+    guess = jnp.where(section < 2, images, shift(guess, 2, sections).astype(FULL))
     both = jnp.stack([guess, end_adjoint[0]], axis=1).astype(SENT)
     both = lax.all_to_all(jnp.tile(both, (tiles // 4, 1, 1, 1, 1)), "space", 0, 0, tiled=True)
     both = both.astype(FULL)
@@ -334,16 +352,21 @@
     )
     image_shape, pair_shape = shape(*IMAGE), shape(2, *IMAGE)
 
-    relaxed = call(relax_kernel, image_shape, [wide(), padding()], 8, None, start, weights)
-    closing_weights, _ = lax.optimization_barrier((leading[3], relaxed))
-    received = shift(relaxed, 1, sections)
+    def scratch_like(*arrays):
+        return [pltpu.VMEM(array.shape, array.dtype) for array in arrays]
+
+    low_shape = shape(*IMAGE, dtype=LOW)
+    send, defect, closing_weights = call(
+        fine_kernel,
+        (pair_shape, low_shape, shape(9 * CHANNELS, CHANNELS, dtype=LOW)),
+        [
+            wide(), wide(), wide(), wide(), padding(),
+            *scratch_like(weights, weights, weights[0], low_shape),
+            pltpu.SemaphoreType.DMA((4,)),
+        ],
+        60, place, start, stored=(previous, weights, leading), store=(1, 2),
+    )
     coarse = lax.all_gather(closing_weights, "layer", axis_index_groups=columns_of_groups)
-    defect, send = call(
-        fine_kernel,
-        (shape(*IMAGE, dtype=LOW), pair_shape),
-        [wide(), wide(), wide(), padding()],
-        12, place, start, received, weights, leading,
-    )
     defects = lax.all_gather(defect, "layer", axis_index_groups=rows_of_groups)
     received = swap(send, 1, sections)
     send = call(first_round_kernel, pair_shape, [wide(), padding()], 10, place, send, received, leading)
@@ -367,9 +390,6 @@
     widened[4] = ups[-1].astype(FULL)
     slots = [defect_two] + [widened[distance] for distance in range(1, 8)]
 
-    def scratch_like(*arrays):
-        return [pltpu.VMEM(array.shape, array.dtype) for array in arrays]
-
     before, own = call(
         chain_kernel,
         (image_shape, image_shape),
@@ -379,37 +399,30 @@
             *scratch_like(coarse, base),
             pltpu.SemaphoreType.DMA((10,)),
         ],
-        60, place, stored=(*slots, coarse, base), store=True,
+        60, place, stored=(*slots, coarse, base), store=(0, 1),
     )
     stored = (before, own, defects, leading, weights, flipped, adjoint_whole)
-    ends, grads = call(
+    parts = call(
         final_kernel,
-        (shape(3, 256, CHANNELS, dtype=LOW), shape(SECTION, 288, CHANNELS, dtype=LOW)),
+        shape(4, 512, CHANNELS, dtype=LOW),
         [
             wide(),
             pltpu.VMEM((SECTION, *IMAGE), FULL),
             wide(),
             pltpu.VMEM((SECTION, *PAD_SCRATCH), LOW),
             padding(),
-            pltpu.VMEM((3 * CHANNELS, CHANNELS), FULL),
+            pltpu.VMEM((3 * CHANNELS + 8, CHANNELS), FULL),
             *scratch_like(*stored),
             pltpu.SemaphoreType.DMA((len(stored),)),
         ],
         60, place, stored=stored,
-    )
-    parts = jnp.concatenate(
-        [
-            ends.reshape(3, 4, 64, CHANNELS).transpose(1, 0, 2, 3).reshape(4, 192, CHANNELS),
-            grads.reshape(SECTION, 4, 72, CHANNELS).transpose(1, 0, 2, 3).reshape(4, 288, CHANNELS),
-        ],
-        axis=1,
     )
     row_groups = [[4 * r + n for n in range(4)] for r in range(tiles // 4)]
     parts = lax.all_to_all(parts, "space", 0, 0, axis_index_groups=row_groups, tiled=True).astype(FULL)
     tile_shape = (1, 4, 2, SIDE, CHANNELS)
     section_ends = (parts[:, 0:64] + parts[:, 64:128]).reshape(tile_shape)
     start_adjoint = end_adjoint + parts[:, 128:192].reshape(tile_shape)
-    weight_grad = parts[:, 192:].sum(0).reshape(SECTION, 72, CHANNELS)
+    weight_grad = parts[:, 192:].sum(0).reshape(SECTION, 80, CHANNELS)[:, :72]
     return section_ends, start_adjoint, weight_grad
 
 

time: 202 us -> 211 us (1.045)
  the two profiles are of different devices: /device:TPU:24 before, /device:TPU:62 now
where the time goes in v4:
time: 211 us; the launch traced here: 210 us
  waiting for transfers between devices  86.2 us (41%)
  starting transfers between devices  39.4 us (19%)
  Pallas kernels  39.4 us (19%)
  between operations  14.1 us (7%)
  blocking collectives  12.3 us (6%)
  other arithmetic  11.7 us (6%)
  local copies, waits for them, and re-layouts  7.13 us (3%)
    pallas_call x5, Pallas kernels, call(): pl.pallas_call(body, out_shape=outs, in_specs=in_specs, out_specs=jax.tre...  39.4 us
    ppermute x2, waiting for transfers between devices, swap(): lax.ppermute(block.astype(SENT), 'layer', [(i, i ^ distance) for i in ran...  23.9 us
    ppermute x1, waiting for transfers between devices, local(): lax.ppermute(weights, 'layer', [(i, i + 1) for i in range(sections - 1)])  22.5 us
    all_to_all x1, waiting for transfers between devices, local(): lax.all_to_all(jnp.tile(both, (tiles // 4, 1, 1, 1, 1)), 'space', 0, 0, t...  14 us
    all_to_all x1, blocking collectives, local(): lax.all_to_all(parts, 'space', 0, 0, axis_index_groups=row_groups, tiled=...  12.3 us
    all_to_all x1, starting transfers between devices, local(): lax.all_to_all(jnp.tile(both, (tiles // 4, 1, 1, 1, 1)), 'space', 0, 0, t...  10.4 us
    ppermute x4, waiting for transfers between devices, local(): moved = [lax.ppermute(ups[-1], 'layer', up)]  10.1 us
    ppermute x3, starting transfers between devices, local(): moved.append(lax.ppermute(downs[-1], 'layer', down))  9.81 us
  transfers between devices with their start and end apart: 15, of which 12 were waited for; matrix products, arithmetic and copies ran while one was open for 6% of the time, Pallas kernels for 6%

profile of v4, /device:TPU:62, one launch (start us, length us, event | category | flops | bytes accessed | tf_op | source)
XLA Modules:
  0.0 210.2 jit_solution(15008755341896742862)
XLA Ops:
  7.2 1.7 slice_bitcast_fusion
  9.9 1.3 collective-permute-start
  12.1 5.4 %collective-permute-done = f16[4,2,32,128]{3,2,1,0:T(8,128)(2,1)S(1)} collective-permute-done((f16[4,2,32,128]{3,2,1,0:T(8,128)(2,1)S(1)}, f16[4,2,32,128]{3,2,1,0:T(8,128)(2,1)S(1)}, u32[]{:S(2)}, u32[]{:S(2)}) %collective-permute-start) | collective-permute-done | bytes 65568 | tf_op jit(solution)/shard_map/ppermute | solution.py:325
  18.6 10.4 %all-to-all-start = ((f16[16,2,2,32,128]{4,3,2,1,0:T(8,128)(2,1)}), f16[16,2,2,32,128]{4,3,2,1,0:T(8,128)(2,1)S(1)}, u32[]{:S(2)}, u32[]{:S(2)}) async-start(f16[16,2,2,32,128]{4,3,2,1,0:T(8,128)(2,1)} %bitcast.8), calls=%async_computation | async-start | bytes 1048576 | tf_op jit(solution)/shard_map/all_to_all | solution.py:344
  29.0 1.3 collective-permute-start.1
  31.0 14.0 %all-to-all-done = f16[16,2,2,32,128]{4,3,2,1,0:T(8,128)(2,1)S(1)} async-done(((f16[16,2,2,32,128]{4,3,2,1,0:T(8,128)(2,1)}), f16[16,2,2,32,128]{4,3,2,1,0:T(8,128)(2,1)S(1)}, u32[]{:S(2)}, u32[]{:S(2)}) %all-to-all-start) | async-done | bytes 524320 | tf_op jit(solution)/shard_map/all_to_all | solution.py:344
  45.1 1.1 fusion.1
  46.3 22.5 %collective-permute-done.1.previous_stored = bf16[4,1152,128]{2,1,0:T(8,128)(2,1)S(1)} collective-permute-done((bf16[4,1152,128]{2,1,0:T(8,128)(2,1)S(1)}, bf16[4,1152,128]{2,1,0:T(8,128)(2,1)S(1)}, u32[]{:S(2)}, u32[]{:S(2)}) %collective-permute-start.1) | collective-permute-done | bytes 1179680 | tf_op jit(solution)/shard_map/ppermute | solution.py:341
  68.7 2.2 %all-gather.7.cloned.1.call-done = bf16[4608,128]{1,0:T(8,128)(2,1)} async-done(((bf16[1152,128]{1,0:T(8,128)(2,1)}), bf16[4608,128]{1,0:T(8,128)(2,1)}) %all-gather.7.cloned.1.call-update) | async-done | bytes 1179664 | tf_op jit(solution)/shard_map/all_gather | solution.py:340
  70.9 12.8 %shard_map.67 = (f32[2,1024,128]{2,1,0:T(8,128)}, bf16[1024,128]{1,0:T(8,128)(2,1)}, bf16[1152,128]{1,0:T(8,128)(2,1)}) custom-call(s32[4]{0:T(128)} %pad_add_fusion.place, f32[1024,128]{1,0:T(8,128)} %bitcast.32, bf16[4,1152,128]{2,1,0:T(8,128)(2,1)} %copy-done.7, bf16[4,1152,128]{2,1,0:T(8,128)(2,1)} %refs_4_.1, bf16[4,1152,128]{2,1,0:T(8,128)(2,1)} %bitcast.25), custom_call_target="tpu_custom_call" | custom-call | tf_op jit(solution)/shard_map/pallas_call | solution.py:293
  83.8 1.4 convert_element_type.61
  85.2 3.4 %collective-permute-start.2 = (f16[2,1024,128]{2,1,0:T(8,128)(2,1)S(1)}, f16[2,1024,128]{2,1,0:T(8,128)(2,1)S(1)}, u32[]{:S(2)}, u32[]{:S(2)}) collective-permute-start(f16[2,1024,128]{2,1,0:T(8,128)(2,1)S(1)} %convert_element_type.61), channel_id=1, source_target_pairs={{0,16},{16,0},{32,48},{48,32},{64,80},{80,64},{96,112},{112,96},{1... | collective-permute-start | bytes 1572872 | tf_op jit(solution)/shard_map/ppermute | solution.py:319
  88.6 11.9 %collective-permute-done.2 = f16[2,1024,128]{2,1,0:T(8,128)(2,1)S(1)} collective-permute-done((f16[2,1024,128]{2,1,0:T(8,128)(2,1)S(1)}, f16[2,1024,128]{2,1,0:T(8,128)(2,1)S(1)}, u32[]{:S(2)}, u32[]{:S(2)}) %collective-permute-start.2) | collective-permute-done | bytes 524320 | tf_op jit(solution)/shard_map/ppermute | solution.py:319
  101.4 3.5 %collective-permute-start.3 = (f16[2,1024,128]{2,1,0:T(8,128)(2,1)S(1)}, f16[2,1024,128]{2,1,0:T(8,128)(2,1)S(1)}, u32[]{:S(2)}, u32[]{:S(2)}) collective-permute-start(f16[2,1024,128]{2,1,0:T(8,128)(2,1)S(1)} %convert_element_type.63), channel_id=1, source_target_pairs={{0,48},{16,32},{32,16},{48,0},{64,112},{80,96},{96,80},{112,64},{1... | collective-permute-start | bytes 1572872 | tf_op jit(solution)/shard_map/ppermute | solution.py:319
  104.9 12.0 %collective-permute-done.3 = f16[2,1024,128]{2,1,0:T(8,128)(2,1)S(1)} collective-permute-done((f16[2,1024,128]{2,1,0:T(8,128)(2,1)S(1)}, f16[2,1024,128]{2,1,0:T(8,128)(2,1)S(1)}, u32[]{:S(2)}, u32[]{:S(2)}) %collective-permute-start.3) | collective-permute-done | bytes 524320 | tf_op jit(solution)/shard_map/ppermute | solution.py:319
  117.0 2.4 %shard_map.69 = (f32[1024,128]{1,0:T(8,128)S(1)}, f32[1024,128]{1,0:T(8,128)S(1)}) custom-call(s32[4]{0:T(128)S(1)} %copy-done.4, f32[2,1024,128]{2,1,0:T(8,128)S(1)} %shard_map.68.sent, f32[2,1024,128]{2,1,0:T(8,128)S(1)} %convert_element_type.64.received, bf16[4,1152,128]{2,1,0:T(8,128)(2,1)S(1)} %bitcast.28), custom_call_target="tpu_custom_call" | custom-call | tf_op jit(solution)/shard_map/pallas_call | solution.py:293
  120.2 1.9 collective-permute-start.4
  122.1 3.9 %collective-permute-start.6 = (f16[1024,128]{1,0:T(8,128)(2,1)S(1)}, f16[1024,128]{1,0:T(8,128)(2,1)S(1)}, u32[]{:S(2)}, u32[]{:S(2)}) collective-permute-start(f16[1024,128]{1,0:T(8,128)(2,1)S(1)} %convert_element_type.65), channel_id=1, source_target_pairs={{64,0},{80,16},{96,32},{112,48},{128,64},{144,80},{160,96},{176,11... | collective-permute-start | bytes 786440 | tf_op jit(solution)/shard_map/ppermute | solution.py:383
  126.0 5.1 %collective-permute-done.4 = f16[1024,128]{1,0:T(8,128)(2,1)S(1)} collective-permute-done((f16[1024,128]{1,0:T(8,128)(2,1)S(1)}, f16[1024,128]{1,0:T(8,128)(2,1)S(1)}, u32[]{:S(2)}, u32[]{:S(2)}) %collective-permute-start.4) | collective-permute-done | bytes 262176 | tf_op jit(solution)/shard_map/ppermute | solution.py:381
  131.1 3.9 %collective-permute-start.5 = (f16[1024,128]{1,0:T(8,128)(2,1)S(1)}, f16[1024,128]{1,0:T(8,128)(2,1)S(1)}, u32[]{:S(2)}, u32[]{:S(2)}) collective-permute-start(f16[1024,128]{1,0:T(8,128)(2,1)S(1)} %collective-permute-done.4), channel_id=1, source_target_pairs={{0,64},{16,80},{32,96},{48,112},{64,128},{80,144},{96,160},{112,17... | collective-permute-start | bytes 786440 | tf_op jit(solution)/shard_map/ppermute | solution.py:381
  135.0 2.0 collective-permute-start.7
  138.7 1.5 collective-permute-done.5
  140.2 5.0 %collective-permute-done.7 = f16[1024,128]{1,0:T(8,128)(2,1)S(1)} collective-permute-done((f16[1024,128]{1,0:T(8,128)(2,1)S(1)}, f16[1024,128]{1,0:T(8,128)(2,1)S(1)}, u32[]{:S(2)}, u32[]{:S(2)}) %collective-permute-start.7) | collective-permute-done | bytes 262176 | tf_op jit(solution)/shard_map/ppermute | solution.py:383
  145.1 1.9 collective-permute-start.8
  147.1 3.9 %collective-permute-start.9 = (f16[1024,128]{1,0:T(8,128)(2,1)S(1)}, f16[1024,128]{1,0:T(8,128)(2,1)S(1)}, u32[]{:S(2)}, u32[]{:S(2)}) collective-permute-start(f16[1024,128]{1,0:T(8,128)(2,1)S(1)} %collective-permute-done.7), channel_id=1, source_target_pairs={{64,0},{80,16},{96,32},{112,48},{128,64},{144,80},{160,96},{176,11... | collective-permute-start | bytes 786440 | tf_op jit(solution)/shard_map/ppermute | solution.py:383
  153.4 3.1 %collective-permute-done.9 = f16[1024,128]{1,0:T(8,128)(2,1)S(1)} collective-permute-done((f16[1024,128]{1,0:T(8,128)(2,1)S(1)}, f16[1024,128]{1,0:T(8,128)(2,1)S(1)}, u32[]{:S(2)}, u32[]{:S(2)}) %collective-permute-start.9) | collective-permute-done | bytes 262176 | tf_op jit(solution)/shard_map/ppermute | solution.py:383
  156.5 1.9 collective-permute-start.10
  159.2 1.1 rev.3
  162.0 2.8 %collective-permute-done.10 = f16[1024,128]{1,0:T(8,128)(2,1)S(1)} collective-permute-done((f16[1024,128]{1,0:T(8,128)(2,1)S(1)}, f16[1024,128]{1,0:T(8,128)(2,1)S(1)}, u32[]{:S(2)}, u32[]{:S(2)}) %collective-permute-start.10) | collective-permute-done | bytes 262176 | tf_op jit(solution)/shard_map/ppermute | solution.py:381
  165.6 10.5 %shard_map.70 = (f32[1024,128]{1,0:T(8,128)}, f32[1024,128]{1,0:T(8,128)}) custom-call(s32[4]{0:T(128)} %pad_add_fusion.place, f32[1024,128]{1,0:T(8,128)} %copy-done.2, f32[1024,128]{1,0:T(8,128)} %convert_element_type.66.refs_1_, f32[1024,128]{1,0:T(8,128)} %convert_element_type.68.refs_2_, f32[1024,128]{1,0:T(8,128)} %convert_element_type.70.refs_3_, ...), custom_call_target="tpu_custom_call" | custom-call | tf_op jit(solution)/shard_map/pallas_call | solution.py:293
  176.1 13.1 %shard_map.71 = bf16[4,512,128]{2,1,0:T(8,128)(2,1)} custom-call(s32[4]{0:T(128)} %pad_add_fusion.place, f32[1024,128]{1,0:T(8,128)} %get-tuple-element.40.refs_0_, f32[1024,128]{1,0:T(8,128)} %get-tuple-element.41.refs_1_, bf16[4,1024,128]{2,1,0:T(8,128)(2,1)} %bitcast.34, bf16[4,1152,128]{2,1,0:T(8,128)(2,1)} %bitcast.26, bf16[4,1152,128]{2,1,0:T(8,128)(2,1)} %refs_4_.1, ...), custom_call_target="tpu_custom_call" | custom-call | tf_op jit(solution)/shard_map/pallas_call | solution.py:293
  189.2 12.3 %all_to_all.10 = bf16[4,512,128]{2,1,0:T(8,128)(2,1)S(1)} all-to-all(bf16[4,512,128]{2,1,0:T(8,128)(2,1)} %shard_map.71), channel_id=1, replica_groups={{0,1,2,3},{4,5,6,7},{8,9,10,11},{12,13,14,15},{16,17,18,19},{20,21,22,2..., dimensions={0} | all-to-all | bytes 1048576 | tf_op jit(solution)/shard_map/all_to_all | solution.py:421
  (57 shorter events, 15.1 us)
Async XLA Ops:
  7.2 10.4 %copy-start.9 = (f32[4,2,32,128]{3,2,1,0:T(8,128)S(1)}, f32[4,2,32,128]{3,2,1,0:T(8,128)}, u32[]{:S(2)}) copy-start(f32[4,2,32,128]{3,2,1,0:T(8,128)} %param.4) | copy-start | bytes 393220
  7.2 63.7 %all-gather.7.cloned.1.call-start = ((), (), s32[]{:S(2)}) async-start(), calls=%async_computation.2 | async-start | bytes 1474560 | tf_op jit(solution)/shard_map/all_gather | solution.py:340
  9.9 7.7 %collective-permute-start = (f16[4,2,32,128]{3,2,1,0:T(8,128)(2,1)S(1)}, f16[4,2,32,128]{3,2,1,0:T(8,128)(2,1)S(1)}, u32[]{:S(2)}, u32[]{:S(2)}) collective-permute-start(f16[4,2,32,128]{3,2,1,0:T(8,128)(2,1)S(1)} %convert_bitcast_fusion.1), channel_id=1, source_target_pairs={{0,32},{16,48},{32,64},{48,80},{64,96},{80,112},{96,128},{112,144}... | collective-permute-start | bytes 196616 | tf_op jit(solution)/shard_map/ppermute | solution.py:325
  17.5 11.5 %copy-start.5 = (bf16[4,1152,128]{2,1,0:T(8,128)(2,1)S(1)}, bf16[4,1152,128]{2,1,0:T(8,128)(2,1)}, u32[]{:S(2)}) copy-start(bf16[4,1152,128]{2,1,0:T(8,128)(2,1)} %refs_4_.1) | copy-start | bytes 3538948
  18.6 26.5 %all-to-all-start = ((f16[16,2,2,32,128]{4,3,2,1,0:T(8,128)(2,1)}), f16[16,2,2,32,128]{4,3,2,1,0:T(8,128)(2,1)S(1)}, u32[]{:S(2)}, u32[]{:S(2)}) async-start(f16[16,2,2,32,128]{4,3,2,1,0:T(8,128)(2,1)} %bitcast.8), calls=%async_computation | async-start | bytes 1048576 | tf_op jit(solution)/shard_map/all_to_all | solution.py:344
  29.0 136.6 %all-gather.9.cloned.1.call-start = ((), (), s32[]{:S(2)}) async-start(), calls=%async_computation.3 | async-start | bytes 2654208 | tf_op jit(solution)/shard_map/all_gather | solution.py:369
  29.0 39.7 %collective-permute-start.1 = (bf16[4,1152,128]{2,1,0:T(8,128)(2,1)S(1)}, bf16[4,1152,128]{2,1,0:T(8,128)(2,1)S(1)}, u32[]{:S(2)}, u32[]{:S(2)}) collective-permute-start(bf16[4,1152,128]{2,1,0:T(8,128)(2,1)S(1)} %copy-done.5), channel_id=1, source_target_pairs={{0,16},{16,32},{32,48},{48,64},{64,80},{80,96},{96,112},{112,128},... | collective-permute-start | bytes 3538952 | tf_op jit(solution)/shard_map/ppermute | solution.py:341
  68.7 2.2 %copy-start.7 = (bf16[4,1152,128]{2,1,0:T(8,128)(2,1)}, bf16[4,1152,128]{2,1,0:T(8,128)(2,1)S(1)}, u32[]{:S(2)}) copy-start(bf16[4,1152,128]{2,1,0:T(8,128)(2,1)S(1)} %collective-permute-done.1.previous_stored) | copy-start | bytes 3538948
  83.7 92.3 %all-gather.11.cloned.1.call-start = ((), (), s32[]{:S(2)}) async-start(), calls=%async_computation.4 | async-start | bytes 1310720 | tf_op jit(solution)/shard_map/all_gather | solution.py:370
  83.8 16.8 %copy-start.1 = (f32[2,1024,128]{2,1,0:T(8,128)S(1)}, f32[2,1024,128]{2,1,0:T(8,128)}, u32[]{:S(2)}) copy-start(f32[2,1024,128]{2,1,0:T(8,128)} %get-tuple-element.25.sent) | copy-start | bytes 3145732
  85.2 15.4 %copy-start = (bf16[4608,128]{1,0:T(8,128)(2,1)S(1)}, bf16[4608,128]{1,0:T(8,128)(2,1)}, u32[]{:S(2)}) copy-start(bf16[4608,128]{1,0:T(8,128)(2,1)} %all-gather.7.cloned.1.call-done) | copy-start | bytes 3538948
  85.2 15.4 %copy-start.4 = (s32[4]{0:T(128)S(1)}, s32[4]{0:T(128)}, u32[]{:S(2)}) copy-start(s32[4]{0:T(128)} %pad_add_fusion.place) | copy-start | bytes 52
  85.2 15.3 %collective-permute-start.2 = (f16[2,1024,128]{2,1,0:T(8,128)(2,1)S(1)}, f16[2,1024,128]{2,1,0:T(8,128)(2,1)S(1)}, u32[]{:S(2)}, u32[]{:S(2)}) collective-permute-start(f16[2,1024,128]{2,1,0:T(8,128)(2,1)S(1)} %convert_element_type.61), channel_id=1, source_target_pairs={{0,16},{16,0},{32,48},{48,32},{64,80},{80,64},{96,112},{112,96},{1... | collective-permute-start | bytes 1572872 | tf_op jit(solution)/shard_map/ppermute | solution.py:319
  101.4 15.5 %collective-permute-start.3 = (f16[2,1024,128]{2,1,0:T(8,128)(2,1)S(1)}, f16[2,1024,128]{2,1,0:T(8,128)(2,1)S(1)}, u32[]{:S(2)}, u32[]{:S(2)}) collective-permute-start(f16[2,1024,128]{2,1,0:T(8,128)(2,1)S(1)} %convert_element_type.63), channel_id=1, source_target_pairs={{0,48},{16,32},{32,16},{48,0},{64,112},{80,96},{96,80},{112,64},{1... | collective-permute-start | bytes 1572872 | tf_op jit(solution)/shard_map/ppermute | solution.py:319
  119.3 0.8 copy-start.3
  120.1 18.5 %copy-start.2 = (f32[1024,128]{1,0:T(8,128)}, f32[1024,128]{1,0:T(8,128)S(1)}, u32[]{:S(2)}) copy-start(f32[1024,128]{1,0:T(8,128)S(1)} %get-tuple-element.26.refs_0_) | copy-start | bytes 1572868
  120.2 10.9 %collective-permute-start.4 = (f16[1024,128]{1,0:T(8,128)(2,1)S(1)}, f16[1024,128]{1,0:T(8,128)(2,1)S(1)}, u32[]{:S(2)}, u32[]{:S(2)}) collective-permute-start(f16[1024,128]{1,0:T(8,128)(2,1)S(1)} %convert_element_type.65), channel_id=1, source_target_pairs={{0,64},{16,80},{32,96},{48,112},{64,128},{80,144},{96,160},{112,17... | collective-permute-start | bytes 786440 | tf_op jit(solution)/shard_map/ppermute | solution.py:381
  122.1 12.9 %collective-permute-start.6 = (f16[1024,128]{1,0:T(8,128)(2,1)S(1)}, f16[1024,128]{1,0:T(8,128)(2,1)S(1)}, u32[]{:S(2)}, u32[]{:S(2)}) collective-permute-start(f16[1024,128]{1,0:T(8,128)(2,1)S(1)} %convert_element_type.65), channel_id=1, source_target_pairs={{64,0},{80,16},{96,32},{112,48},{128,64},{144,80},{160,96},{176,11... | collective-permute-start | bytes 786440 | tf_op jit(solution)/shard_map/ppermute | solution.py:383
  131.1 9.1 %collective-permute-start.5 = (f16[1024,128]{1,0:T(8,128)(2,1)S(1)}, f16[1024,128]{1,0:T(8,128)(2,1)S(1)}, u32[]{:S(2)}, u32[]{:S(2)}) collective-permute-start(f16[1024,128]{1,0:T(8,128)(2,1)S(1)} %collective-permute-done.4), channel_id=1, source_target_pairs={{0,64},{16,80},{32,96},{48,112},{64,128},{80,144},{96,160},{112,17... | collective-permute-start | bytes 786440 | tf_op jit(solution)/shard_map/ppermute | solution.py:381
  135.0 10.1 %collective-permute-start.7 = (f16[1024,128]{1,0:T(8,128)(2,1)S(1)}, f16[1024,128]{1,0:T(8,128)(2,1)S(1)}, u32[]{:S(2)}, u32[]{:S(2)}) collective-permute-start(f16[1024,128]{1,0:T(8,128)(2,1)S(1)} %collective-permute-done.6), channel_id=1, source_target_pairs={{64,0},{80,16},{96,32},{112,48},{128,64},{144,80},{160,96},{176,11... | collective-permute-start | bytes 786440 | tf_op jit(solution)/shard_map/ppermute | solution.py:383
  137.9 20.6 %copy-start.6 = (bf16[4,1152,128]{2,1,0:T(8,128)(2,1)S(1)}, bf16[4,1152,128]{2,1,0:T(8,128)(2,1)}, u32[]{:S(2)}) copy-start(bf16[4,1152,128]{2,1,0:T(8,128)(2,1)} %refs_4_.1) | copy-start | bytes 3538948
  145.1 8.3 %collective-permute-start.8 = (f16[1024,128]{1,0:T(8,128)(2,1)S(1)}, f16[1024,128]{1,0:T(8,128)(2,1)S(1)}, u32[]{:S(2)}, u32[]{:S(2)}) collective-permute-start(f16[1024,128]{1,0:T(8,128)(2,1)S(1)} %collective-permute-done.5), channel_id=1, source_target_pairs={{0,64},{16,80},{32,96},{48,112},{64,128},{80,144},{96,160},{112,17... | collective-permute-start | bytes 786440 | tf_op jit(solution)/shard_map/ppermute | solution.py:381
  147.1 9.5 %collective-permute-start.9 = (f16[1024,128]{1,0:T(8,128)(2,1)S(1)}, f16[1024,128]{1,0:T(8,128)(2,1)S(1)}, u32[]{:S(2)}, u32[]{:S(2)}) collective-permute-start(f16[1024,128]{1,0:T(8,128)(2,1)S(1)} %collective-permute-done.7), channel_id=1, source_target_pairs={{64,0},{80,16},{96,32},{112,48},{128,64},{144,80},{160,96},{176,11... | collective-permute-start | bytes 786440 | tf_op jit(solution)/shard_map/ppermute | solution.py:383
  156.5 8.3 %collective-permute-start.10 = (f16[1024,128]{1,0:T(8,128)(2,1)S(1)}, f16[1024,128]{1,0:T(8,128)(2,1)S(1)}, u32[]{:S(2)}, u32[]{:S(2)}) collective-permute-start(f16[1024,128]{1,0:T(8,128)(2,1)S(1)} %collective-permute-done.8), channel_id=1, source_target_pairs={{0,64},{16,80},{32,96},{48,112},{64,128},{80,144},{96,160},{112,17... | collective-permute-start | bytes 786440 | tf_op jit(solution)/shard_map/ppermute | solution.py:381
  201.5 1.4 copy-start.8
Sparse Core Ops, SparseCore 0:
  11.3 59.5 all-gather.6
  83.9 46.8 all-gather.8
  132.8 28.1 all-gather.10

commit v5 on v2

--- a/solution.py
+++ b/solution.py
@@ -67,12 +67,9 @@
     out[...] = state[...]
 
 
-def fine_kernel(
-    place, own, received, weights, closing, defect_out, send_out, closing_out, state, base, first, pad
-):
+def fine_kernel(place, own, received, weights, closing, defect_out, send_out, state, base, first, pad):
     section, phase = place[0], place[1]
     clear(pad)
-    closing_out[...] = closing[SECTION - 1]
     for _, rows in chunks():
         begin = jnp.where(section == 0, own[rows, :], received[rows, :])
         state[rows, :] = begin
@@ -151,22 +148,27 @@
         out[rows, :] = jnp.where(in_first_group, state[rows, :], total[rows, :])
 
 
+def load(sources, targets, arrived):
+    copies = [
+        pltpu.make_async_copy(source, target, arrived.at[number])
+        for number, (source, target) in enumerate(zip(sources, targets))
+    ]
+    for copy in copies:
+        copy.start()
+    return copies
+
+
 def final_kernel(place, *refs):
-    stored, (ends_out, grad_out), refs = refs[:15], refs[15:17], refs[17:]
+    stored, out, refs = refs[:15], refs[15], refs[16:]
     state, begin, end, slopes, change, pads, back_pad, grads, slots = refs[:9]
     held, arrived = refs[9:16], refs[16]
     coarse, images, defects, leading, weights, flipped, end_adjoint = held
     phase, group, replica = place[1], place[2], place[3]
-    targets = [slots.at[number] for number in range(8)] + list(held)
-    copies = [
-        pltpu.make_async_copy(source, target, arrived.at[number])
-        for number, (source, target) in enumerate(zip(stored, targets))
-    ]
-    for copy in copies:
-        copy.start()
+    copies = load(stored, [slots.at[number] for number in range(8)] + list(held), arrived)
     clear(back_pad)
     for layer in range(SECTION):
         clear(pads.at[layer])
+    grads[3 * CHANNELS :, :] = jnp.zeros((8, CHANNELS), FULL)
 
     for copy in copies[:10]:
         copy.wait()
@@ -191,7 +193,7 @@
     for _, rows in chunks():
         end[rows, :] = state[rows, :]
         state[rows, :] = begin[rows, :]
-    for copy in copies[10:]:
+    for copy in copies[10:12]:
         copy.wait()
 
     def level_step(turn, carry):
@@ -213,6 +215,8 @@
         return carry
 
     lax.fori_loop(0, 3, level_step, 0)
+    for copy in copies[12:]:
+        copy.wait()
 
     def active(layer):
         for piece in range(PIXELS // PIECE):
@@ -247,17 +251,20 @@
             grads[pl.ds(part * CHANNELS, CHANNELS), :] = STEP_SIZE * lax.dot_general(
                 columns, low, (((0,), (0,)), ((), ())), preferred_element_type=FULL
             )
-        grad_out[layer] = grads[pl.ds(pl.multiple_of(SIDE * replica, SIDE), 288), :].astype(LOW)
+        for block in range(4):
+            rows = pl.ds(pl.multiple_of(SIDE * replica + 72 * block, 8), 80)
+            out[block, pl.ds(pl.multiple_of(192 + 80 * layer, 16), 80), :] = grads[rows, :].astype(LOW)
         for chunk, rows in chunks():
             change[rows, :] += slopes[layer, rows, :] * conv(back_pad, flipped.at[layer], chunk)
         return carry
 
     lax.fori_loop(0, SECTION, backward, 0)
-    kept = pl.ds(pl.multiple_of(replica * 256, 256), 256)
-    high = end[kept, :].astype(LOW)
-    ends_out[0] = high
-    ends_out[1] = (end[kept, :] - high.astype(FULL)).astype(LOW)
-    ends_out[2] = change[kept, :].astype(LOW)
+    for block in range(4):
+        kept = pl.ds(pl.multiple_of(replica * 256 + block * 64, 64), 64)
+        high = end[kept, :].astype(LOW)
+        out[block, 0:64, :] = high
+        out[block, 64:128, :] = (end[kept, :] - high.astype(FULL)).astype(LOW)
+        out[block, 128:192, :] = change[kept, :].astype(LOW)
 
 
 def call(body, outs, scratch, megabytes, place, *operands, stored=()):
@@ -310,13 +317,14 @@
     rows_of_groups = [[4 * g + i for i in range(4)] for g in range(sections // 4)]
     columns_of_groups = [[4 * g + i for g in range(sections // 4)] for i in range(4)]
 
-    guess = jnp.where(section == 0, images, shift(end_guess[0], 1, sections))
+    guess, leading = lax.optimization_barrier((end_guess[0].astype(SENT), weights[0]))
+    leading = lax.all_gather(leading, "layer", axis_index_groups=rows_of_groups)
+    guess = jnp.where(section == 0, images, shift(guess, 1, sections).astype(FULL))
     both = jnp.stack([guess, end_adjoint[0]], axis=1).astype(SENT)
     both = lax.all_to_all(jnp.tile(both, (tiles // 4, 1, 1, 1, 1)), "space", 0, 0, tiled=True)
     both = both.astype(FULL)
     start, adjoint_whole = both[:, 0].reshape(IMAGE), both[:, 1].reshape(IMAGE)
 
-    leading = lax.all_gather(weights[0], "layer", axis_index_groups=rows_of_groups)
     flipped = (
         weights.reshape(SECTION, 9, CHANNELS, CHANNELS)[:, ::-1]
         .transpose(0, 1, 3, 2)
@@ -325,14 +333,15 @@
     image_shape, pair_shape = shape(*IMAGE), shape(2, *IMAGE)
 
     relaxed = call(relax_kernel, image_shape, [wide(), padding()], 8, None, start, weights)
+    closing_weights, _ = lax.optimization_barrier((leading[3], relaxed))
     received = shift(relaxed, 1, sections)
-    defect, send, closing_weights = call(
+    coarse = lax.all_gather(closing_weights, "layer", axis_index_groups=columns_of_groups)
+    defect, send = call(
         fine_kernel,
-        (shape(*IMAGE, dtype=LOW), pair_shape, shape(9 * CHANNELS, CHANNELS, dtype=LOW)),
+        (shape(*IMAGE, dtype=LOW), pair_shape),
         [wide(), wide(), wide(), padding()],
         12, place, start, received, weights, leading,
     )
-    coarse = lax.all_gather(closing_weights, "layer", axis_index_groups=columns_of_groups)
     defects = lax.all_gather(defect, "layer", axis_index_groups=rows_of_groups)
     received = swap(send, 1, sections)
     send = call(first_round_kernel, pair_shape, [wide(), padding()], 10, place, send, received, leading)
@@ -342,43 +351,42 @@
     )
     up = [(i, (i + 4) % sections) for i in range(sections)]
     down = [(j, i) for i, j in up]
-    ups, downs = [defect_two.astype(SENT)], [defect_two.astype(SENT)]
+    ups, downs, widened = [defect_two.astype(SENT)], [defect_two.astype(SENT)], {}
     for turn in range(4):
-        ups.append(lax.ppermute(ups[-1], "layer", up))
+        moved = [lax.ppermute(ups[-1], "layer", up)]
         if turn < 3:
-            downs.append(lax.ppermute(downs[-1], "layer", down))
-    slots = [defect_two] + [block.astype(FULL) for block in ups[1:] + downs[:0:-1]]
-
+            moved.append(lax.ppermute(downs[-1], "layer", down))
+        if turn:
+            ready = [ups[-1].astype(FULL), downs[-1].astype(FULL)]
+            moved, (widened[turn], widened[8 - turn]) = lax.optimization_barrier((moved, ready))
+        ups.append(moved[0])
+        if turn < 3:
+            downs.append(moved[1])
+    widened[4], coarse = lax.optimization_barrier((ups[-1], coarse))
+    slots = [defect_two] + [widened[distance].astype(FULL) for distance in range(1, 8)]
     stored = (coarse, base, defects, leading, weights, flipped, adjoint_whole)
-    ends, grads = call(
+    parts = call(
         final_kernel,
-        (shape(3, 256, CHANNELS, dtype=LOW), shape(SECTION, 288, CHANNELS, dtype=LOW)),
+        shape(4, 512, CHANNELS, dtype=LOW),
         [
             wide(), wide(), wide(),
             pltpu.VMEM((SECTION, *IMAGE), FULL),
             wide(),
             pltpu.VMEM((SECTION, *PAD_SCRATCH), LOW),
             padding(),
-            pltpu.VMEM((3 * CHANNELS, CHANNELS), FULL),
+            pltpu.VMEM((3 * CHANNELS + 8, CHANNELS), FULL),
             pltpu.VMEM((8, *IMAGE), FULL),
             *[pltpu.VMEM(array.shape, array.dtype) for array in stored],
             pltpu.SemaphoreType.DMA((8 + len(stored),)),
         ],
         60, place, stored=(*slots, *stored),
     )
-    parts = jnp.concatenate(
-        [
-            ends.reshape(3, 4, 64, CHANNELS).transpose(1, 0, 2, 3).reshape(4, 192, CHANNELS),
-            grads.reshape(SECTION, 4, 72, CHANNELS).transpose(1, 0, 2, 3).reshape(4, 288, CHANNELS),
-        ],
-        axis=1,
-    )
     row_groups = [[4 * r + n for n in range(4)] for r in range(tiles // 4)]
     parts = lax.all_to_all(parts, "space", 0, 0, axis_index_groups=row_groups, tiled=True).astype(FULL)
     tile_shape = (1, 4, 2, SIDE, CHANNELS)
     section_ends = (parts[:, 0:64] + parts[:, 64:128]).reshape(tile_shape)
     start_adjoint = end_adjoint + parts[:, 128:192].reshape(tile_shape)
-    weight_grad = parts[:, 192:].sum(0).reshape(SECTION, 72, CHANNELS)
+    weight_grad = parts[:, 192:].sum(0).reshape(SECTION, 80, CHANNELS)[:, :72]
     return section_ends, start_adjoint, weight_grad
 
 

time: 211 us -> 200 us (0.948)
  waiting for transfers between devices: 65 us -> 58.9 us
    ppermute x7, waiting for transfers between devices: 20.3 us -> 16.1 us  [the longest x3 11.9 us: local(): moved.append(lax.ppermute(downs[-1], 'layer', down))]
    ppermute x7, starting transfers between devices: 30.7 us -> 27.4 us  [the longest x4 21.5 us: local(): moved = [lax.ppermute(ups[-1], 'layer', up)]]
    ppermute x2, waiting for transfers between devices: 31.4 us -> 28.2 us  [swap(): lax.ppermute(block.astype(SENT), 'layer', [(i, i ^ distance) for i in ran...]
    convert_element_type x8 -> x9, other arithmetic: 9.79 us -> 6.97 us  [the longest x6 5.15 us: local(): ready = [ups[-1].astype(FULL), downs[-1].astype(FULL)]]
    unnamed x24 -> x16, local copies, waits for them, and re-layouts: 4.05 us -> 1.36 us
  transfers between devices with their start and end apart: 14 -> 14, of which waited for: 9 -> 10; matrix products, arithmetic and copies ran while one was open for 8% -> 7% of each run, Pallas kernels for 3% -> 6%
where the time goes in v5:
time: 200 us; the launch traced here: 199 us
  waiting for transfers between devices  58.9 us (29%)
  blocking collectives  38.5 us (19%)
  starting transfers between devices  38.2 us (19%)
  Pallas kernels  28.7 us (14%)
  between operations  14.1 us (7%)
  other arithmetic  12.5 us (6%)
  local copies, waits for them, and re-layouts  8.44 us (4%)
    pallas_call x5, Pallas kernels, call(): pl.pallas_call(body, out_shape=outs, in_specs=in_specs, out_specs=jax.tre...  28.7 us
    ppermute x2, waiting for transfers between devices, swap(): lax.ppermute(block.astype(SENT), 'layer', [(i, i ^ distance) for i in ran...  28.2 us
    all_to_all x1, blocking collectives, local(): lax.all_to_all(jnp.tile(both, (tiles // 4, 1, 1, 1, 1)), 'space', 0, 0, t...  26.2 us
    ppermute x4, starting transfers between devices, local(): moved = [lax.ppermute(ups[-1], 'layer', up)]  21.5 us
    ppermute x2, waiting for transfers between devices, shift(): return lax.ppermute(block.astype(SENT), 'layer', route).astype(block.dtype)  14.6 us
    all_to_all x1, blocking collectives, local(): lax.all_to_all(parts, 'space', 0, 0, axis_index_groups=row_groups, tiled=...  12.3 us
    ppermute x3, waiting for transfers between devices, local(): moved.append(lax.ppermute(downs[-1], 'layer', down))  11.9 us
    ppermute x3, starting transfers between devices, local(): moved.append(lax.ppermute(downs[-1], 'layer', down))  5.92 us
  transfers between devices with their start and end apart: 14, of which 10 were waited for; matrix products, arithmetic and copies ran while one was open for 7% of the time, Pallas kernels for 6%

profile of v5, /device:TPU:24, one launch (start us, length us, event | category | flops | bytes accessed | tf_op | source)
XLA Modules:
  0.0 199.4 jit_solution(7484644653384571779)
XLA Ops:
  7.2 0.9 convert_bitcast_fusion.1
  8.2 1.7 slice_bitcast_fusion
  9.9 3.4 %collective-permute-start = (f16[4,2,32,128]{3,2,1,0:T(8,128)(2,1)S(1)}, f16[4,2,32,128]{3,2,1,0:T(8,128)(2,1)S(1)}, u32[]{:S(2)}, u32[]{:S(2)}) collective-permute-start(f16[4,2,32,128]{3,2,1,0:T(8,128)(2,1)S(1)} %convert_bitcast_fusion.1), channel_id=1, source_target_pairs={{0,16},{16,32},{32,48},{48,64},{64,80},{80,96},{96,112},{112,128},... | collective-permute-start | bytes 196616 | tf_op jit(solution)/shard_map/ppermute | solution.py:306
  14.3 3.9 %collective-permute-done = f16[4,2,32,128]{3,2,1,0:T(8,128)(2,1)S(1)} collective-permute-done((f16[4,2,32,128]{3,2,1,0:T(8,128)(2,1)S(1)}, f16[4,2,32,128]{3,2,1,0:T(8,128)(2,1)S(1)}, u32[]{:S(2)}, u32[]{:S(2)}) %collective-permute-start) | collective-permute-done | bytes 65568 | tf_op jit(solution)/shard_map/ppermute | solution.py:306
  18.4 26.2 %all_to_all.10 = f16[16,2,2,32,128]{4,3,2,1,0:T(8,128)(2,1)S(1)} all-to-all(f16[16,2,2,32,128]{4,3,2,1,0:T(8,128)(2,1)S(1)} %bitcast.34), channel_id=1, replica_groups=mesh['layer'=32,'space'=16] {'space'}, dimensions={0} | all-to-all | bytes 1048576 | tf_op jit(solution)/shard_map/all_to_all | solution.py:324
  46.3 3.2 %shard_map.67 = f32[1024,128]{1,0:T(8,128)S(1)} custom-call(f32[1024,128]{1,0:T(8,128)S(1)} %bitcast.30, bf16[4,1152,128]{2,1,0:T(8,128)(2,1)S(1)} %copy-done.1), custom_call_target="tpu_custom_call" | custom-call | tf_op jit(solution)/shard_map/pallas_call | solution.py:277
  49.5 1.8 slice.38
  52.1 1.9 collective-permute-start.1
  54.2 10.7 %collective-permute-done.1 = f16[1024,128]{1,0:T(8,128)(2,1)S(1)} collective-permute-done((f16[1024,128]{1,0:T(8,128)(2,1)}, f16[1024,128]{1,0:T(8,128)(2,1)S(1)}, u32[]{:S(2)}, u32[]{:S(2)}) %collective-permute-start.1) | collective-permute-done | bytes 262176 | tf_op jit(solution)/shard_map/ppermute | solution.py:306
  64.9 4.6 %shard_map.68 = (bf16[1024,128]{1,0:T(8,128)(2,1)S(1)}, f32[2,1024,128]{2,1,0:T(8,128)S(1)}) custom-call(s32[4]{0:T(128)S(1)} %pad_add_fusion.place, f32[1024,128]{1,0:T(8,128)S(1)} %bitcast.31, f32[1024,128]{1,0:T(8,128)S(1)} %convert_element_type.68.received, bf16[4,1152,128]{2,1,0:T(8,128)(2,1)S(1)} %copy-done.1, bf16[4,1152,128]{2,1,0:T(8,128)(2,1)S(1)} %bitcast.26), custom_call_target="tpu_custom_call" | custom-call | tf_op jit(solution)/shard_map/pallas_call | solution.py:277
  70.3 1.9 collective-permute-start.2
  72.2 14.3 %collective-permute-done.2 = f16[2,1024,128]{2,1,0:T(8,128)(2,1)S(1)} collective-permute-done((f16[2,1024,128]{2,1,0:T(8,128)(2,1)S(1)}, f16[2,1024,128]{2,1,0:T(8,128)(2,1)S(1)}, u32[]{:S(2)}, u32[]{:S(2)}) %collective-permute-start.2) | collective-permute-done | bytes 524320 | tf_op jit(solution)/shard_map/ppermute | solution.py:300
  86.6 1.5 shard_map.69.sent
  89.0 3.5 %collective-permute-start.3 = (f16[2,1024,128]{2,1,0:T(8,128)(2,1)}, f16[2,1024,128]{2,1,0:T(8,128)(2,1)}, u32[]{:S(2)}, u32[]{:S(2)}) collective-permute-start(f16[2,1024,128]{2,1,0:T(8,128)(2,1)} %convert_element_type.71), channel_id=1, source_target_pairs={{0,48},{16,32},{32,16},{48,0},{64,112},{80,96},{96,80},{112,64},{1... | collective-permute-start | bytes 1572872 | tf_op jit(solution)/shard_map/ppermute | solution.py:300
  92.5 13.8 %collective-permute-done.3 = f16[2,1024,128]{2,1,0:T(8,128)(2,1)} collective-permute-done((f16[2,1024,128]{2,1,0:T(8,128)(2,1)}, f16[2,1024,128]{2,1,0:T(8,128)(2,1)}, u32[]{:S(2)}, u32[]{:S(2)}) %collective-permute-start.3) | collective-permute-done | bytes 524320 | tf_op jit(solution)/shard_map/ppermute | solution.py:300
  106.3 1.1 convert_element_type.72.received
  107.5 2.4 %shard_map.70 = (f32[1024,128]{1,0:T(8,128)S(1)}, f32[1024,128]{1,0:T(8,128)S(1)}) custom-call(s32[4]{0:T(128)S(1)} %pad_add_fusion.place, f32[2,1024,128]{2,1,0:T(8,128)S(1)} %shard_map.69.sent, f32[2,1024,128]{2,1,0:T(8,128)S(1)} %convert_element_type.72.received, bf16[4,1152,128]{2,1,0:T(8,128)(2,1)S(1)} %bitcast.28), custom_call_target="tpu_custom_call" | custom-call | tf_op jit(solution)/shard_map/pallas_call | solution.py:277
  110.0 2.1 %collective-permute-start.6 = (f16[1024,128]{1,0:T(8,128)(2,1)S(1)}, f16[1024,128]{1,0:T(8,128)(2,1)S(1)}, u32[]{:S(2)}, u32[]{:S(2)}) collective-permute-start(f16[1024,128]{1,0:T(8,128)(2,1)S(1)} %convert_element_type.73), channel_id=1, source_target_pairs={{64,0},{80,16},{96,32},{112,48},{128,64},{144,80},{160,96},{176,11... | collective-permute-start | bytes 786440 | tf_op jit(solution)/shard_map/ppermute | solution.py:358
  112.1 8.9 %collective-permute-start.4 = (f16[1024,128]{1,0:T(8,128)(2,1)S(1)}, f16[1024,128]{1,0:T(8,128)(2,1)S(1)}, u32[]{:S(2)}, u32[]{:S(2)}) collective-permute-start(f16[1024,128]{1,0:T(8,128)(2,1)S(1)} %convert_element_type.73), channel_id=1, source_target_pairs={{0,64},{16,80},{32,96},{48,112},{64,128},{80,144},{96,160},{112,17... | collective-permute-start | bytes 786440 | tf_op jit(solution)/shard_map/ppermute | solution.py:356
  121.0 4.4 %collective-permute-done.6 = f16[1024,128]{1,0:T(8,128)(2,1)S(1)} collective-permute-done((f16[1024,128]{1,0:T(8,128)(2,1)S(1)}, f16[1024,128]{1,0:T(8,128)(2,1)S(1)}, u32[]{:S(2)}, u32[]{:S(2)}) %collective-permute-start.6) | collective-permute-done | bytes 262176 | tf_op jit(solution)/shard_map/ppermute | solution.py:358
  125.4 1.9 collective-permute-start.7
  127.3 5.1 %collective-permute-start.5 = (f16[1024,128]{1,0:T(8,128)(2,1)S(1)}, f16[1024,128]{1,0:T(8,128)(2,1)S(1)}, u32[]{:S(2)}, u32[]{:S(2)}) collective-permute-start(f16[1024,128]{1,0:T(8,128)(2,1)S(1)} %collective-permute-done.4), channel_id=1, source_target_pairs={{0,64},{16,80},{32,96},{48,112},{64,128},{80,144},{96,160},{112,17... | collective-permute-start | bytes 786440 | tf_op jit(solution)/shard_map/ppermute | solution.py:356
  134.1 1.9 collective-permute-done.7
  136.0 1.2 collective-permute-done.5
  137.2 5.6 %collective-permute-start.8 = (f16[1024,128]{1,0:T(8,128)(2,1)S(1)}, f16[1024,128]{1,0:T(8,128)(2,1)S(1)}, u32[]{:S(2)}, u32[]{:S(2)}) collective-permute-start(f16[1024,128]{1,0:T(8,128)(2,1)S(1)} %collective-permute-done.5), channel_id=1, source_target_pairs={{0,64},{16,80},{32,96},{48,112},{64,128},{80,144},{96,160},{112,17... | collective-permute-start | bytes 786440 | tf_op jit(solution)/shard_map/ppermute | solution.py:356
  142.8 1.9 collective-permute-start.9
  146.7 5.6 %collective-permute-done.9 = f16[1024,128]{1,0:T(8,128)(2,1)S(1)} collective-permute-done((f16[1024,128]{1,0:T(8,128)(2,1)S(1)}, f16[1024,128]{1,0:T(8,128)(2,1)S(1)}, u32[]{:S(2)}, u32[]{:S(2)}) %collective-permute-start.9) | collective-permute-done | bytes 262176 | tf_op jit(solution)/shard_map/ppermute | solution.py:358
  152.3 1.9 collective-permute-start.10
  155.0 1.1 rev.3
  157.9 2.7 %collective-permute-done.10 = f16[1024,128]{1,0:T(8,128)(2,1)S(1)} collective-permute-done((f16[1024,128]{1,0:T(8,128)(2,1)S(1)}, f16[1024,128]{1,0:T(8,128)(2,1)S(1)}, u32[]{:S(2)}, u32[]{:S(2)}) %collective-permute-start.10) | collective-permute-done | bytes 262176 | tf_op jit(solution)/shard_map/ppermute | solution.py:356
  161.4 16.9 %shard_map.71 = bf16[4,512,128]{2,1,0:T(8,128)(2,1)} custom-call(s32[4]{0:T(128)} %copy-done.5, f32[1024,128]{1,0:T(8,128)} %copy-done.2, f32[1024,128]{1,0:T(8,128)} %convert_element_type.74.refs_1_, f32[1024,128]{1,0:T(8,128)} %convert_element_type.76.refs_2_, f32[1024,128]{1,0:T(8,128)} %convert_element_type.78.refs_3_, ...), custom_call_target="tpu_custom_call" | custom-call | tf_op jit(solution)/shard_map/pallas_call | solution.py:277
  178.3 12.3 %all_to_all.11 = bf16[4,512,128]{2,1,0:T(8,128)(2,1)S(1)} all-to-all(bf16[4,512,128]{2,1,0:T(8,128)(2,1)} %shard_map.71), channel_id=1, replica_groups={{0,1,2,3},{4,5,6,7},{8,9,10,11},{12,13,14,15},{16,17,18,19},{20,21,22,2..., dimensions={0} | all-to-all | bytes 1048576 | tf_op jit(solution)/shard_map/all_to_all | solution.py:385
  (55 shorter events, 14.7 us)
Async XLA Ops:
  7.2 11.0 %copy-start.7 = (f32[4,2,32,128]{3,2,1,0:T(8,128)S(1)}, f32[4,2,32,128]{3,2,1,0:T(8,128)}, u32[]{:S(2)}) copy-start(f32[4,2,32,128]{3,2,1,0:T(8,128)} %param.4) | copy-start | bytes 393220
  7.2 42.3 %all-gather.7.cloned.1.call-start = ((), (), s32[]{:S(2)}) async-start(), calls=%async_computation.2 | async-start | bytes 1474560 | tf_op jit(solution)/shard_map/all_gather | solution.py:321
  9.9 150.7 %all-gather.9.cloned.1.call-start = ((), (), s32[]{:S(2)}) async-start(), calls=%async_computation.3 | async-start | bytes 2654208 | tf_op jit(solution)/shard_map/all_gather | solution.py:338
  9.9 8.3 %collective-permute-start = (f16[4,2,32,128]{3,2,1,0:T(8,128)(2,1)S(1)}, f16[4,2,32,128]{3,2,1,0:T(8,128)(2,1)S(1)}, u32[]{:S(2)}, u32[]{:S(2)}) collective-permute-start(f16[4,2,32,128]{3,2,1,0:T(8,128)(2,1)S(1)} %convert_bitcast_fusion.1), channel_id=1, source_target_pairs={{0,16},{16,32},{32,48},{48,64},{64,80},{80,96},{96,112},{112,128},... | collective-permute-start | bytes 196616 | tf_op jit(solution)/shard_map/ppermute | solution.py:306
  44.8 1.5 copy-start.1
  49.5 15.4 %copy-start = (bf16[4608,128]{1,0:T(8,128)(2,1)S(1)}, bf16[4608,128]{1,0:T(8,128)(2,1)}, u32[]{:S(2)}) copy-start(bf16[4608,128]{1,0:T(8,128)(2,1)} %all-gather.7.cloned.1.call-done) | copy-start | bytes 3538948
  51.4 110.0 %all-gather.11.cloned.1.call-start = ((), (), s32[]{:S(2)}) async-start(), calls=%async_computation.4 | async-start | bytes 1310720 | tf_op jit(solution)/shard_map/all_gather | solution.py:345
  52.1 12.7 %collective-permute-start.1 = (f16[1024,128]{1,0:T(8,128)(2,1)}, f16[1024,128]{1,0:T(8,128)(2,1)S(1)}, u32[]{:S(2)}, u32[]{:S(2)}) collective-permute-start(f16[1024,128]{1,0:T(8,128)(2,1)} %convert_element_type.67), channel_id=1, source_target_pairs={{0,16},{16,32},{32,48},{48,64},{64,80},{80,96},{96,112},{112,128},... | collective-permute-start | bytes 786440 | tf_op jit(solution)/shard_map/ppermute | solution.py:306
  54.2 53.3 %copy-start.5 = (s32[4]{0:T(128)}, s32[4]{0:T(128)S(1)}, u32[]{:S(2)}) copy-start(s32[4]{0:T(128)S(1)} %pad_add_fusion.place) | copy-start | bytes 52
  69.5 0.7 copy-start.4
  70.3 16.3 %collective-permute-start.2 = (f16[2,1024,128]{2,1,0:T(8,128)(2,1)S(1)}, f16[2,1024,128]{2,1,0:T(8,128)(2,1)S(1)}, u32[]{:S(2)}, u32[]{:S(2)}) collective-permute-start(f16[2,1024,128]{2,1,0:T(8,128)(2,1)S(1)} %convert_element_type.69), channel_id=1, source_target_pairs={{0,16},{16,0},{32,48},{48,32},{64,80},{80,64},{96,112},{112,96},{1... | collective-permute-start | bytes 1572872 | tf_op jit(solution)/shard_map/ppermute | solution.py:300
  89.0 17.3 %collective-permute-start.3 = (f16[2,1024,128]{2,1,0:T(8,128)(2,1)}, f16[2,1024,128]{2,1,0:T(8,128)(2,1)}, u32[]{:S(2)}, u32[]{:S(2)}) collective-permute-start(f16[2,1024,128]{2,1,0:T(8,128)(2,1)} %convert_element_type.71), channel_id=1, source_target_pairs={{0,48},{16,32},{32,16},{48,0},{64,112},{80,96},{96,80},{112,64},{1... | collective-permute-start | bytes 1572872 | tf_op jit(solution)/shard_map/ppermute | solution.py:300
  109.9 24.2 %copy-start.2 = (f32[1024,128]{1,0:T(8,128)}, f32[1024,128]{1,0:T(8,128)S(1)}, u32[]{:S(2)}) copy-start(f32[1024,128]{1,0:T(8,128)S(1)} %get-tuple-element.26.refs_0_) | copy-start | bytes 1572868
  109.9 24.2 %copy-start.3 = (f32[1024,128]{1,0:T(8,128)}, f32[1024,128]{1,0:T(8,128)S(1)}, u32[]{:S(2)}) copy-start(f32[1024,128]{1,0:T(8,128)S(1)} %get-tuple-element.41.refs_9_) | copy-start | bytes 1572868
  110.0 15.4 %collective-permute-start.6 = (f16[1024,128]{1,0:T(8,128)(2,1)S(1)}, f16[1024,128]{1,0:T(8,128)(2,1)S(1)}, u32[]{:S(2)}, u32[]{:S(2)}) collective-permute-start(f16[1024,128]{1,0:T(8,128)(2,1)S(1)} %convert_element_type.73), channel_id=1, source_target_pairs={{64,0},{80,16},{96,32},{112,48},{128,64},{144,80},{160,96},{176,11... | collective-permute-start | bytes 786440 | tf_op jit(solution)/shard_map/ppermute | solution.py:358
  112.1 15.2 %collective-permute-start.4 = (f16[1024,128]{1,0:T(8,128)(2,1)S(1)}, f16[1024,128]{1,0:T(8,128)(2,1)S(1)}, u32[]{:S(2)}, u32[]{:S(2)}) collective-permute-start(f16[1024,128]{1,0:T(8,128)(2,1)S(1)} %convert_element_type.73), channel_id=1, source_target_pairs={{0,64},{16,80},{32,96},{48,112},{64,128},{80,144},{96,160},{112,17... | collective-permute-start | bytes 786440 | tf_op jit(solution)/shard_map/ppermute | solution.py:356
  125.4 10.7 %collective-permute-start.7 = (f16[1024,128]{1,0:T(8,128)(2,1)S(1)}, f16[1024,128]{1,0:T(8,128)(2,1)S(1)}, u32[]{:S(2)}, u32[]{:S(2)}) collective-permute-start(f16[1024,128]{1,0:T(8,128)(2,1)S(1)} %collective-permute-done.6), channel_id=1, source_target_pairs={{64,0},{80,16},{96,32},{112,48},{128,64},{144,80},{160,96},{176,11... | collective-permute-start | bytes 786440 | tf_op jit(solution)/shard_map/ppermute | solution.py:358
  127.3 9.9 %collective-permute-start.5 = (f16[1024,128]{1,0:T(8,128)(2,1)S(1)}, f16[1024,128]{1,0:T(8,128)(2,1)S(1)}, u32[]{:S(2)}, u32[]{:S(2)}) collective-permute-start(f16[1024,128]{1,0:T(8,128)(2,1)S(1)} %collective-permute-done.4), channel_id=1, source_target_pairs={{0,64},{16,80},{32,96},{48,112},{64,128},{80,144},{96,160},{112,17... | collective-permute-start | bytes 786440 | tf_op jit(solution)/shard_map/ppermute | solution.py:356
  137.2 9.5 %collective-permute-start.8 = (f16[1024,128]{1,0:T(8,128)(2,1)S(1)}, f16[1024,128]{1,0:T(8,128)(2,1)S(1)}, u32[]{:S(2)}, u32[]{:S(2)}) collective-permute-start(f16[1024,128]{1,0:T(8,128)(2,1)S(1)} %collective-permute-done.5), channel_id=1, source_target_pairs={{0,64},{16,80},{32,96},{48,112},{64,128},{80,144},{96,160},{112,17... | collective-permute-start | bytes 786440 | tf_op jit(solution)/shard_map/ppermute | solution.py:356
  142.8 9.5 %collective-permute-start.9 = (f16[1024,128]{1,0:T(8,128)(2,1)S(1)}, f16[1024,128]{1,0:T(8,128)(2,1)S(1)}, u32[]{:S(2)}, u32[]{:S(2)}) collective-permute-start(f16[1024,128]{1,0:T(8,128)(2,1)S(1)} %collective-permute-done.7), channel_id=1, source_target_pairs={{64,0},{80,16},{96,32},{112,48},{128,64},{144,80},{160,96},{176,11... | collective-permute-start | bytes 786440 | tf_op jit(solution)/shard_map/ppermute | solution.py:358
  152.3 8.3 %collective-permute-start.10 = (f16[1024,128]{1,0:T(8,128)(2,1)S(1)}, f16[1024,128]{1,0:T(8,128)(2,1)S(1)}, u32[]{:S(2)}, u32[]{:S(2)}) collective-permute-start(f16[1024,128]{1,0:T(8,128)(2,1)S(1)} %collective-permute-done.8), channel_id=1, source_target_pairs={{0,64},{16,80},{32,96},{48,112},{64,128},{80,144},{96,160},{112,17... | collective-permute-start | bytes 786440 | tf_op jit(solution)/shard_map/ppermute | solution.py:356
  190.6 0.9 copy-start.6
Sparse Core Ops, SparseCore 0:
  10.1 34.0 all-gather.6
  51.5 40.2 all-gather.8
  93.9 29.0 all-gather.10

commit v6 on v5

--- a/solution.py
+++ b/solution.py
@@ -67,7 +67,7 @@
     out[...] = state[...]
 
 
-def fine_kernel(place, own, received, weights, closing, defect_out, send_out, state, base, first, pad):
+def fine_kernel(place, own, received, weights, closing, defect_out, first_out, second_out, state, base, first, pad):
     section, phase = place[0], place[1]
     clear(pad)
     for _, rows in chunks():
@@ -99,53 +99,68 @@
         last = state[rows, :]
         defect = (last - begin) - SECTION * STEP_SIZE * first[rows, :]
         defect_out[rows, :] = defect.astype(LOW)
-        send_out[0, rows, :] = jnp.where(phase == 0, last, defect)
-        total = jnp.where(section == 0, begin, last - base[rows, :])
-        send_out[1, rows, :] = jnp.where(phase == 0, total, defect)
-
-
-def first_round_kernel(place, sent, received, leading, out, state, pad):
-    phase, in_first_group = place[1], place[0] < 4
+        first_out[rows, :] = jnp.where(phase == 0, last, defect)
+        coarse_part = jnp.where(section == 0, begin, -base[rows, :])
+        second_out[rows, :] = jnp.where(phase == 0, coarse_part, defect)
+
+
+def first_round_kernel(place, mine, coarse_part, near, across, leading, near_out, across_out, state, pad):
+    phase = place[1]
 
     @pl.when(phase < 2)
     def _():
         clear(pad)
         for _, rows in chunks():
-            state[rows, :] = jnp.where(phase == 0, sent[0, rows, :], received[0, rows, :])
+            state[rows, :] = jnp.where(phase == 0, mine[rows, :], near[rows, :])
         put_active(pad, state)
         for chunk, rows in chunks():
-            defect = jnp.where(phase == 0, received[0, rows, :], sent[0, rows, :])
-            total = jnp.where(phase == 0, sent[1, rows, :], received[1, rows, :])
-            change = SECTION * STEP_SIZE * conv(pad, leading.at[1], chunk) + defect
-            out[0, rows, :] = state[rows, :] + change
-            out[1, rows, :] = total + jnp.where(in_first_group, 0.0, change)
+            defect = jnp.where(phase == 0, near[rows, :], mine[rows, :])
+            state[rows, :] += SECTION * STEP_SIZE * conv(pad, leading.at[1], chunk) + defect
+            across_out[rows, :] = state[rows, :]
+            near_out[rows, :] = coarse_part[rows, :]
+
+    @pl.when(phase == 1)
+    def _():
+        put_active(pad, state)
+        for chunk, rows in chunks():
+            change = SECTION * STEP_SIZE * conv(pad, leading.at[2], chunk) + across[rows, :]
+            near_out[rows, :] = state[rows, :] + change
 
     @pl.when(phase >= 2)
     def _():
         for _, rows in chunks():
-            out[0, rows, :] = jnp.where(phase == 2, sent[0, rows, :], received[0, rows, :])
-            out[1, rows, :] = jnp.where(phase == 2, received[0, rows, :], sent[0, rows, :])
-
-
-def closing_kernel(place, sent, received, leading, out, total, state, pad):
+            near_out[rows, :] = jnp.where(phase == 3, across[rows, :], near[rows, :])
+            across_out[rows, :] = near[rows, :]
+
+
+def closing_kernel(
+    place, mine, coarse_part, near, across, level, near_later, across_later, leading, out, base, state, pad
+):
     phase, in_first_group = place[1], place[0] < 4
     clear(pad)
-    for _, rows in chunks():
-        state[rows, :] = jnp.where(phase < 2, sent[0, rows, :], received[0, rows, :])
-        total[rows, :] = jnp.where(phase < 2, sent[1, rows, :], received[1, rows, :])
-
-    def step(turn, carry):
+
+    @pl.when(phase < 2)
+    def _():
+        for _, rows in chunks():
+            state[rows, :] = jnp.where(phase == 0, near_later[rows, :], level[rows, :])
+            base[rows, :] = jnp.where(phase == 0, coarse_part[rows, :], near_later[rows, :])
+            out[rows, :] = jnp.where(phase == 0, across[rows, :], across_later[rows, :])
+
+    @pl.when(phase >= 2)
+    def _():
+        for _, rows in chunks():
+            state[rows, :] = across_later[rows, :]
+            base[rows, :] = jnp.where(phase == 2, near_later[rows, :], across[rows, :])
+            out[rows, :] = jnp.where(phase == 2, near[rows, :], mine[rows, :])
         put_active(pad, state)
         for chunk, rows in chunks():
-            defect = jnp.where(phase < 2, received[turn, rows, :], sent[turn, rows, :])
-            change = SECTION * STEP_SIZE * conv(pad, leading.at[2 + turn], chunk) + defect
-            state[rows, :] += change
-            total[rows, :] += jnp.where(in_first_group, 0.0, change)
-        return carry
-
-    lax.fori_loop(0, 2, step, 0)
-    for _, rows in chunks():
-        out[rows, :] = jnp.where(in_first_group, state[rows, :], total[rows, :])
+            defect = jnp.where(phase == 2, mine[rows, :], near[rows, :])
+            state[rows, :] += SECTION * STEP_SIZE * conv(pad, leading.at[2], chunk) + defect
+
+    put_active(pad, state)
+    for chunk, rows in chunks():
+        closing = state[rows, :] + SECTION * STEP_SIZE * conv(pad, leading.at[3], chunk) + out[rows, :]
+        out[rows, :] = closing + jnp.where(in_first_group, 0.0, base[rows, :])
 
 
 def load(sources, targets, arrived):
@@ -240,7 +255,7 @@
         for piece in range(PIXELS // PIECE):
             rows = pl.ds(piece * PIECE, PIECE)
             put(back_pad, piece, end_adjoint[rows, :] + change[rows, :])
-        low = back_pad[pl.ds(SIDE, PIXELS), CHANNELS : 2 * CHANNELS]
+        low = back_pad[pl.ds(SIDE, PIXELS), CHANNELS : 2 * CHANNELS].T
         for part in range(3):
             offset = 2 * replica + part
             columns = pads[
@@ -248,9 +263,8 @@
                 pl.ds(pl.multiple_of(SIDE * (offset // 3), SIDE), PIXELS),
                 pl.ds(pl.multiple_of(CHANNELS * (offset % 3), CHANNELS), CHANNELS),
             ]
-            grads[pl.ds(part * CHANNELS, CHANNELS), :] = STEP_SIZE * lax.dot_general(
-                columns, low, (((0,), (0,)), ((), ())), preferred_element_type=FULL
-            )
+            term = jnp.dot(low, columns, preferred_element_type=FULL)
+            grads[pl.ds(part * CHANNELS, CHANNELS), :] = STEP_SIZE * term.T
         for block in range(4):
             rows = pl.ds(pl.multiple_of(SIDE * replica + 72 * block, 8), 80)
             out[block, pl.ds(pl.multiple_of(192 + 80 * layer, 16), 80), :] = grads[rows, :].astype(LOW)
@@ -330,24 +344,28 @@
         .transpose(0, 1, 3, 2)
         .reshape(SECTION, 9 * CHANNELS, CHANNELS)
     )
-    image_shape, pair_shape = shape(*IMAGE), shape(2, *IMAGE)
+    image_shape = shape(*IMAGE)
 
     relaxed = call(relax_kernel, image_shape, [wide(), padding()], 8, None, start, weights)
     closing_weights, _ = lax.optimization_barrier((leading[3], relaxed))
     received = shift(relaxed, 1, sections)
     coarse = lax.all_gather(closing_weights, "layer", axis_index_groups=columns_of_groups)
-    defect, send = call(
+    defect, mine, coarse_part = call(
         fine_kernel,
-        (shape(*IMAGE, dtype=LOW), pair_shape),
+        (shape(*IMAGE, dtype=LOW), image_shape, image_shape),
         [wide(), wide(), wide(), padding()],
         12, place, start, received, weights, leading,
     )
     defects = lax.all_gather(defect, "layer", axis_index_groups=rows_of_groups)
-    received = swap(send, 1, sections)
-    send = call(first_round_kernel, pair_shape, [wide(), padding()], 10, place, send, received, leading)
-    received = swap(send, 3, sections)
+    near, across = swap(mine, 1, sections), swap(coarse_part, 3, sections)
+    level, passed = call(
+        first_round_kernel, (image_shape, image_shape), [wide(), padding()], 10,
+        place, mine, coarse_part, near, across, leading,
+    )
+    near_later, across_later = swap(level, 1, sections), swap(passed, 3, sections)
     defect_two, base = call(
-        closing_kernel, (image_shape, image_shape), [wide(), padding()], 10, place, send, received, leading
+        closing_kernel, (image_shape, image_shape), [wide(), padding()], 12,
+        place, mine, coarse_part, near, across, level, near_later, across_later, leading,
     )
     up = [(i, (i + 4) % sections) for i in range(sections)]
     down = [(j, i) for i, j in up]

time: 200 us -> 193 us (0.965)
  waiting for transfers between devices: 58.9 us -> 48.2 us
  starting transfers between devices: 38.2 us -> 40.6 us
    ppermute x2 -> x4, waiting for transfers between devices: 28.2 us -> 17.2 us  [swap(): lax.ppermute(block.astype(SENT), 'layer', [(i, i ^ distance) for i in ran...]
    ppermute x2 -> x4, starting transfers between devices: 5.39 us -> 10.8 us  [swap(): lax.ppermute(block.astype(SENT), 'layer', [(i, i ^ distance) for i in ran...]
    ppermute x4, starting transfers between devices: 21.5 us -> 18.6 us  [local(): moved = [lax.ppermute(ups[-1], 'layer', up)]]
  transfers between devices with their start and end apart: 14 -> 16, of which waited for: 10 -> 12; matrix products, arithmetic and copies ran while one was open for 7% -> 7% of each run, Pallas kernels for 6% -> 6%
where the time goes in v6:
time: 193 us
  waiting for transfers between devices  48.2 us (25%)
  starting transfers between devices  40.6 us (21%)
  blocking collectives  38.5 us (20%)
  Pallas kernels  27.6 us (14%)
  between operations  14.1 us (7%)
  other arithmetic  13.2 us (7%)
  local copies, waits for them, and re-layouts  10.3 us (5%)
    pallas_call x5, Pallas kernels, call(): pl.pallas_call(body, out_shape=outs, in_specs=in_specs, out_specs=jax.tre...  27.6 us
    all_to_all x1, blocking collectives, local(): lax.all_to_all(jnp.tile(both, (tiles // 4, 1, 1, 1, 1)), 'space', 0, 0, t...  26.2 us
    ppermute x4, starting transfers between devices, local(): moved = [lax.ppermute(ups[-1], 'layer', up)]  18.6 us
    ppermute x4, waiting for transfers between devices, swap(): lax.ppermute(block.astype(SENT), 'layer', [(i, i ^ distance) for i in ran...  17.2 us
    ppermute x2, waiting for transfers between devices, shift(): return lax.ppermute(block.astype(SENT), 'layer', route).astype(block.dtype)  14.4 us
    all_to_all x1, blocking collectives, local(): lax.all_to_all(parts, 'space', 0, 0, axis_index_groups=row_groups, tiled=...  12.3 us
    ppermute x3, waiting for transfers between devices, local(): moved.append(lax.ppermute(downs[-1], 'layer', down))  12.2 us
    ppermute x4, starting transfers between devices, swap(): lax.ppermute(block.astype(SENT), 'layer', [(i, i ^ distance) for i in ran...  10.8 us
  transfers between devices with their start and end apart: 16, of which 12 were waited for; matrix products, arithmetic and copies ran while one was open for 7% of the time, Pallas kernels for 6%

profile of v6, /device:TPU:24, one launch (start us, length us, event | category | flops | bytes accessed | tf_op | source)
XLA Modules:
  0.0 192.5 jit_solution(14001808394220109379)
XLA Ops:
  8.2 1.7 slice_bitcast_fusion
  9.9 3.4 %collective-permute-start = (f16[4,2,32,128]{3,2,1,0:T(8,128)(2,1)S(1)}, f16[4,2,32,128]{3,2,1,0:T(8,128)(2,1)S(1)}, u32[]{:S(2)}, u32[]{:S(2)}) collective-permute-start(f16[4,2,32,128]{3,2,1,0:T(8,128)(2,1)S(1)} %convert_bitcast_fusion.1), channel_id=1, source_target_pairs={{0,16},{16,32},{32,48},{48,64},{64,80},{80,96},{96,112},{112,128},... | collective-permute-start | bytes 196616 | tf_op jit(solution)/shard_map/ppermute | solution.py:320
  14.3 3.9 %collective-permute-done = f16[4,2,32,128]{3,2,1,0:T(8,128)(2,1)S(1)} collective-permute-done((f16[4,2,32,128]{3,2,1,0:T(8,128)(2,1)S(1)}, f16[4,2,32,128]{3,2,1,0:T(8,128)(2,1)S(1)}, u32[]{:S(2)}, u32[]{:S(2)}) %collective-permute-start) | collective-permute-done | bytes 65568 | tf_op jit(solution)/shard_map/ppermute | solution.py:320
  18.4 26.2 %all_to_all.10 = f16[16,2,2,32,128]{4,3,2,1,0:T(8,128)(2,1)S(1)} all-to-all(f16[16,2,2,32,128]{4,3,2,1,0:T(8,128)(2,1)S(1)} %bitcast.34), channel_id=1, replica_groups=mesh['layer'=32,'space'=16] {'space'}, dimensions={0} | all-to-all | bytes 1048576 | tf_op jit(solution)/shard_map/all_to_all | solution.py:338
  46.3 3.2 %shard_map.67 = f32[1024,128]{1,0:T(8,128)S(1)} custom-call(f32[1024,128]{1,0:T(8,128)S(1)} %bitcast.30, bf16[4,1152,128]{2,1,0:T(8,128)(2,1)S(1)} %copy-done.1), custom_call_target="tpu_custom_call" | custom-call | tf_op jit(solution)/shard_map/pallas_call | solution.py:291
  50.3 1.8 slice.38
  52.2 1.9 collective-permute-start.1
  54.3 10.4 %collective-permute-done.1 = f16[1024,128]{1,0:T(8,128)(2,1)S(1)} collective-permute-done((f16[1024,128]{1,0:T(8,128)(2,1)S(1)}, f16[1024,128]{1,0:T(8,128)(2,1)S(1)}, u32[]{:S(2)}, u32[]{:S(2)}) %collective-permute-start.1) | collective-permute-done | bytes 262176 | tf_op jit(solution)/shard_map/ppermute | solution.py:320
  65.8 4.6 %shard_map.68 = (bf16[1024,128]{1,0:T(8,128)(2,1)S(1)}, f32[1024,128]{1,0:T(8,128)S(1)}, f32[1024,128]{1,0:T(8,128)S(1)}) custom-call(s32[4]{0:T(128)S(1)} %pad_add_fusion.place, f32[1024,128]{1,0:T(8,128)S(1)} %bitcast.31, f32[1024,128]{1,0:T(8,128)S(1)} %convert_element_type.80.received, bf16[4,1152,128]{2,1,0:T(8,128)(2,1)S(1)} %copy-done.1, ...), custom_call_target="tpu_custom_call" | custom-call | tf_op jit(solution)/shard_map/pallas_call | solution.py:291
  71.9 4.1 %collective-permute-start.3 = (f16[1024,128]{1,0:T(8,128)(2,1)}, f16[1024,128]{1,0:T(8,128)(2,1)}, u32[]{:S(2)}, u32[]{:S(2)}) collective-permute-start(f16[1024,128]{1,0:T(8,128)(2,1)} %convert_element_type.83), channel_id=1, source_target_pairs={{0,48},{16,32},{32,16},{48,0},{64,112},{80,96},{96,80},{112,64},{1... | collective-permute-start | bytes 786440 | tf_op jit(solution)/shard_map/ppermute | solution.py:314
  76.7 1.9 collective-permute-start.2
  78.6 5.4 %collective-permute-done.3 = f16[1024,128]{1,0:T(8,128)(2,1)} collective-permute-done((f16[1024,128]{1,0:T(8,128)(2,1)}, f16[1024,128]{1,0:T(8,128)(2,1)}, u32[]{:S(2)}, u32[]{:S(2)}) %collective-permute-start.3) | collective-permute-done | bytes 262176 | tf_op jit(solution)/shard_map/ppermute | solution.py:314
  85.0 2.1 %collective-permute-done.2 = f16[1024,128]{1,0:T(8,128)(2,1)} collective-permute-done((f16[1024,128]{1,0:T(8,128)(2,1)}, f16[1024,128]{1,0:T(8,128)(2,1)}, u32[]{:S(2)}, u32[]{:S(2)}) %collective-permute-start.2) | collective-permute-done | bytes 262176 | tf_op jit(solution)/shard_map/ppermute | solution.py:314
  88.1 1.4 shard_map.69
  89.6 2.4 %collective-permute-start.4 = (f16[1024,128]{1,0:T(8,128)(2,1)S(1)}, f16[1024,128]{1,0:T(8,128)(2,1)S(1)}, u32[]{:S(2)}, u32[]{:S(2)}) collective-permute-start(f16[1024,128]{1,0:T(8,128)(2,1)S(1)} %convert_element_type.85), channel_id=1, source_target_pairs={{0,16},{16,0},{32,48},{48,32},{64,80},{80,64},{96,112},{112,96},{1... | collective-permute-start | bytes 786440 | tf_op jit(solution)/shard_map/ppermute | solution.py:314
  92.0 2.4 %collective-permute-start.5 = (f16[1024,128]{1,0:T(8,128)(2,1)S(1)}, f16[1024,128]{1,0:T(8,128)(2,1)S(1)}, u32[]{:S(2)}, u32[]{:S(2)}) collective-permute-start(f16[1024,128]{1,0:T(8,128)(2,1)S(1)} %convert_element_type.87), channel_id=1, source_target_pairs={{0,48},{16,32},{32,16},{48,0},{64,112},{80,96},{96,80},{112,64},{1... | collective-permute-start | bytes 786440 | tf_op jit(solution)/shard_map/ppermute | solution.py:314
  94.4 6.1 %collective-permute-done.4 = f16[1024,128]{1,0:T(8,128)(2,1)S(1)} collective-permute-done((f16[1024,128]{1,0:T(8,128)(2,1)S(1)}, f16[1024,128]{1,0:T(8,128)(2,1)S(1)}, u32[]{:S(2)}, u32[]{:S(2)}) %collective-permute-start.4) | collective-permute-done | bytes 262176 | tf_op jit(solution)/shard_map/ppermute | solution.py:314
  100.6 3.6 %collective-permute-done.5 = f16[1024,128]{1,0:T(8,128)(2,1)S(1)} collective-permute-done((f16[1024,128]{1,0:T(8,128)(2,1)S(1)}, f16[1024,128]{1,0:T(8,128)(2,1)S(1)}, u32[]{:S(2)}, u32[]{:S(2)}) %collective-permute-start.5) | collective-permute-done | bytes 262176 | tf_op jit(solution)/shard_map/ppermute | solution.py:314
  104.2 1.5 shard_map.70
  105.8 1.9 collective-permute-start.8
  107.7 6.0 %collective-permute-start.6 = (f16[1024,128]{1,0:T(8,128)(2,1)S(1)}, f16[1024,128]{1,0:T(8,128)(2,1)S(1)}, u32[]{:S(2)}, u32[]{:S(2)}) collective-permute-start(f16[1024,128]{1,0:T(8,128)(2,1)S(1)} %convert_element_type.89), channel_id=1, source_target_pairs={{0,64},{16,80},{32,96},{48,112},{64,128},{80,144},{96,160},{112,17... | collective-permute-start | bytes 786440 | tf_op jit(solution)/shard_map/ppermute | solution.py:374
  113.7 4.6 %collective-permute-done.8 = f16[1024,128]{1,0:T(8,128)(2,1)S(1)} collective-permute-done((f16[1024,128]{1,0:T(8,128)(2,1)S(1)}, f16[1024,128]{1,0:T(8,128)(2,1)S(1)}, u32[]{:S(2)}, u32[]{:S(2)}) %collective-permute-start.8) | collective-permute-done | bytes 262176 | tf_op jit(solution)/shard_map/ppermute | solution.py:376
  118.3 1.9 collective-permute-start.9
  120.2 5.1 %collective-permute-start.7 = (f16[1024,128]{1,0:T(8,128)(2,1)S(1)}, f16[1024,128]{1,0:T(8,128)(2,1)S(1)}, u32[]{:S(2)}, u32[]{:S(2)}) collective-permute-start(f16[1024,128]{1,0:T(8,128)(2,1)S(1)} %collective-permute-done.6), channel_id=1, source_target_pairs={{0,64},{16,80},{32,96},{48,112},{64,128},{80,144},{96,160},{112,17... | collective-permute-start | bytes 786440 | tf_op jit(solution)/shard_map/ppermute | solution.py:374
  127.0 2.2 %collective-permute-done.9 = f16[1024,128]{1,0:T(8,128)(2,1)S(1)} collective-permute-done((f16[1024,128]{1,0:T(8,128)(2,1)S(1)}, f16[1024,128]{1,0:T(8,128)(2,1)S(1)}, u32[]{:S(2)}, u32[]{:S(2)}) %collective-permute-start.9) | collective-permute-done | bytes 262176 | tf_op jit(solution)/shard_map/ppermute | solution.py:376
  130.4 5.6 %collective-permute-start.10 = (f16[1024,128]{1,0:T(8,128)(2,1)S(1)}, f16[1024,128]{1,0:T(8,128)(2,1)S(1)}, u32[]{:S(2)}, u32[]{:S(2)}) collective-permute-start(f16[1024,128]{1,0:T(8,128)(2,1)S(1)} %collective-permute-done.7), channel_id=1, source_target_pairs={{0,64},{16,80},{32,96},{48,112},{64,128},{80,144},{96,160},{112,17... | collective-permute-start | bytes 786440 | tf_op jit(solution)/shard_map/ppermute | solution.py:374
  136.0 1.9 collective-permute-start.11
  140.2 5.3 %collective-permute-done.11 = f16[1024,128]{1,0:T(8,128)(2,1)S(1)} collective-permute-done((f16[1024,128]{1,0:T(8,128)(2,1)S(1)}, f16[1024,128]{1,0:T(8,128)(2,1)S(1)}, u32[]{:S(2)}, u32[]{:S(2)}) %collective-permute-start.11) | collective-permute-done | bytes 262176 | tf_op jit(solution)/shard_map/ppermute | solution.py:376
  145.5 1.9 collective-permute-start.12
  151.1 2.7 %collective-permute-done.12 = f16[1024,128]{1,0:T(8,128)(2,1)S(1)} collective-permute-done((f16[1024,128]{1,0:T(8,128)(2,1)S(1)}, f16[1024,128]{1,0:T(8,128)(2,1)S(1)}, u32[]{:S(2)}, u32[]{:S(2)}) %collective-permute-start.12) | collective-permute-done | bytes 262176 | tf_op jit(solution)/shard_map/ppermute | solution.py:374
  154.6 16.8 %shard_map.71 = bf16[4,512,128]{2,1,0:T(8,128)(2,1)} custom-call(s32[4]{0:T(128)} %copy-done.7, f32[1024,128]{1,0:T(8,128)} %copy-done.4, f32[1024,128]{1,0:T(8,128)} %convert_element_type.90.refs_1_, f32[1024,128]{1,0:T(8,128)} %convert_element_type.92.refs_2_, f32[1024,128]{1,0:T(8,128)} %convert_element_type.94.refs_3_, ...), custom_call_target="tpu_custom_call" | custom-call | tf_op jit(solution)/shard_map/pallas_call | solution.py:291
  171.4 12.3 %all_to_all.11 = bf16[4,512,128]{2,1,0:T(8,128)(2,1)S(1)} all-to-all(bf16[4,512,128]{2,1,0:T(8,128)(2,1)} %shard_map.71), channel_id=1, replica_groups={{0,1,2,3},{4,5,6,7},{8,9,10,11},{12,13,14,15},{16,17,18,19},{20,21,22,2..., dimensions={0} | all-to-all | bytes 1048576 | tf_op jit(solution)/shard_map/all_to_all | solution.py:403
  (67 shorter events, 21.9 us)
Async XLA Ops:
  7.2 11.1 %copy-start.9 = (f32[4,2,32,128]{3,2,1,0:T(8,128)S(1)}, f32[4,2,32,128]{3,2,1,0:T(8,128)}, u32[]{:S(2)}) copy-start(f32[4,2,32,128]{3,2,1,0:T(8,128)} %param.4) | copy-start | bytes 393220
  7.2 43.1 %all-gather.7.cloned.1.call-start = ((), (), s32[]{:S(2)}) async-start(), calls=%async_computation.2 | async-start | bytes 1474560 | tf_op jit(solution)/shard_map/all_gather | solution.py:335
  9.9 143.9 %all-gather.9.cloned.1.call-start = ((), (), s32[]{:S(2)}) async-start(), calls=%async_computation.3 | async-start | bytes 2654208 | tf_op jit(solution)/shard_map/all_gather | solution.py:352
  9.9 8.3 %collective-permute-start = (f16[4,2,32,128]{3,2,1,0:T(8,128)(2,1)S(1)}, f16[4,2,32,128]{3,2,1,0:T(8,128)(2,1)S(1)}, u32[]{:S(2)}, u32[]{:S(2)}) collective-permute-start(f16[4,2,32,128]{3,2,1,0:T(8,128)(2,1)S(1)} %convert_bitcast_fusion.1), channel_id=1, source_target_pairs={{0,16},{16,32},{32,48},{48,64},{64,80},{80,96},{96,112},{112,128},... | collective-permute-start | bytes 196616 | tf_op jit(solution)/shard_map/ppermute | solution.py:320
  44.8 1.5 copy-start.1
  49.5 0.8 copy-start.2
  50.3 14.4 %copy-start = (bf16[4608,128]{1,0:T(8,128)(2,1)S(1)}, bf16[4608,128]{1,0:T(8,128)(2,1)}, u32[]{:S(2)}) copy-start(bf16[4608,128]{1,0:T(8,128)(2,1)} %all-gather.7.cloned.1.call-done) | copy-start | bytes 3538948
  52.1 102.5 %all-gather.11.cloned.1.call-start = ((), (), s32[]{:S(2)}) async-start(), calls=%async_computation.4 | async-start | bytes 1310720 | tf_op jit(solution)/shard_map/all_gather | solution.py:359
  52.2 12.5 %collective-permute-start.1 = (f16[1024,128]{1,0:T(8,128)(2,1)S(1)}, f16[1024,128]{1,0:T(8,128)(2,1)S(1)}, u32[]{:S(2)}, u32[]{:S(2)}) collective-permute-start(f16[1024,128]{1,0:T(8,128)(2,1)S(1)} %convert_element_type.79), channel_id=1, source_target_pairs={{0,16},{16,32},{32,48},{48,64},{64,80},{80,96},{96,112},{112,128},... | collective-permute-start | bytes 786440 | tf_op jit(solution)/shard_map/ppermute | solution.py:320
  54.2 50.0 %copy-start.7 = (s32[4]{0:T(128)}, s32[4]{0:T(128)S(1)}, u32[]{:S(2)}) copy-start(s32[4]{0:T(128)S(1)} %pad_add_fusion.place) | copy-start | bytes 52
  64.7 1.0 copy-start.3
  70.4 0.7 copy-start.6
  71.9 12.2 %collective-permute-start.3 = (f16[1024,128]{1,0:T(8,128)(2,1)}, f16[1024,128]{1,0:T(8,128)(2,1)}, u32[]{:S(2)}, u32[]{:S(2)}) collective-permute-start(f16[1024,128]{1,0:T(8,128)(2,1)} %convert_element_type.83), channel_id=1, source_target_pairs={{0,48},{16,32},{32,16},{48,0},{64,112},{80,96},{96,80},{112,64},{1... | collective-permute-start | bytes 786440 | tf_op jit(solution)/shard_map/ppermute | solution.py:314
  76.7 10.4 %collective-permute-start.2 = (f16[1024,128]{1,0:T(8,128)(2,1)}, f16[1024,128]{1,0:T(8,128)(2,1)}, u32[]{:S(2)}, u32[]{:S(2)}) collective-permute-start(f16[1024,128]{1,0:T(8,128)(2,1)} %convert_element_type.81), channel_id=1, source_target_pairs={{0,16},{16,0},{32,48},{48,32},{64,80},{80,64},{96,112},{112,96},{1... | collective-permute-start | bytes 786440 | tf_op jit(solution)/shard_map/ppermute | solution.py:314
  89.6 11.0 %collective-permute-start.4 = (f16[1024,128]{1,0:T(8,128)(2,1)S(1)}, f16[1024,128]{1,0:T(8,128)(2,1)S(1)}, u32[]{:S(2)}, u32[]{:S(2)}) collective-permute-start(f16[1024,128]{1,0:T(8,128)(2,1)S(1)} %convert_element_type.85), channel_id=1, source_target_pairs={{0,16},{16,0},{32,48},{48,32},{64,80},{80,64},{96,112},{112,96},{1... | collective-permute-start | bytes 786440 | tf_op jit(solution)/shard_map/ppermute | solution.py:314
  92.0 12.1 %collective-permute-start.5 = (f16[1024,128]{1,0:T(8,128)(2,1)S(1)}, f16[1024,128]{1,0:T(8,128)(2,1)S(1)}, u32[]{:S(2)}, u32[]{:S(2)}) collective-permute-start(f16[1024,128]{1,0:T(8,128)(2,1)S(1)} %convert_element_type.87), channel_id=1, source_target_pairs={{0,48},{16,32},{32,16},{48,0},{64,112},{80,96},{96,80},{112,64},{1... | collective-permute-start | bytes 786440 | tf_op jit(solution)/shard_map/ppermute | solution.py:314
  105.7 21.2 %copy-start.4 = (f32[1024,128]{1,0:T(8,128)}, f32[1024,128]{1,0:T(8,128)S(1)}, u32[]{:S(2)}) copy-start(f32[1024,128]{1,0:T(8,128)S(1)} %get-tuple-element.32.refs_0_) | copy-start | bytes 1572868
  105.7 21.2 %copy-start.5 = (f32[1024,128]{1,0:T(8,128)}, f32[1024,128]{1,0:T(8,128)S(1)}, u32[]{:S(2)}) copy-start(f32[1024,128]{1,0:T(8,128)S(1)} %get-tuple-element.47.refs_9_) | copy-start | bytes 1572868
  105.8 12.5 %collective-permute-start.8 = (f16[1024,128]{1,0:T(8,128)(2,1)S(1)}, f16[1024,128]{1,0:T(8,128)(2,1)S(1)}, u32[]{:S(2)}, u32[]{:S(2)}) collective-permute-start(f16[1024,128]{1,0:T(8,128)(2,1)S(1)} %convert_element_type.89), channel_id=1, source_target_pairs={{64,0},{80,16},{96,32},{112,48},{128,64},{144,80},{160,96},{176,11... | collective-permute-start | bytes 786440 | tf_op jit(solution)/shard_map/ppermute | solution.py:376
  107.7 12.5 %collective-permute-start.6 = (f16[1024,128]{1,0:T(8,128)(2,1)S(1)}, f16[1024,128]{1,0:T(8,128)(2,1)S(1)}, u32[]{:S(2)}, u32[]{:S(2)}) collective-permute-start(f16[1024,128]{1,0:T(8,128)(2,1)S(1)} %convert_element_type.89), channel_id=1, source_target_pairs={{0,64},{16,80},{32,96},{48,112},{64,128},{80,144},{96,160},{112,17... | collective-permute-start | bytes 786440 | tf_op jit(solution)/shard_map/ppermute | solution.py:374
  118.3 10.9 %collective-permute-start.9 = (f16[1024,128]{1,0:T(8,128)(2,1)S(1)}, f16[1024,128]{1,0:T(8,128)(2,1)S(1)}, u32[]{:S(2)}, u32[]{:S(2)}) collective-permute-start(f16[1024,128]{1,0:T(8,128)(2,1)S(1)} %collective-permute-done.8), channel_id=1, source_target_pairs={{64,0},{80,16},{96,32},{112,48},{128,64},{144,80},{160,96},{176,11... | collective-permute-start | bytes 786440 | tf_op jit(solution)/shard_map/ppermute | solution.py:376
  120.2 10.2 %collective-permute-start.7 = (f16[1024,128]{1,0:T(8,128)(2,1)S(1)}, f16[1024,128]{1,0:T(8,128)(2,1)S(1)}, u32[]{:S(2)}, u32[]{:S(2)}) collective-permute-start(f16[1024,128]{1,0:T(8,128)(2,1)S(1)} %collective-permute-done.6), channel_id=1, source_target_pairs={{0,64},{16,80},{32,96},{48,112},{64,128},{80,144},{96,160},{112,17... | collective-permute-start | bytes 786440 | tf_op jit(solution)/shard_map/ppermute | solution.py:374
  130.4 9.7 %collective-permute-start.10 = (f16[1024,128]{1,0:T(8,128)(2,1)S(1)}, f16[1024,128]{1,0:T(8,128)(2,1)S(1)}, u32[]{:S(2)}, u32[]{:S(2)}) collective-permute-start(f16[1024,128]{1,0:T(8,128)(2,1)S(1)} %collective-permute-done.7), channel_id=1, source_target_pairs={{0,64},{16,80},{32,96},{48,112},{64,128},{80,144},{96,160},{112,17... | collective-permute-start | bytes 786440 | tf_op jit(solution)/shard_map/ppermute | solution.py:374
  136.0 9.5 %collective-permute-start.11 = (f16[1024,128]{1,0:T(8,128)(2,1)S(1)}, f16[1024,128]{1,0:T(8,128)(2,1)S(1)}, u32[]{:S(2)}, u32[]{:S(2)}) collective-permute-start(f16[1024,128]{1,0:T(8,128)(2,1)S(1)} %collective-permute-done.9), channel_id=1, source_target_pairs={{64,0},{80,16},{96,32},{112,48},{128,64},{144,80},{160,96},{176,11... | collective-permute-start | bytes 786440 | tf_op jit(solution)/shard_map/ppermute | solution.py:376
  145.5 8.3 %collective-permute-start.12 = (f16[1024,128]{1,0:T(8,128)(2,1)S(1)}, f16[1024,128]{1,0:T(8,128)(2,1)S(1)}, u32[]{:S(2)}, u32[]{:S(2)}) collective-permute-start(f16[1024,128]{1,0:T(8,128)(2,1)S(1)} %collective-permute-done.10), channel_id=1, source_target_pairs={{0,64},{16,80},{32,96},{48,112},{64,128},{80,144},{96,160},{112,17... | collective-permute-start | bytes 786440 | tf_op jit(solution)/shard_map/ppermute | solution.py:374
  183.7 0.9 copy-start.8
Sparse Core Ops, SparseCore 0:
  10.1 34.0 all-gather.6
  52.2 40.3 all-gather.8
  94.7 28.9 all-gather.10

commit v7 on v6

--- a/solution.py
+++ b/solution.py
@@ -37,11 +37,6 @@
     pad[rows, 2 * CHANNELS : 3 * CHANNELS] = right.astype(LOW)
 
 
-def put_active(pad, state):
-    for piece in range(PIXELS // PIECE):
-        put(pad, piece, jnp.tanh(state[pl.ds(piece * PIECE, PIECE), :]))
-
-
 def conv(pad, kernel, chunk):
     columns = jnp.concatenate(
         [pad[pl.ds(chunk * CHUNK + SIDE * shift, CHUNK), :] for shift in range(3)], axis=1
@@ -53,13 +48,24 @@
     return [(chunk, pl.ds(chunk * CHUNK, CHUNK)) for chunk in range(PIXELS // CHUNK)]
 
 
+def swept(pad, state, put_piece=None):
+    done = 0
+    for chunk, rows in chunks():
+        while done < min(2 * chunk + 3, PIXELS // PIECE):
+            if put_piece is None:
+                put(pad, done, jnp.tanh(state[pl.ds(done * PIECE, PIECE), :]))
+            else:
+                put_piece(done)
+            done += 1
+        yield chunk, rows
+
+
 def relax_kernel(begin, weights, out, state, pad):
     clear(pad)
     state[...] = begin[...]
 
     def step(layer, carry):
-        put_active(pad, state)
-        for chunk, rows in chunks():
+        for chunk, rows in swept(pad, state):
             state[rows, :] += STEP_SIZE * conv(pad, weights.at[layer], chunk)
         return carry
 
@@ -75,8 +81,7 @@
         state[rows, :] = begin
         base[rows, :] = begin
 
-    put_active(pad, state)
-    for chunk, rows in chunks():
+    for chunk, rows in swept(pad, state):
         term = conv(pad, weights.at[0], chunk)
         first[rows, :] = term
         state[rows, :] += STEP_SIZE * term
@@ -88,8 +93,7 @@
             base[rows, :] += long_term
 
     def step(layer, carry):
-        put_active(pad, state)
-        for chunk, rows in chunks():
+        for chunk, rows in swept(pad, state):
             state[rows, :] += STEP_SIZE * conv(pad, weights.at[layer], chunk)
         return carry
 
@@ -112,8 +116,7 @@
         clear(pad)
         for _, rows in chunks():
             state[rows, :] = jnp.where(phase == 0, mine[rows, :], near[rows, :])
-        put_active(pad, state)
-        for chunk, rows in chunks():
+        for chunk, rows in swept(pad, state):
             defect = jnp.where(phase == 0, near[rows, :], mine[rows, :])
             state[rows, :] += SECTION * STEP_SIZE * conv(pad, leading.at[1], chunk) + defect
             across_out[rows, :] = state[rows, :]
@@ -121,8 +124,7 @@
 
     @pl.when(phase == 1)
     def _():
-        put_active(pad, state)
-        for chunk, rows in chunks():
+        for chunk, rows in swept(pad, state):
             change = SECTION * STEP_SIZE * conv(pad, leading.at[2], chunk) + across[rows, :]
             near_out[rows, :] = state[rows, :] + change
 
@@ -152,13 +154,11 @@
             state[rows, :] = across_later[rows, :]
             base[rows, :] = jnp.where(phase == 2, near_later[rows, :], across[rows, :])
             out[rows, :] = jnp.where(phase == 2, near[rows, :], mine[rows, :])
-        put_active(pad, state)
-        for chunk, rows in chunks():
+        for chunk, rows in swept(pad, state):
             defect = jnp.where(phase == 2, mine[rows, :], near[rows, :])
             state[rows, :] += SECTION * STEP_SIZE * conv(pad, leading.at[2], chunk) + defect
 
-    put_active(pad, state)
-    for chunk, rows in chunks():
+    for chunk, rows in swept(pad, state):
         closing = state[rows, :] + SECTION * STEP_SIZE * conv(pad, leading.at[3], chunk) + out[rows, :]
         out[rows, :] = closing + jnp.where(in_first_group, 0.0, base[rows, :])
 
@@ -179,20 +179,20 @@
     held, arrived = refs[9:16], refs[16]
     coarse, images, defects, leading, weights, flipped, end_adjoint = held
     phase, group, replica = place[1], place[2], place[3]
-    copies = load(stored, [slots.at[number] for number in range(8)] + list(held), arrived)
+    copies = load(stored[:10], [slots.at[number] for number in range(8)] + list(held[:2]), arrived)
     clear(back_pad)
     for layer in range(SECTION):
         clear(pads.at[layer])
     grads[3 * CHANNELS :, :] = jnp.zeros((8, CHANNELS), FULL)
 
-    for copy in copies[:10]:
+    for copy in copies:
         copy.wait()
+    copies = load(stored[10:], held[2:], arrived)
     for _, rows in chunks():
         state[rows, :] = slots[group, rows, :]
 
     def chain_step(turn, carry):
-        put_active(back_pad, state)
-        for chunk, rows in chunks():
+        for chunk, rows in swept(back_pad, state):
             long_term = (4 * SECTION * STEP_SIZE) * conv(back_pad, coarse.at[turn], chunk)
             state[rows, :] += long_term + slots[group - turn, rows, :]
         return carry
@@ -208,12 +208,11 @@
     for _, rows in chunks():
         end[rows, :] = state[rows, :]
         state[rows, :] = begin[rows, :]
-    for copy in copies[10:12]:
+    for copy in copies[:2]:
         copy.wait()
 
     def level_step(turn, carry):
-        put_active(back_pad, state)
-        for chunk, rows in chunks():
+        for chunk, rows in swept(back_pad, state):
             state[rows, :] += (
                 SECTION * STEP_SIZE * conv(back_pad, leading.at[turn], chunk)
                 + defects[turn, rows, :].astype(FULL)
@@ -230,24 +229,23 @@
         return carry
 
     lax.fori_loop(0, 3, level_step, 0)
-    for copy in copies[12:]:
+    for copy in copies[2:]:
         copy.wait()
 
-    def active(layer):
-        for piece in range(PIXELS // PIECE):
-            rows = pl.ds(piece * PIECE, PIECE)
-            slope = jnp.tanh(begin[rows, :])
-            slopes[layer, rows, :] = STEP_SIZE * (1.0 - slope * slope)
-            put(pads.at[layer], piece, slope)
+    def active(layer, piece):
+        rows = pl.ds(piece * PIECE, PIECE)
+        slope = jnp.tanh(begin[rows, :])
+        slopes[layer, rows, :] = STEP_SIZE * (1.0 - slope * slope)
+        put(pads.at[layer], piece, slope)
 
     def forward(layer, carry):
-        active(layer)
-        for chunk, rows in chunks():
+        for chunk, rows in swept(None, None, lambda piece: active(layer, piece)):
             begin[rows, :] += STEP_SIZE * conv(pads.at[layer], weights.at[layer], chunk)
         return carry
 
     lax.fori_loop(0, SECTION - 1, forward, 0)
-    active(SECTION - 1)
+    for piece in range(PIXELS // PIECE):
+        active(SECTION - 1, piece)
     change[...] = jnp.zeros(IMAGE, FULL)
 
     def backward(turn, carry):

time: 193 us -> 193 us (level)
  no operation moved by 1% of the time
where the time goes in v7:
time: 193 us
  waiting for transfers between devices  48.2 us (25%)
  starting transfers between devices  40.6 us (21%)
  blocking collectives  38.5 us (20%)
  Pallas kernels  27.6 us (14%)
  between operations  14.1 us (7%)
  other arithmetic  13.2 us (7%)
  local copies, waits for them, and re-layouts  10.3 us (5%)
    pallas_call x5, Pallas kernels, call(): pl.pallas_call(body, out_shape=outs, in_specs=in_specs, out_specs=jax.tre...  27.6 us
    all_to_all x1, blocking collectives, local(): lax.all_to_all(jnp.tile(both, (tiles // 4, 1, 1, 1, 1)), 'space', 0, 0, t...  26.2 us
    ppermute x4, starting transfers between devices, local(): moved = [lax.ppermute(ups[-1], 'layer', up)]  18.6 us
    ppermute x4, waiting for transfers between devices, swap(): lax.ppermute(block.astype(SENT), 'layer', [(i, i ^ distance) for i in ran...  17.2 us
    ppermute x2, waiting for transfers between devices, shift(): return lax.ppermute(block.astype(SENT), 'layer', route).astype(block.dtype)  14.4 us
    all_to_all x1, blocking collectives, local(): lax.all_to_all(parts, 'space', 0, 0, axis_index_groups=row_groups, tiled=...  12.3 us
    ppermute x3, waiting for transfers between devices, local(): moved.append(lax.ppermute(downs[-1], 'layer', down))  12.2 us
    ppermute x4, starting transfers between devices, swap(): lax.ppermute(block.astype(SENT), 'layer', [(i, i ^ distance) for i in ran...  10.8 us
  transfers between devices with their start and end apart: 16, of which 12 were waited for; matrix products, arithmetic and copies ran while one was open for 7% of the time, Pallas kernels for 6%

profile of v7, /device:TPU:24, one launch (start us, length us, event | category | flops | bytes accessed | tf_op | source)
XLA Modules:
  0.0 192.5 jit_solution(132836210588672222)
XLA Ops:
  8.2 1.7 slice_bitcast_fusion
  9.9 3.4 %collective-permute-start = (f16[4,2,32,128]{3,2,1,0:T(8,128)(2,1)S(1)}, f16[4,2,32,128]{3,2,1,0:T(8,128)(2,1)S(1)}, u32[]{:S(2)}, u32[]{:S(2)}) collective-permute-start(f16[4,2,32,128]{3,2,1,0:T(8,128)(2,1)S(1)} %convert_bitcast_fusion.1), channel_id=1, source_target_pairs={{0,16},{16,32},{32,48},{48,64},{64,80},{80,96},{96,112},{112,128},... | collective-permute-start | bytes 196616 | tf_op jit(solution)/shard_map/ppermute | solution.py:318
  14.3 3.9 %collective-permute-done = f16[4,2,32,128]{3,2,1,0:T(8,128)(2,1)S(1)} collective-permute-done((f16[4,2,32,128]{3,2,1,0:T(8,128)(2,1)S(1)}, f16[4,2,32,128]{3,2,1,0:T(8,128)(2,1)S(1)}, u32[]{:S(2)}, u32[]{:S(2)}) %collective-permute-start) | collective-permute-done | bytes 65568 | tf_op jit(solution)/shard_map/ppermute | solution.py:318
  18.4 26.2 %all_to_all.10 = f16[16,2,2,32,128]{4,3,2,1,0:T(8,128)(2,1)S(1)} all-to-all(f16[16,2,2,32,128]{4,3,2,1,0:T(8,128)(2,1)S(1)} %bitcast.34), channel_id=1, replica_groups=mesh['layer'=32,'space'=16] {'space'}, dimensions={0} | all-to-all | bytes 1048576 | tf_op jit(solution)/shard_map/all_to_all | solution.py:336
  46.3 3.2 %shard_map.67 = f32[1024,128]{1,0:T(8,128)S(1)} custom-call(f32[1024,128]{1,0:T(8,128)S(1)} %bitcast.30, bf16[4,1152,128]{2,1,0:T(8,128)(2,1)S(1)} %copy-done.1), custom_call_target="tpu_custom_call" | custom-call | tf_op jit(solution)/shard_map/pallas_call | solution.py:289
  50.3 1.8 slice.38
  52.2 1.9 collective-permute-start.1
  54.3 10.4 %collective-permute-done.1 = f16[1024,128]{1,0:T(8,128)(2,1)S(1)} collective-permute-done((f16[1024,128]{1,0:T(8,128)(2,1)S(1)}, f16[1024,128]{1,0:T(8,128)(2,1)S(1)}, u32[]{:S(2)}, u32[]{:S(2)}) %collective-permute-start.1) | collective-permute-done | bytes 262176 | tf_op jit(solution)/shard_map/ppermute | solution.py:318
  65.8 4.6 %shard_map.68 = (bf16[1024,128]{1,0:T(8,128)(2,1)S(1)}, f32[1024,128]{1,0:T(8,128)S(1)}, f32[1024,128]{1,0:T(8,128)S(1)}) custom-call(s32[4]{0:T(128)S(1)} %pad_add_fusion.place, f32[1024,128]{1,0:T(8,128)S(1)} %bitcast.31, f32[1024,128]{1,0:T(8,128)S(1)} %convert_element_type.80.received, bf16[4,1152,128]{2,1,0:T(8,128)(2,1)S(1)} %copy-done.1, ...), custom_call_target="tpu_custom_call" | custom-call | tf_op jit(solution)/shard_map/pallas_call | solution.py:289
  71.9 4.1 %collective-permute-start.3 = (f16[1024,128]{1,0:T(8,128)(2,1)}, f16[1024,128]{1,0:T(8,128)(2,1)}, u32[]{:S(2)}, u32[]{:S(2)}) collective-permute-start(f16[1024,128]{1,0:T(8,128)(2,1)} %convert_element_type.83), channel_id=1, source_target_pairs={{0,48},{16,32},{32,16},{48,0},{64,112},{80,96},{96,80},{112,64},{1... | collective-permute-start | bytes 786440 | tf_op jit(solution)/shard_map/ppermute | solution.py:312
  76.7 1.9 collective-permute-start.2
  78.6 5.4 %collective-permute-done.3 = f16[1024,128]{1,0:T(8,128)(2,1)} collective-permute-done((f16[1024,128]{1,0:T(8,128)(2,1)}, f16[1024,128]{1,0:T(8,128)(2,1)}, u32[]{:S(2)}, u32[]{:S(2)}) %collective-permute-start.3) | collective-permute-done | bytes 262176 | tf_op jit(solution)/shard_map/ppermute | solution.py:312
  85.0 2.1 %collective-permute-done.2 = f16[1024,128]{1,0:T(8,128)(2,1)} collective-permute-done((f16[1024,128]{1,0:T(8,128)(2,1)}, f16[1024,128]{1,0:T(8,128)(2,1)}, u32[]{:S(2)}, u32[]{:S(2)}) %collective-permute-start.2) | collective-permute-done | bytes 262176 | tf_op jit(solution)/shard_map/ppermute | solution.py:312
  88.1 1.4 shard_map.69
  89.6 2.4 %collective-permute-start.4 = (f16[1024,128]{1,0:T(8,128)(2,1)S(1)}, f16[1024,128]{1,0:T(8,128)(2,1)S(1)}, u32[]{:S(2)}, u32[]{:S(2)}) collective-permute-start(f16[1024,128]{1,0:T(8,128)(2,1)S(1)} %convert_element_type.85), channel_id=1, source_target_pairs={{0,16},{16,0},{32,48},{48,32},{64,80},{80,64},{96,112},{112,96},{1... | collective-permute-start | bytes 786440 | tf_op jit(solution)/shard_map/ppermute | solution.py:312
  92.0 2.4 %collective-permute-start.5 = (f16[1024,128]{1,0:T(8,128)(2,1)S(1)}, f16[1024,128]{1,0:T(8,128)(2,1)S(1)}, u32[]{:S(2)}, u32[]{:S(2)}) collective-permute-start(f16[1024,128]{1,0:T(8,128)(2,1)S(1)} %convert_element_type.87), channel_id=1, source_target_pairs={{0,48},{16,32},{32,16},{48,0},{64,112},{80,96},{96,80},{112,64},{1... | collective-permute-start | bytes 786440 | tf_op jit(solution)/shard_map/ppermute | solution.py:312
  94.4 6.1 %collective-permute-done.4 = f16[1024,128]{1,0:T(8,128)(2,1)S(1)} collective-permute-done((f16[1024,128]{1,0:T(8,128)(2,1)S(1)}, f16[1024,128]{1,0:T(8,128)(2,1)S(1)}, u32[]{:S(2)}, u32[]{:S(2)}) %collective-permute-start.4) | collective-permute-done | bytes 262176 | tf_op jit(solution)/shard_map/ppermute | solution.py:312
  100.6 3.6 %collective-permute-done.5 = f16[1024,128]{1,0:T(8,128)(2,1)S(1)} collective-permute-done((f16[1024,128]{1,0:T(8,128)(2,1)S(1)}, f16[1024,128]{1,0:T(8,128)(2,1)S(1)}, u32[]{:S(2)}, u32[]{:S(2)}) %collective-permute-start.5) | collective-permute-done | bytes 262176 | tf_op jit(solution)/shard_map/ppermute | solution.py:312
  104.2 1.5 shard_map.70
  105.8 1.9 collective-permute-start.8
  107.7 6.0 %collective-permute-start.6 = (f16[1024,128]{1,0:T(8,128)(2,1)S(1)}, f16[1024,128]{1,0:T(8,128)(2,1)S(1)}, u32[]{:S(2)}, u32[]{:S(2)}) collective-permute-start(f16[1024,128]{1,0:T(8,128)(2,1)S(1)} %convert_element_type.89), channel_id=1, source_target_pairs={{0,64},{16,80},{32,96},{48,112},{64,128},{80,144},{96,160},{112,17... | collective-permute-start | bytes 786440 | tf_op jit(solution)/shard_map/ppermute | solution.py:372
  113.7 4.6 %collective-permute-done.8 = f16[1024,128]{1,0:T(8,128)(2,1)S(1)} collective-permute-done((f16[1024,128]{1,0:T(8,128)(2,1)S(1)}, f16[1024,128]{1,0:T(8,128)(2,1)S(1)}, u32[]{:S(2)}, u32[]{:S(2)}) %collective-permute-start.8) | collective-permute-done | bytes 262176 | tf_op jit(solution)/shard_map/ppermute | solution.py:374
  118.3 1.9 collective-permute-start.9
  120.2 5.1 %collective-permute-start.7 = (f16[1024,128]{1,0:T(8,128)(2,1)S(1)}, f16[1024,128]{1,0:T(8,128)(2,1)S(1)}, u32[]{:S(2)}, u32[]{:S(2)}) collective-permute-start(f16[1024,128]{1,0:T(8,128)(2,1)S(1)} %collective-permute-done.6), channel_id=1, source_target_pairs={{0,64},{16,80},{32,96},{48,112},{64,128},{80,144},{96,160},{112,17... | collective-permute-start | bytes 786440 | tf_op jit(solution)/shard_map/ppermute | solution.py:372
  127.0 2.2 %collective-permute-done.9 = f16[1024,128]{1,0:T(8,128)(2,1)S(1)} collective-permute-done((f16[1024,128]{1,0:T(8,128)(2,1)S(1)}, f16[1024,128]{1,0:T(8,128)(2,1)S(1)}, u32[]{:S(2)}, u32[]{:S(2)}) %collective-permute-start.9) | collective-permute-done | bytes 262176 | tf_op jit(solution)/shard_map/ppermute | solution.py:374
  130.4 5.6 %collective-permute-start.10 = (f16[1024,128]{1,0:T(8,128)(2,1)S(1)}, f16[1024,128]{1,0:T(8,128)(2,1)S(1)}, u32[]{:S(2)}, u32[]{:S(2)}) collective-permute-start(f16[1024,128]{1,0:T(8,128)(2,1)S(1)} %collective-permute-done.7), channel_id=1, source_target_pairs={{0,64},{16,80},{32,96},{48,112},{64,128},{80,144},{96,160},{112,17... | collective-permute-start | bytes 786440 | tf_op jit(solution)/shard_map/ppermute | solution.py:372
  136.0 1.9 collective-permute-start.11
  140.2 5.3 %collective-permute-done.11 = f16[1024,128]{1,0:T(8,128)(2,1)S(1)} collective-permute-done((f16[1024,128]{1,0:T(8,128)(2,1)S(1)}, f16[1024,128]{1,0:T(8,128)(2,1)S(1)}, u32[]{:S(2)}, u32[]{:S(2)}) %collective-permute-start.11) | collective-permute-done | bytes 262176 | tf_op jit(solution)/shard_map/ppermute | solution.py:374
  145.5 1.9 collective-permute-start.12
  151.1 2.7 %collective-permute-done.12 = f16[1024,128]{1,0:T(8,128)(2,1)S(1)} collective-permute-done((f16[1024,128]{1,0:T(8,128)(2,1)S(1)}, f16[1024,128]{1,0:T(8,128)(2,1)S(1)}, u32[]{:S(2)}, u32[]{:S(2)}) %collective-permute-start.12) | collective-permute-done | bytes 262176 | tf_op jit(solution)/shard_map/ppermute | solution.py:372
  154.6 16.8 %shard_map.71 = bf16[4,512,128]{2,1,0:T(8,128)(2,1)} custom-call(s32[4]{0:T(128)} %copy-done.7, f32[1024,128]{1,0:T(8,128)} %copy-done.4, f32[1024,128]{1,0:T(8,128)} %convert_element_type.90.refs_1_, f32[1024,128]{1,0:T(8,128)} %convert_element_type.92.refs_2_, f32[1024,128]{1,0:T(8,128)} %convert_element_type.94.refs_3_, ...), custom_call_target="tpu_custom_call" | custom-call | tf_op jit(solution)/shard_map/pallas_call | solution.py:289
  171.4 12.3 %all_to_all.11 = bf16[4,512,128]{2,1,0:T(8,128)(2,1)S(1)} all-to-all(bf16[4,512,128]{2,1,0:T(8,128)(2,1)} %shard_map.71), channel_id=1, replica_groups={{0,1,2,3},{4,5,6,7},{8,9,10,11},{12,13,14,15},{16,17,18,19},{20,21,22,2..., dimensions={0} | all-to-all | bytes 1048576 | tf_op jit(solution)/shard_map/all_to_all | solution.py:401
  (67 shorter events, 21.9 us)
Async XLA Ops:
  7.2 11.1 %copy-start.9 = (f32[4,2,32,128]{3,2,1,0:T(8,128)S(1)}, f32[4,2,32,128]{3,2,1,0:T(8,128)}, u32[]{:S(2)}) copy-start(f32[4,2,32,128]{3,2,1,0:T(8,128)} %param.4) | copy-start | bytes 393220
  7.2 43.1 %all-gather.7.cloned.1.call-start = ((), (), s32[]{:S(2)}) async-start(), calls=%async_computation.2 | async-start | bytes 1474560 | tf_op jit(solution)/shard_map/all_gather | solution.py:333
  9.9 143.9 %all-gather.9.cloned.1.call-start = ((), (), s32[]{:S(2)}) async-start(), calls=%async_computation.3 | async-start | bytes 2654208 | tf_op jit(solution)/shard_map/all_gather | solution.py:350
  9.9 8.3 %collective-permute-start = (f16[4,2,32,128]{3,2,1,0:T(8,128)(2,1)S(1)}, f16[4,2,32,128]{3,2,1,0:T(8,128)(2,1)S(1)}, u32[]{:S(2)}, u32[]{:S(2)}) collective-permute-start(f16[4,2,32,128]{3,2,1,0:T(8,128)(2,1)S(1)} %convert_bitcast_fusion.1), channel_id=1, source_target_pairs={{0,16},{16,32},{32,48},{48,64},{64,80},{80,96},{96,112},{112,128},... | collective-permute-start | bytes 196616 | tf_op jit(solution)/shard_map/ppermute | solution.py:318
  44.8 1.5 copy-start.1
  49.5 0.8 copy-start.2
  50.3 14.4 %copy-start = (bf16[4608,128]{1,0:T(8,128)(2,1)S(1)}, bf16[4608,128]{1,0:T(8,128)(2,1)}, u32[]{:S(2)}) copy-start(bf16[4608,128]{1,0:T(8,128)(2,1)} %all-gather.7.cloned.1.call-done) | copy-start | bytes 3538948
  52.1 102.5 %all-gather.11.cloned.1.call-start = ((), (), s32[]{:S(2)}) async-start(), calls=%async_computation.4 | async-start | bytes 1310720 | tf_op jit(solution)/shard_map/all_gather | solution.py:357
  52.2 12.5 %collective-permute-start.1 = (f16[1024,128]{1,0:T(8,128)(2,1)S(1)}, f16[1024,128]{1,0:T(8,128)(2,1)S(1)}, u32[]{:S(2)}, u32[]{:S(2)}) collective-permute-start(f16[1024,128]{1,0:T(8,128)(2,1)S(1)} %convert_element_type.79), channel_id=1, source_target_pairs={{0,16},{16,32},{32,48},{48,64},{64,80},{80,96},{96,112},{112,128},... | collective-permute-start | bytes 786440 | tf_op jit(solution)/shard_map/ppermute | solution.py:318
  54.2 50.0 %copy-start.7 = (s32[4]{0:T(128)}, s32[4]{0:T(128)S(1)}, u32[]{:S(2)}) copy-start(s32[4]{0:T(128)S(1)} %pad_add_fusion.place) | copy-start | bytes 52
  64.7 1.0 copy-start.3
  70.4 0.7 copy-start.6
  71.9 12.2 %collective-permute-start.3 = (f16[1024,128]{1,0:T(8,128)(2,1)}, f16[1024,128]{1,0:T(8,128)(2,1)}, u32[]{:S(2)}, u32[]{:S(2)}) collective-permute-start(f16[1024,128]{1,0:T(8,128)(2,1)} %convert_element_type.83), channel_id=1, source_target_pairs={{0,48},{16,32},{32,16},{48,0},{64,112},{80,96},{96,80},{112,64},{1... | collective-permute-start | bytes 786440 | tf_op jit(solution)/shard_map/ppermute | solution.py:312
  76.7 10.4 %collective-permute-start.2 = (f16[1024,128]{1,0:T(8,128)(2,1)}, f16[1024,128]{1,0:T(8,128)(2,1)}, u32[]{:S(2)}, u32[]{:S(2)}) collective-permute-start(f16[1024,128]{1,0:T(8,128)(2,1)} %convert_element_type.81), channel_id=1, source_target_pairs={{0,16},{16,0},{32,48},{48,32},{64,80},{80,64},{96,112},{112,96},{1... | collective-permute-start | bytes 786440 | tf_op jit(solution)/shard_map/ppermute | solution.py:312
  89.6 11.0 %collective-permute-start.4 = (f16[1024,128]{1,0:T(8,128)(2,1)S(1)}, f16[1024,128]{1,0:T(8,128)(2,1)S(1)}, u32[]{:S(2)}, u32[]{:S(2)}) collective-permute-start(f16[1024,128]{1,0:T(8,128)(2,1)S(1)} %convert_element_type.85), channel_id=1, source_target_pairs={{0,16},{16,0},{32,48},{48,32},{64,80},{80,64},{96,112},{112,96},{1... | collective-permute-start | bytes 786440 | tf_op jit(solution)/shard_map/ppermute | solution.py:312
  92.0 12.1 %collective-permute-start.5 = (f16[1024,128]{1,0:T(8,128)(2,1)S(1)}, f16[1024,128]{1,0:T(8,128)(2,1)S(1)}, u32[]{:S(2)}, u32[]{:S(2)}) collective-permute-start(f16[1024,128]{1,0:T(8,128)(2,1)S(1)} %convert_element_type.87), channel_id=1, source_target_pairs={{0,48},{16,32},{32,16},{48,0},{64,112},{80,96},{96,80},{112,64},{1... | collective-permute-start | bytes 786440 | tf_op jit(solution)/shard_map/ppermute | solution.py:312
  105.7 21.2 %copy-start.4 = (f32[1024,128]{1,0:T(8,128)}, f32[1024,128]{1,0:T(8,128)S(1)}, u32[]{:S(2)}) copy-start(f32[1024,128]{1,0:T(8,128)S(1)} %get-tuple-element.32.refs_0_) | copy-start | bytes 1572868
  105.7 21.2 %copy-start.5 = (f32[1024,128]{1,0:T(8,128)}, f32[1024,128]{1,0:T(8,128)S(1)}, u32[]{:S(2)}) copy-start(f32[1024,128]{1,0:T(8,128)S(1)} %get-tuple-element.47.refs_9_) | copy-start | bytes 1572868
  105.8 12.5 %collective-permute-start.8 = (f16[1024,128]{1,0:T(8,128)(2,1)S(1)}, f16[1024,128]{1,0:T(8,128)(2,1)S(1)}, u32[]{:S(2)}, u32[]{:S(2)}) collective-permute-start(f16[1024,128]{1,0:T(8,128)(2,1)S(1)} %convert_element_type.89), channel_id=1, source_target_pairs={{64,0},{80,16},{96,32},{112,48},{128,64},{144,80},{160,96},{176,11... | collective-permute-start | bytes 786440 | tf_op jit(solution)/shard_map/ppermute | solution.py:374
  107.7 12.5 %collective-permute-start.6 = (f16[1024,128]{1,0:T(8,128)(2,1)S(1)}, f16[1024,128]{1,0:T(8,128)(2,1)S(1)}, u32[]{:S(2)}, u32[]{:S(2)}) collective-permute-start(f16[1024,128]{1,0:T(8,128)(2,1)S(1)} %convert_element_type.89), channel_id=1, source_target_pairs={{0,64},{16,80},{32,96},{48,112},{64,128},{80,144},{96,160},{112,17... | collective-permute-start | bytes 786440 | tf_op jit(solution)/shard_map/ppermute | solution.py:372
  118.3 10.9 %collective-permute-start.9 = (f16[1024,128]{1,0:T(8,128)(2,1)S(1)}, f16[1024,128]{1,0:T(8,128)(2,1)S(1)}, u32[]{:S(2)}, u32[]{:S(2)}) collective-permute-start(f16[1024,128]{1,0:T(8,128)(2,1)S(1)} %collective-permute-done.8), channel_id=1, source_target_pairs={{64,0},{80,16},{96,32},{112,48},{128,64},{144,80},{160,96},{176,11... | collective-permute-start | bytes 786440 | tf_op jit(solution)/shard_map/ppermute | solution.py:374
  120.2 10.2 %collective-permute-start.7 = (f16[1024,128]{1,0:T(8,128)(2,1)S(1)}, f16[1024,128]{1,0:T(8,128)(2,1)S(1)}, u32[]{:S(2)}, u32[]{:S(2)}) collective-permute-start(f16[1024,128]{1,0:T(8,128)(2,1)S(1)} %collective-permute-done.6), channel_id=1, source_target_pairs={{0,64},{16,80},{32,96},{48,112},{64,128},{80,144},{96,160},{112,17... | collective-permute-start | bytes 786440 | tf_op jit(solution)/shard_map/ppermute | solution.py:372
  130.4 9.7 %collective-permute-start.10 = (f16[1024,128]{1,0:T(8,128)(2,1)S(1)}, f16[1024,128]{1,0:T(8,128)(2,1)S(1)}, u32[]{:S(2)}, u32[]{:S(2)}) collective-permute-start(f16[1024,128]{1,0:T(8,128)(2,1)S(1)} %collective-permute-done.7), channel_id=1, source_target_pairs={{0,64},{16,80},{32,96},{48,112},{64,128},{80,144},{96,160},{112,17... | collective-permute-start | bytes 786440 | tf_op jit(solution)/shard_map/ppermute | solution.py:372
  136.0 9.5 %collective-permute-start.11 = (f16[1024,128]{1,0:T(8,128)(2,1)S(1)}, f16[1024,128]{1,0:T(8,128)(2,1)S(1)}, u32[]{:S(2)}, u32[]{:S(2)}) collective-permute-start(f16[1024,128]{1,0:T(8,128)(2,1)S(1)} %collective-permute-done.9), channel_id=1, source_target_pairs={{64,0},{80,16},{96,32},{112,48},{128,64},{144,80},{160,96},{176,11... | collective-permute-start | bytes 786440 | tf_op jit(solution)/shard_map/ppermute | solution.py:374
  145.5 8.3 %collective-permute-start.12 = (f16[1024,128]{1,0:T(8,128)(2,1)S(1)}, f16[1024,128]{1,0:T(8,128)(2,1)S(1)}, u32[]{:S(2)}, u32[]{:S(2)}) collective-permute-start(f16[1024,128]{1,0:T(8,128)(2,1)S(1)} %collective-permute-done.10), channel_id=1, source_target_pairs={{0,64},{16,80},{32,96},{48,112},{64,128},{80,144},{96,160},{112,17... | collective-permute-start | bytes 786440 | tf_op jit(solution)/shard_map/ppermute | solution.py:372
  183.7 0.9 copy-start.8
Sparse Core Ops, SparseCore 0:
  10.1 34.0 all-gather.6
  52.2 40.3 all-gather.8
  94.7 28.9 all-gather.10

commit v8 on v6

--- a/solution.py
+++ b/solution.py
@@ -369,19 +369,21 @@
     )
     up = [(i, (i + 4) % sections) for i in range(sections)]
     down = [(j, i) for i, j in up]
-    ups, downs, widened = [defect_two.astype(SENT)], [defect_two.astype(SENT)], {}
-    for turn in range(4):
-        moved = [lax.ppermute(ups[-1], "layer", up)]
-        if turn < 3:
-            moved.append(lax.ppermute(downs[-1], "layer", down))
-        if turn:
-            ready = [ups[-1].astype(FULL), downs[-1].astype(FULL)]
-            moved, (widened[turn], widened[8 - turn]) = lax.optimization_barrier((moved, ready))
-        ups.append(moved[0])
-        if turn < 3:
-            downs.append(moved[1])
-    widened[4], coarse = lax.optimization_barrier((ups[-1], coarse))
-    slots = [defect_two] + [widened[distance].astype(FULL) for distance in range(1, 8)]
+    def ring(route, turns):
+        block, wide_blocks = lax.ppermute(defect_two.astype(SENT), "layer", route), []
+        for _ in range(turns - 1):
+            moved, ready = lax.optimization_barrier((lax.ppermute(block, "layer", route), block.astype(FULL)))
+            wide_blocks.append(ready)
+            block = moved
+        return block, wide_blocks
+
+    farthest, ups = ring(up, 4)
+    last_down, downs = ring(down, 3)
+    farthest, last_down = lax.optimization_barrier((farthest, last_down.astype(FULL)))
+    downs.append(last_down)
+
+    farthest, coarse = lax.optimization_barrier((farthest, coarse))
+    slots = [defect_two, *ups, farthest.astype(FULL), *downs[::-1]]
     stored = (coarse, base, defects, leading, weights, flipped, adjoint_whole)
     parts = call(
         final_kernel,

time: 193 us -> 189 us (0.979)
  the two profiles are of different devices: /device:TPU:24 before, /device:TPU:32 now
where the time goes in v8:
time: 189 us; the launch traced here: 188 us
  waiting for transfers between devices  44.4 us (23%)
  starting transfers between devices  38.9 us (21%)
  blocking collectives  38.5 us (20%)
  Pallas kernels  28.4 us (15%)
  between operations  14.1 us (7%)
  other arithmetic  13.2 us (7%)
  local copies, waits for them, and re-layouts  10.3 us (5%)
    pallas_call x5, Pallas kernels, call(): pl.pallas_call(body, out_shape=outs, in_specs=in_specs, out_specs=jax.tre...  28.4 us
    all_to_all x1, blocking collectives, local(): lax.all_to_all(jnp.tile(both, (tiles // 4, 1, 1, 1, 1)), 'space', 0, 0, t...  26.2 us
    ppermute x2, waiting for transfers between devices, shift(): return lax.ppermute(block.astype(SENT), 'layer', route).astype(block.dtype)  17.7 us
    ppermute x5, starting transfers between devices, ring(): lax.ppermute(block, 'layer', route)  16 us
    ppermute x4, waiting for transfers between devices, swap(): lax.ppermute(block.astype(SENT), 'layer', [(i, i ^ distance) for i in ran...  15.5 us
    all_to_all x1, blocking collectives, local(): lax.all_to_all(parts, 'space', 0, 0, axis_index_groups=row_groups, tiled=...  12.3 us
    ppermute x4, starting transfers between devices, swap(): lax.ppermute(block.astype(SENT), 'layer', [(i, i ^ distance) for i in ran...  10.4 us
    ppermute x2, starting transfers between devices, ring(): lax.ppermute(defect_two.astype(SENT), 'layer', route)  7.05 us
  transfers between devices with their start and end apart: 16, of which 10 were waited for; matrix products, arithmetic and copies ran while one was open for 7% of the time, Pallas kernels for 6%

profile of v8, /device:TPU:32, one launch (start us, length us, event | category | flops | bytes accessed | tf_op | source)
XLA Modules:
  0.0 187.8 jit_solution(4540137480962561915)
XLA Ops:
  8.2 1.7 slice_bitcast_fusion
  9.9 3.4 %collective-permute-start = (f16[4,2,32,128]{3,2,1,0:T(8,128)(2,1)S(1)}, f16[4,2,32,128]{3,2,1,0:T(8,128)(2,1)S(1)}, u32[]{:S(2)}, u32[]{:S(2)}) collective-permute-start(f16[4,2,32,128]{3,2,1,0:T(8,128)(2,1)S(1)} %convert_bitcast_fusion.1), channel_id=1, source_target_pairs={{0,16},{16,32},{32,48},{48,64},{64,80},{80,96},{96,112},{112,128},... | collective-permute-start | bytes 196616 | tf_op jit(solution)/shard_map/ppermute | solution.py:320
  14.3 5.1 %collective-permute-done = f16[4,2,32,128]{3,2,1,0:T(8,128)(2,1)S(1)} collective-permute-done((f16[4,2,32,128]{3,2,1,0:T(8,128)(2,1)S(1)}, f16[4,2,32,128]{3,2,1,0:T(8,128)(2,1)S(1)}, u32[]{:S(2)}, u32[]{:S(2)}) %collective-permute-start) | collective-permute-done | bytes 65568 | tf_op jit(solution)/shard_map/ppermute | solution.py:320
  19.7 26.2 %all_to_all.10 = f16[16,2,2,32,128]{4,3,2,1,0:T(8,128)(2,1)S(1)} all-to-all(f16[16,2,2,32,128]{4,3,2,1,0:T(8,128)(2,1)S(1)} %bitcast.34), channel_id=1, replica_groups=mesh['layer'=32,'space'=16] {'space'}, dimensions={0} | all-to-all | bytes 1048576 | tf_op jit(solution)/shard_map/all_to_all | solution.py:338
  47.5 3.2 %shard_map.67 = f32[1024,128]{1,0:T(8,128)S(1)} custom-call(f32[1024,128]{1,0:T(8,128)S(1)} %bitcast.30, bf16[4,1152,128]{2,1,0:T(8,128)(2,1)S(1)} %copy-done.1), custom_call_target="tpu_custom_call" | custom-call | tf_op jit(solution)/shard_map/pallas_call | solution.py:291
  51.5 1.8 slice.38
  53.4 1.9 %collective-permute-start.1 = (f16[1024,128]{1,0:T(8,128)(2,1)S(1)}, f16[1024,128]{1,0:T(8,128)(2,1)S(1)}, u32[]{:S(2)}, u32[]{:S(2)}) collective-permute-start(f16[1024,128]{1,0:T(8,128)(2,1)S(1)} %convert_element_type.79), channel_id=1, source_target_pairs={{0,16},{16,32},{32,48},{48,64},{64,80},{80,96},{96,112},{112,128},... | collective-permute-start | bytes 786440 | tf_op jit(solution)/shard_map/ppermute | solution.py:320
  55.5 12.5 %collective-permute-done.1 = f16[1024,128]{1,0:T(8,128)(2,1)S(1)} collective-permute-done((f16[1024,128]{1,0:T(8,128)(2,1)S(1)}, f16[1024,128]{1,0:T(8,128)(2,1)S(1)}, u32[]{:S(2)}, u32[]{:S(2)}) %collective-permute-start.1) | collective-permute-done | bytes 262176 | tf_op jit(solution)/shard_map/ppermute | solution.py:320
  68.1 1.0 copy-done.3
  69.1 4.6 %shard_map.68 = (bf16[1024,128]{1,0:T(8,128)(2,1)S(1)}, f32[1024,128]{1,0:T(8,128)S(1)}, f32[1024,128]{1,0:T(8,128)S(1)}) custom-call(s32[4]{0:T(128)S(1)} %pad_add_fusion.place, f32[1024,128]{1,0:T(8,128)S(1)} %bitcast.31, f32[1024,128]{1,0:T(8,128)S(1)} %convert_element_type.80.received, bf16[4,1152,128]{2,1,0:T(8,128)(2,1)S(1)} %copy-done.1, ...), custom_call_target="tpu_custom_call" | custom-call | tf_op jit(solution)/shard_map/pallas_call | solution.py:291
  75.2 1.9 %collective-permute-start.3 = (f16[1024,128]{1,0:T(8,128)(2,1)}, f16[1024,128]{1,0:T(8,128)(2,1)}, u32[]{:S(2)}, u32[]{:S(2)}) collective-permute-start(f16[1024,128]{1,0:T(8,128)(2,1)} %convert_element_type.83), channel_id=1, source_target_pairs={{0,48},{16,32},{32,16},{48,0},{64,112},{80,96},{96,80},{112,64},{1... | collective-permute-start | bytes 786440 | tf_op jit(solution)/shard_map/ppermute | solution.py:314
  77.8 1.9 %collective-permute-start.2 = (f16[1024,128]{1,0:T(8,128)(2,1)}, f16[1024,128]{1,0:T(8,128)(2,1)}, u32[]{:S(2)}, u32[]{:S(2)}) collective-permute-start(f16[1024,128]{1,0:T(8,128)(2,1)} %convert_element_type.81), channel_id=1, source_target_pairs={{0,16},{16,0},{32,48},{48,32},{64,80},{80,64},{96,112},{112,96},{1... | collective-permute-start | bytes 786440 | tf_op jit(solution)/shard_map/ppermute | solution.py:314
  79.8 7.1 %collective-permute-done.3 = f16[1024,128]{1,0:T(8,128)(2,1)} collective-permute-done((f16[1024,128]{1,0:T(8,128)(2,1)}, f16[1024,128]{1,0:T(8,128)(2,1)}, u32[]{:S(2)}, u32[]{:S(2)}) %collective-permute-start.3) | collective-permute-done | bytes 262176 | tf_op jit(solution)/shard_map/ppermute | solution.py:314
  89.3 1.4 shard_map.69
  90.7 2.4 %collective-permute-start.4 = (f16[1024,128]{1,0:T(8,128)(2,1)S(1)}, f16[1024,128]{1,0:T(8,128)(2,1)S(1)}, u32[]{:S(2)}, u32[]{:S(2)}) collective-permute-start(f16[1024,128]{1,0:T(8,128)(2,1)S(1)} %convert_element_type.85), channel_id=1, source_target_pairs={{0,16},{16,0},{32,48},{48,32},{64,80},{80,64},{96,112},{112,96},{1... | collective-permute-start | bytes 786440 | tf_op jit(solution)/shard_map/ppermute | solution.py:314
  93.2 4.2 %collective-permute-start.5 = (f16[1024,128]{1,0:T(8,128)(2,1)S(1)}, f16[1024,128]{1,0:T(8,128)(2,1)S(1)}, u32[]{:S(2)}, u32[]{:S(2)}) collective-permute-start(f16[1024,128]{1,0:T(8,128)(2,1)S(1)} %convert_element_type.87), channel_id=1, source_target_pairs={{0,48},{16,32},{32,16},{48,0},{64,112},{80,96},{96,80},{112,64},{1... | collective-permute-start | bytes 786440 | tf_op jit(solution)/shard_map/ppermute | solution.py:314
  97.4 4.3 %collective-permute-done.4 = f16[1024,128]{1,0:T(8,128)(2,1)S(1)} collective-permute-done((f16[1024,128]{1,0:T(8,128)(2,1)S(1)}, f16[1024,128]{1,0:T(8,128)(2,1)S(1)}, u32[]{:S(2)}, u32[]{:S(2)}) %collective-permute-start.4) | collective-permute-done | bytes 262176 | tf_op jit(solution)/shard_map/ppermute | solution.py:314
  101.8 3.7 %collective-permute-done.5 = f16[1024,128]{1,0:T(8,128)(2,1)S(1)} collective-permute-done((f16[1024,128]{1,0:T(8,128)(2,1)S(1)}, f16[1024,128]{1,0:T(8,128)(2,1)S(1)}, u32[]{:S(2)}, u32[]{:S(2)}) %collective-permute-start.5) | collective-permute-done | bytes 262176 | tf_op jit(solution)/shard_map/ppermute | solution.py:314
  105.5 1.5 shard_map.70
  107.1 1.9 %collective-permute-start.6 = (f16[1024,128]{1,0:T(8,128)(2,1)S(1)}, f16[1024,128]{1,0:T(8,128)(2,1)S(1)}, u32[]{:S(2)}, u32[]{:S(2)}) collective-permute-start(f16[1024,128]{1,0:T(8,128)(2,1)S(1)} %convert_element_type.89), channel_id=1, source_target_pairs={{0,64},{16,80},{32,96},{48,112},{64,128},{80,144},{96,160},{112,17... | collective-permute-start | bytes 786440 | tf_op jit(solution)/shard_map/ppermute | solution.py:373
  109.0 5.1 %collective-permute-start.10 = (f16[1024,128]{1,0:T(8,128)(2,1)S(1)}, f16[1024,128]{1,0:T(8,128)(2,1)S(1)}, u32[]{:S(2)}, u32[]{:S(2)}) collective-permute-start(f16[1024,128]{1,0:T(8,128)(2,1)S(1)} %convert_element_type.89), channel_id=1, source_target_pairs={{64,0},{80,16},{96,32},{112,48},{128,64},{144,80},{160,96},{176,11... | collective-permute-start | bytes 786440 | tf_op jit(solution)/shard_map/ppermute | solution.py:373
  114.1 4.3 %collective-permute-done.6 = f16[1024,128]{1,0:T(8,128)(2,1)S(1)} collective-permute-done((f16[1024,128]{1,0:T(8,128)(2,1)S(1)}, f16[1024,128]{1,0:T(8,128)(2,1)S(1)}, u32[]{:S(2)}, u32[]{:S(2)}) %collective-permute-start.6) | collective-permute-done | bytes 262176 | tf_op jit(solution)/shard_map/ppermute | solution.py:373
  118.4 1.9 %collective-permute-start.7 = (f16[1024,128]{1,0:T(8,128)(2,1)S(1)}, f16[1024,128]{1,0:T(8,128)(2,1)S(1)}, u32[]{:S(2)}, u32[]{:S(2)}) collective-permute-start(f16[1024,128]{1,0:T(8,128)(2,1)S(1)} %collective-permute-done.6), channel_id=1, source_target_pairs={{0,64},{16,80},{32,96},{48,112},{64,128},{80,144},{96,160},{112,17... | collective-permute-start | bytes 786440 | tf_op jit(solution)/shard_map/ppermute | solution.py:375
  121.2 5.1 %collective-permute-start.11 = (f16[1024,128]{1,0:T(8,128)(2,1)S(1)}, f16[1024,128]{1,0:T(8,128)(2,1)S(1)}, u32[]{:S(2)}, u32[]{:S(2)}) collective-permute-start(f16[1024,128]{1,0:T(8,128)(2,1)S(1)} %collective-permute-done.10), channel_id=1, source_target_pairs={{64,0},{80,16},{96,32},{112,48},{128,64},{144,80},{160,96},{176,11... | collective-permute-start | bytes 786440 | tf_op jit(solution)/shard_map/ppermute | solution.py:375
  126.3 2.8 %collective-permute-done.7 = f16[1024,128]{1,0:T(8,128)(2,1)S(1)} collective-permute-done((f16[1024,128]{1,0:T(8,128)(2,1)S(1)}, f16[1024,128]{1,0:T(8,128)(2,1)S(1)}, u32[]{:S(2)}, u32[]{:S(2)}) %collective-permute-start.7) | collective-permute-done | bytes 262176 | tf_op jit(solution)/shard_map/ppermute | solution.py:375
  129.1 1.9 %collective-permute-start.8 = (f16[1024,128]{1,0:T(8,128)(2,1)S(1)}, f16[1024,128]{1,0:T(8,128)(2,1)S(1)}, u32[]{:S(2)}, u32[]{:S(2)}) collective-permute-start(f16[1024,128]{1,0:T(8,128)(2,1)S(1)} %collective-permute-done.7), channel_id=1, source_target_pairs={{0,64},{16,80},{32,96},{48,112},{64,128},{80,144},{96,160},{112,17... | collective-permute-start | bytes 786440 | tf_op jit(solution)/shard_map/ppermute | solution.py:375
  132.7 5.1 %collective-permute-start.12 = (f16[1024,128]{1,0:T(8,128)(2,1)S(1)}, f16[1024,128]{1,0:T(8,128)(2,1)S(1)}, u32[]{:S(2)}, u32[]{:S(2)}) collective-permute-start(f16[1024,128]{1,0:T(8,128)(2,1)S(1)} %collective-permute-done.11), channel_id=1, source_target_pairs={{64,0},{80,16},{96,32},{112,48},{128,64},{144,80},{160,96},{176,11... | collective-permute-start | bytes 786440 | tf_op jit(solution)/shard_map/ppermute | solution.py:375
  138.8 1.9 %collective-permute-start.9 = (f16[1024,128]{1,0:T(8,128)(2,1)S(1)}, f16[1024,128]{1,0:T(8,128)(2,1)S(1)}, u32[]{:S(2)}, u32[]{:S(2)}) collective-permute-start(f16[1024,128]{1,0:T(8,128)(2,1)S(1)} %collective-permute-done.8), channel_id=1, source_target_pairs={{0,64},{16,80},{32,96},{48,112},{64,128},{80,144},{96,160},{112,17... | collective-permute-start | bytes 786440 | tf_op jit(solution)/shard_map/ppermute | solution.py:375
  141.4 1.1 rev.3
  145.2 3.1 %collective-permute-done.9 = f16[1024,128]{1,0:T(8,128)(2,1)S(1)} collective-permute-done((f16[1024,128]{1,0:T(8,128)(2,1)S(1)}, f16[1024,128]{1,0:T(8,128)(2,1)S(1)}, u32[]{:S(2)}, u32[]{:S(2)}) %collective-permute-start.9) | collective-permute-done | bytes 262176 | tf_op jit(solution)/shard_map/ppermute | solution.py:375
  149.1 17.7 %shard_map.71 = bf16[4,512,128]{2,1,0:T(8,128)(2,1)} custom-call(s32[4]{0:T(128)} %copy-done.7, f32[1024,128]{1,0:T(8,128)} %copy-done.4, f32[1024,128]{1,0:T(8,128)} %convert_element_type.90.refs_1_, f32[1024,128]{1,0:T(8,128)} %convert_element_type.91.refs_2_, f32[1024,128]{1,0:T(8,128)} %convert_element_type.92.refs_3_, ...), custom_call_target="tpu_custom_call" | custom-call | tf_op jit(solution)/shard_map/pallas_call | solution.py:291
  166.7 12.3 %all_to_all.11 = bf16[4,512,128]{2,1,0:T(8,128)(2,1)S(1)} all-to-all(bf16[4,512,128]{2,1,0:T(8,128)(2,1)} %shard_map.71), channel_id=1, replica_groups={{0,1,2,3},{4,5,6,7},{8,9,10,11},{12,13,14,15},{16,17,18,19},{20,21,22,2..., dimensions={0} | all-to-all | bytes 1048576 | tf_op jit(solution)/shard_map/all_to_all | solution.py:405
  (67 shorter events, 19.4 us)
Async XLA Ops:
  7.2 12.3 %copy-start.9 = (f32[4,2,32,128]{3,2,1,0:T(8,128)S(1)}, f32[4,2,32,128]{3,2,1,0:T(8,128)}, u32[]{:S(2)}) copy-start(f32[4,2,32,128]{3,2,1,0:T(8,128)} %param.4) | copy-start | bytes 393220
  7.2 44.3 %all-gather.7.cloned.1.call-start = ((), (), s32[]{:S(2)}) async-start(), calls=%async_computation.2 | async-start | bytes 1474560 | tf_op jit(solution)/shard_map/all_gather | solution.py:335
  9.9 138.3 %all-gather.9.cloned.1.call-start = ((), (), s32[]{:S(2)}) async-start(), calls=%async_computation.3 | async-start | bytes 2654208 | tf_op jit(solution)/shard_map/all_gather | solution.py:352
  9.9 9.5 %collective-permute-start = (f16[4,2,32,128]{3,2,1,0:T(8,128)(2,1)S(1)}, f16[4,2,32,128]{3,2,1,0:T(8,128)(2,1)S(1)}, u32[]{:S(2)}, u32[]{:S(2)}) collective-permute-start(f16[4,2,32,128]{3,2,1,0:T(8,128)(2,1)S(1)} %convert_bitcast_fusion.1), channel_id=1, source_target_pairs={{0,16},{16,32},{32,48},{48,64},{64,80},{80,96},{96,112},{112,128},... | collective-permute-start | bytes 196616 | tf_op jit(solution)/shard_map/ppermute | solution.py:320
  46.0 1.5 copy-start.1
  50.7 0.8 copy-start.2
  51.5 16.5 %copy-start = (bf16[4608,128]{1,0:T(8,128)(2,1)S(1)}, bf16[4608,128]{1,0:T(8,128)(2,1)}, u32[]{:S(2)}) copy-start(bf16[4608,128]{1,0:T(8,128)(2,1)} %all-gather.7.cloned.1.call-done) | copy-start | bytes 3538948
  53.3 95.8 %all-gather.11.cloned.1.call-start = ((), (), s32[]{:S(2)}) async-start(), calls=%async_computation.4 | async-start | bytes 1310720 | tf_op jit(solution)/shard_map/all_gather | solution.py:359
  53.4 14.6 %collective-permute-start.1 = (f16[1024,128]{1,0:T(8,128)(2,1)S(1)}, f16[1024,128]{1,0:T(8,128)(2,1)S(1)}, u32[]{:S(2)}, u32[]{:S(2)}) collective-permute-start(f16[1024,128]{1,0:T(8,128)(2,1)S(1)} %convert_element_type.79), channel_id=1, source_target_pairs={{0,16},{16,32},{32,48},{48,64},{64,80},{80,96},{96,112},{112,128},... | collective-permute-start | bytes 786440 | tf_op jit(solution)/shard_map/ppermute | solution.py:320
  55.5 50.0 %copy-start.7 = (s32[4]{0:T(128)}, s32[4]{0:T(128)S(1)}, u32[]{:S(2)}) copy-start(s32[4]{0:T(128)S(1)} %pad_add_fusion.place) | copy-start | bytes 52
  68.1 1.1 copy-start.3
  73.7 0.7 copy-start.6
  75.2 11.7 %collective-permute-start.3 = (f16[1024,128]{1,0:T(8,128)(2,1)}, f16[1024,128]{1,0:T(8,128)(2,1)}, u32[]{:S(2)}, u32[]{:S(2)}) collective-permute-start(f16[1024,128]{1,0:T(8,128)(2,1)} %convert_element_type.83), channel_id=1, source_target_pairs={{0,48},{16,32},{32,16},{48,0},{64,112},{80,96},{96,80},{112,64},{1... | collective-permute-start | bytes 786440 | tf_op jit(solution)/shard_map/ppermute | solution.py:314
  77.8 10.5 %collective-permute-start.2 = (f16[1024,128]{1,0:T(8,128)(2,1)}, f16[1024,128]{1,0:T(8,128)(2,1)}, u32[]{:S(2)}, u32[]{:S(2)}) collective-permute-start(f16[1024,128]{1,0:T(8,128)(2,1)} %convert_element_type.81), channel_id=1, source_target_pairs={{0,16},{16,0},{32,48},{48,32},{64,80},{80,64},{96,112},{112,96},{1... | collective-permute-start | bytes 786440 | tf_op jit(solution)/shard_map/ppermute | solution.py:314
  90.7 11.0 %collective-permute-start.4 = (f16[1024,128]{1,0:T(8,128)(2,1)S(1)}, f16[1024,128]{1,0:T(8,128)(2,1)S(1)}, u32[]{:S(2)}, u32[]{:S(2)}) collective-permute-start(f16[1024,128]{1,0:T(8,128)(2,1)S(1)} %convert_element_type.85), channel_id=1, source_target_pairs={{0,16},{16,0},{32,48},{48,32},{64,80},{80,64},{96,112},{112,96},{1... | collective-permute-start | bytes 786440 | tf_op jit(solution)/shard_map/ppermute | solution.py:314
  93.2 12.2 %collective-permute-start.5 = (f16[1024,128]{1,0:T(8,128)(2,1)S(1)}, f16[1024,128]{1,0:T(8,128)(2,1)S(1)}, u32[]{:S(2)}, u32[]{:S(2)}) collective-permute-start(f16[1024,128]{1,0:T(8,128)(2,1)S(1)} %convert_element_type.87), channel_id=1, source_target_pairs={{0,48},{16,32},{32,16},{48,0},{64,112},{80,96},{96,80},{112,64},{1... | collective-permute-start | bytes 786440 | tf_op jit(solution)/shard_map/ppermute | solution.py:314
  107.0 24.8 %copy-start.4 = (f32[1024,128]{1,0:T(8,128)}, f32[1024,128]{1,0:T(8,128)S(1)}, u32[]{:S(2)}) copy-start(f32[1024,128]{1,0:T(8,128)S(1)} %get-tuple-element.33.refs_0_) | copy-start | bytes 1572868
  107.0 24.8 %copy-start.5 = (f32[1024,128]{1,0:T(8,128)}, f32[1024,128]{1,0:T(8,128)S(1)}, u32[]{:S(2)}) copy-start(f32[1024,128]{1,0:T(8,128)S(1)} %get-tuple-element.49.refs_9_) | copy-start | bytes 1572868
  107.1 11.4 %collective-permute-start.6 = (f16[1024,128]{1,0:T(8,128)(2,1)S(1)}, f16[1024,128]{1,0:T(8,128)(2,1)S(1)}, u32[]{:S(2)}, u32[]{:S(2)}) collective-permute-start(f16[1024,128]{1,0:T(8,128)(2,1)S(1)} %convert_element_type.89), channel_id=1, source_target_pairs={{0,64},{16,80},{32,96},{48,112},{64,128},{80,144},{96,160},{112,17... | collective-permute-start | bytes 786440 | tf_op jit(solution)/shard_map/ppermute | solution.py:373
  109.0 12.2 %collective-permute-start.10 = (f16[1024,128]{1,0:T(8,128)(2,1)S(1)}, f16[1024,128]{1,0:T(8,128)(2,1)S(1)}, u32[]{:S(2)}, u32[]{:S(2)}) collective-permute-start(f16[1024,128]{1,0:T(8,128)(2,1)S(1)} %convert_element_type.89), channel_id=1, source_target_pairs={{64,0},{80,16},{96,32},{112,48},{128,64},{144,80},{160,96},{176,11... | collective-permute-start | bytes 786440 | tf_op jit(solution)/shard_map/ppermute | solution.py:373
  118.4 10.6 %collective-permute-start.7 = (f16[1024,128]{1,0:T(8,128)(2,1)S(1)}, f16[1024,128]{1,0:T(8,128)(2,1)S(1)}, u32[]{:S(2)}, u32[]{:S(2)}) collective-permute-start(f16[1024,128]{1,0:T(8,128)(2,1)S(1)} %collective-permute-done.6), channel_id=1, source_target_pairs={{0,64},{16,80},{32,96},{48,112},{64,128},{80,144},{96,160},{112,17... | collective-permute-start | bytes 786440 | tf_op jit(solution)/shard_map/ppermute | solution.py:375
  121.2 11.5 %collective-permute-start.11 = (f16[1024,128]{1,0:T(8,128)(2,1)S(1)}, f16[1024,128]{1,0:T(8,128)(2,1)S(1)}, u32[]{:S(2)}, u32[]{:S(2)}) collective-permute-start(f16[1024,128]{1,0:T(8,128)(2,1)S(1)} %collective-permute-done.10), channel_id=1, source_target_pairs={{64,0},{80,16},{96,32},{112,48},{128,64},{144,80},{160,96},{176,11... | collective-permute-start | bytes 786440 | tf_op jit(solution)/shard_map/ppermute | solution.py:375
  129.1 9.7 %collective-permute-start.8 = (f16[1024,128]{1,0:T(8,128)(2,1)S(1)}, f16[1024,128]{1,0:T(8,128)(2,1)S(1)}, u32[]{:S(2)}, u32[]{:S(2)}) collective-permute-start(f16[1024,128]{1,0:T(8,128)(2,1)S(1)} %collective-permute-done.7), channel_id=1, source_target_pairs={{0,64},{16,80},{32,96},{48,112},{64,128},{80,144},{96,160},{112,17... | collective-permute-start | bytes 786440 | tf_op jit(solution)/shard_map/ppermute | solution.py:375
  132.7 11.6 %collective-permute-start.12 = (f16[1024,128]{1,0:T(8,128)(2,1)S(1)}, f16[1024,128]{1,0:T(8,128)(2,1)S(1)}, u32[]{:S(2)}, u32[]{:S(2)}) collective-permute-start(f16[1024,128]{1,0:T(8,128)(2,1)S(1)} %collective-permute-done.11), channel_id=1, source_target_pairs={{64,0},{80,16},{96,32},{112,48},{128,64},{144,80},{160,96},{176,11... | collective-permute-start | bytes 786440 | tf_op jit(solution)/shard_map/ppermute | solution.py:375
  138.8 9.5 %collective-permute-start.9 = (f16[1024,128]{1,0:T(8,128)(2,1)S(1)}, f16[1024,128]{1,0:T(8,128)(2,1)S(1)}, u32[]{:S(2)}, u32[]{:S(2)}) collective-permute-start(f16[1024,128]{1,0:T(8,128)(2,1)S(1)} %collective-permute-done.8), channel_id=1, source_target_pairs={{0,64},{16,80},{32,96},{48,112},{64,128},{80,144},{96,160},{112,17... | collective-permute-start | bytes 786440 | tf_op jit(solution)/shard_map/ppermute | solution.py:375
  179.0 0.9 copy-start.8
Sparse Core Ops, SparseCore 0:
  10.1 34.0 all-gather.6
  53.4 37.4 all-gather.8
  93.0 30.5 all-gather.10
